TPU v7x, 32 devices: a whole 2x2x4 slice. The times are simulated.
32 devices in a mesh: band: 8 (over z, y), fft: 4 (over x, core).
Axes of the slice: x: 2, y: 2, z: 4, core: 2. Of those that a mesh axis runs over, the one named last changes fastest.
Arguments:
- wavefunctions: bfloat16 [8, 176, 30976], P('band', 'fft'), may hold values from -6 to 6
- band_occ: int32 [8], P('band'), may hold values from 0 to 2
Outputs:
- exchange_term: float32 [8, 176, 30976], P('band', 'fft')
All inputs are finite; a program needn't handle non-finite values.
Results may differ from a plain program's by a relative error of at most 0.0003.
Values may be sent and summed in bfloat16 or wider, within the bound.
A program may use at most 128 MiB of HBM per device.

v0:
```python
import jax
import jax.numpy as jnp
from jax import lax
from jax.sharding import PartitionSpec as P

CYCLE_STEPS = 2


def passed_along(value, axis, steps):
    count = lax.axis_size(axis)
    pairs = [(source, (source + steps) % count) for source in range(count)]
    return lax.ppermute(value, axis, pairs)


def cas_rows(grid_size):
    indices = jnp.arange(grid_size, dtype=jnp.int32)
    product = indices[:, None] * indices[None, :] % grid_size
    phases = product.astype(jnp.float32) * (2.0 * jnp.pi / grid_size)
    return jnp.cos(phases) + jnp.sin(phases)


def folded_squares(indices, grid_size):
    folded = jnp.minimum(indices, grid_size - indices).astype(jnp.float32)
    return folded * folded


def truncated_kernel(grid_size, slab_rows):
    indices = jnp.arange(grid_size, dtype=jnp.int32)
    squares = folded_squares(indices, grid_size)
    own_rows = lax.axis_index("fft") * slab_rows + jnp.arange(slab_rows, dtype=jnp.int32)
    row_squares = folded_squares(own_rows, grid_size)
    summed = squares[:, None, None] + row_squares[None, :, None] + squares[None, None, :]
    safe_sum = jnp.maximum(summed, 1.0)
    radius = jnp.sqrt(safe_sum)
    profile = jnp.where(
        summed > 0.5, 2.0 * (1.0 - jnp.cos(jnp.pi * radius)) / (jnp.pi * jnp.pi * safe_sum), 1.0
    )
    return profile * (0.25 / float(grid_size) ** 1.5)


def potentials(density, cas_table, kernel):
    partial_field = jnp.einsum("pxyz,kz->pxyk", density, cas_table, precision=lax.Precision.HIGHEST)
    partial_field = jnp.einsum(
        "pxyz,ky->pxkz", partial_field, cas_table, precision=lax.Precision.HIGHEST
    )
    spectrum = jnp.einsum(
        "pxyz,kx->pkyz",
        lax.all_to_all(partial_field, "fft", split_axis=2, concat_axis=1, tiled=True),
        cas_table,
        precision=lax.Precision.HIGHEST,
    )
    filtered = jnp.einsum(
        "pkyz,kx->pxyz", spectrum * kernel[None], cas_table, precision=lax.Precision.HIGHEST
    )
    mixed_field = lax.all_to_all(filtered, "fft", split_axis=1, concat_axis=2, tiled=True)
    mixed_field = jnp.einsum(
        "pxyz,ky->pxkz", mixed_field, cas_table, precision=lax.Precision.HIGHEST
    )
    return jnp.einsum("pxyz,kz->pxyk", mixed_field, cas_table, precision=lax.Precision.HIGHEST)


def pair_density(home_block, visitor, grid_size):
    density = home_block.astype(jnp.float32)[:, None] * visitor.astype(jnp.float32)[None]
    pair_count = home_block.shape[0] * visitor.shape[0]
    return density.reshape(pair_count, home_block.shape[1], grid_size, grid_size)


def split_terms(potential, home_block, home_occ, visitor, visitor_occ):
    band_count, slab_rows, plane_cells = home_block.shape
    field = potential.reshape(band_count, band_count, slab_rows, plane_cells)
    visitor_weighted = visitor.astype(jnp.float32) * visitor_occ.astype(jnp.float32)[:, None, None]
    home_weighted = home_block.astype(jnp.float32) * home_occ.astype(jnp.float32)[:, None, None]
    own_terms = -0.5 * jnp.sum(field * visitor_weighted[None], axis=1)
    return_terms = -0.5 * jnp.sum(field * home_weighted[:, None], axis=0)
    return (own_terms, return_terms)


def shards(wavefunctions, band_occ):
    band_count, slab_rows, plane_cells = wavefunctions.shape
    grid_size = slab_rows * lax.axis_size("fft")
    cas_table = cas_rows(grid_size)
    kernel = truncated_kernel(grid_size, slab_rows)
    occupied = band_occ.astype(jnp.bfloat16)
    collected = jnp.zeros((band_count, slab_rows, plane_cells), jnp.float32)
    for cycle_step in range(1, CYCLE_STEPS + 1):
        visitor, visitor_occ = passed_along((wavefunctions, occupied), "band", cycle_step)
        potential = potentials(pair_density(wavefunctions, visitor, grid_size), cas_table, kernel)
        own_terms, return_terms = split_terms(
            potential, wavefunctions, occupied, visitor, visitor_occ
        )
        collected = collected + own_terms + passed_along(return_terms, "band", -cycle_step)
    return collected


def solution(mesh):
    in_specs = (P("band", "fft", None), P("band"))
    out_specs = P("band", "fft", None)
    return jax.shard_map(shards, mesh=mesh, in_specs=in_specs, out_specs=out_specs, check_vma=False)
```

profile of v0, /device:TPU:0, one launch (start us, length us, event | category | flops | bytes accessed | tf_op | source)
XLA Modules:
  0.0 898.9 jit_solution(5128763353816257561)
XLA Ops:
  0.0 3.0 collective-permute-start
  3.0 1.6 collective-permute-start.3
  4.5 66.9 %collective-permute-done = bf16[1,44,30976]{2,1,0:T(8,128)(2,1)S(1)} collective-permute-done((bf16[1,44,30976]{2,1,0:T(8,128)(2,1)}, bf16[1,44,30976]{2,1,0:T(8,128)(2,1)S(1)}, u32[]{:S(2)}, u32[]{:S(2)}) %collective-permute-start) | collective-permute-done | bytes 2725920 | tf_op jit(solution)/shard_map/ppermute | solution.py:12
  71.5 0.0 collective-permute-done.3
  71.5 9.2 %convert_multiply_fusion = (f32[1,44,30976]{2,1,0:T(8,128)}, f32[1,44,30976]{2,1,0:T(8,128)}) fusion(bf16[1,44,30976]{2,1,0:T(8,128)(2,1)} %param.2, bf16[1,44,30976]{2,1,0:T(8,128)(2,1)S(1)} %collective-permute-done.3, bf16[1,44,30976]{2,1,0:T(8,128)(2,1)S(1)} %collective-permute-done), kind=kLoop, calls=%fused_computation.4 | loop fusion | flops 6814720 | bytes 19081216 | tf_op jit(solution)/shard_map/mul | solution.py:63
  80.7 0.0 copy-done.1
  80.7 0.0 copy-done.3
  80.7 9.9 %mul.302 = f32[44,176,176]{2,1,0:T(8,128)} reshape(f32[1,44,30976]{2,1,0:T(8,128)} %get-tuple-element.7) | data formatting | bytes 10903552 | tf_op jit(solution)/shard_map/mul | solution.py:63
  90.6 11.1 %fusion.46 = f32[44,176,176]{2,1,0:T(8,128)S(1)} fusion(f32[44,176,176]{2,1,0:T(8,128)} %mul.302), kind=kOutput, calls=%fused_computation.50 | convolution fusion | flops 2878847488 | bytes 10903552 | tf_op jit(solution)/shard_map/pxyz,kz->pxyk/dot_general | solution.py:42
  101.7 8.7 convolution_bitcast_fusion
  110.5 9.4 %copy.57 = f32[1,44,176,176]{3,0,1,2:T(1,128)} copy(f32[1,44,176,176]{3,2,1,0:T(8,128)S(1)} %convolution_bitcast_fusion) | data formatting | bytes 10903552 | tf_op jit(solution)/shard_map/pxyz,ky->pxkz/transpose | solution.py:43
  119.9 5.8 all-to-all-start.2
  125.7 9.8 %mul.276 = f32[44,176,176]{2,1,0:T(8,128)} reshape(f32[1,44,30976]{2,1,0:T(8,128)} %get-tuple-element.8) | data formatting | bytes 10903552 | tf_op jit(solution)/shard_map/mul | solution.py:63
  135.4 10.8 %fusion.54 = f32[44,176,176]{2,1,0:T(8,128)S(1)} fusion(f32[44,176,176]{2,1,0:T(8,128)} %mul.276), kind=kOutput, calls=%fused_computation.58 | convolution fusion | flops 2878847488 | bytes 10903552 | tf_op jit(solution)/shard_map/pxyz,kz->pxyk/dot_general | solution.py:42
  146.3 8.7 convolution_bitcast_fusion.1
  155.0 9.4 %copy.49 = f32[1,44,176,176]{3,0,1,2:T(1,128)} copy(f32[1,44,176,176]{3,2,1,0:T(8,128)S(1)} %convolution_bitcast_fusion.1) | data formatting | bytes 10903552 | tf_op jit(solution)/shard_map/pxyz,ky->pxkz/transpose | solution.py:43
  164.4 49.5 %all-to-all-done.2 = f32[1,44,176,176]{3,0,1,2:T(1,128)} async-done(((f32[1,44,176,176]{3,0,1,2:T(1,128)}), f32[1,44,176,176]{3,0,1,2:T(1,128)}, u32[]{:S(2)}, u32[]{:S(2)}) %all-to-all-start.2) | async-done | bytes 5451808 | tf_op jit(solution)/shard_map/all_to_all | solution.py:48
  213.9 6.0 all-to-all-start
  219.9 0.8 fusion.127
  220.7 0.1 broadcast_add_fusion
  220.7 8.7 copy.58
  229.4 8.1 copy.59
  237.4 9.2 %reshape.196 = f32[176,44,176]{2,0,1:T(8,128)} reshape(f32[1,4,44,44,176]{4,2,1,3,0:T(8,128)} %copy.59) | data formatting | bytes 10903552 | tf_op jit(solution)/shard_map/reshape.29
  246.6 11.1 %fusion.43 = f32[176,44,176]{2,0,1:T(8,128)S(1)} fusion(f32[176,44,176]{2,0,1:T(8,128)} %reshape.196), kind=kOutput, calls=%fused_computation.47 | convolution fusion | flops 2878847488 | bytes 10903552 | tf_op jit(solution)/shard_map/pxyz,kx->pkyz/dot_general | solution.py:46
  257.8 51.2 %fusion.33 = f32[1,176,44,176]{3,1,2,0:T(8,128)S(1)} fusion(f32[176,44,176]{2,0,1:T(8,128)S(1)} %fusion.43, f32[176]{0:T(256)S(1)} %fusion.60, f32[176,44]{0,1:T(8,128)S(1)} %broadcast_add_fusion, f32[176,176,1]{1,0,2:T(8,128)S(1)} %fusion.127), kind=kOutput, calls=%fused_computation.36 | convolution fusion | flops 2893530112 | bytes 11059136 | tf_op jit(solution)/shard_map/pkyz,kx->pxyz/dot_general | solution.py:52
  309.0 9.6 %copy.61 = f32[1,176,44,176]{3,0,2,1:T(1,128)} copy(f32[1,176,44,176]{3,1,2,0:T(8,128)S(1)} %fusion.33) | data formatting | bytes 10903552 | tf_op jit(solution)/shard_map/pkyz,kx->pxyz/transpose | solution.py:52
  318.6 0.0 all-to-all-done
  318.6 5.6 all-to-all-start.3
  324.2 0.8 fusion.125
  325.0 8.7 copy.50
  333.7 8.0 copy.51
  341.7 9.2 %reshape.192 = f32[176,44,176]{2,0,1:T(8,128)} reshape(f32[1,4,44,44,176]{4,2,1,3,0:T(8,128)} %copy.51) | data formatting | bytes 10903552 | tf_op jit(solution)/shard_map/reshape.8
  350.9 11.1 %fusion.51 = f32[176,44,176]{2,0,1:T(8,128)S(1)} fusion(f32[176,44,176]{2,0,1:T(8,128)} %reshape.192), kind=kOutput, calls=%fused_computation.55 | convolution fusion | flops 2878847488 | bytes 10903552 | tf_op jit(solution)/shard_map/pxyz,kx->pkyz/dot_general | solution.py:46
  362.0 51.2 %fusion.30 = f32[1,176,44,176]{3,1,2,0:T(8,128)S(1)} fusion(f32[176,44,176]{2,0,1:T(8,128)S(1)} %fusion.51, f32[176]{0:T(256)S(1)} %fusion.60, f32[176,44]{0,1:T(8,128)S(1)} %broadcast_add_fusion, f32[176,176,1]{1,0,2:T(8,128)S(1)} %fusion.125), kind=kOutput, calls=%fused_computation.35 | convolution fusion | flops 2893530112 | bytes 11059136 | tf_op jit(solution)/shard_map/pkyz,kx->pxyz/dot_general | solution.py:52
  413.3 9.8 %copy.53 = f32[1,176,44,176]{3,0,2,1:T(1,128)} copy(f32[1,176,44,176]{3,1,2,0:T(8,128)S(1)} %fusion.30) | data formatting | bytes 10903552 | tf_op jit(solution)/shard_map/pkyz,kx->pxyz/transpose | solution.py:52
  423.1 0.0 all-to-all-done.3
  423.1 5.6 all-to-all-start.1
  429.3 8.0 copy.62
  437.3 9.2 %reshape.197 = f32[44,176,176]{2,1,0:T(8,128)} reshape(f32[1,44,4,44,176]{4,3,2,1,0:T(8,128)} %copy.62) | data formatting | bytes 10903552 | tf_op jit(solution)/shard_map/reshape.35
  446.5 11.1 %fusion.41 = f32[176,44,176]{2,0,1:T(8,128)S(1)} fusion(f32[44,176,176]{2,1,0:T(8,128)} %reshape.197), kind=kOutput, calls=%fused_computation.45 | convolution fusion | flops 2878847488 | bytes 10903552 | tf_op jit(solution)/shard_map/pxyz,ky->pxkz/dot_general | solution.py:56
  457.6 9.9 %fusion.9 = f32[44,176,176]{2,1,0:T(8,128)} fusion(f32[176,44,176]{2,0,1:T(8,128)S(1)} %fusion.41), kind=kOutput, calls=%fused_computation.14 | convolution fusion | flops 2878847488 | bytes 10903552 | tf_op jit(solution)/shard_map/pxyz,kz->pxyk/dot_general | solution.py:59
  467.5 9.2 %reshape.199 = f32[1,44,30976]{2,1,0:T(8,128)} reshape(f32[44,176,176]{2,1,0:T(8,128)} %fusion.9) | data formatting | bytes 10903552 | tf_op jit(solution)/shard_map/reshape | solution.py:70
  476.7 40.2 %all-to-all-done.1 = f32[1,176,44,176]{3,0,2,1:T(1,128)} async-done(((f32[1,176,44,176]{3,0,2,1:T(1,128)}), f32[1,176,44,176]{3,0,2,1:T(1,128)}, u32[]{:S(2)}, u32[]{:S(2)}) %all-to-all-start.1) | async-done | bytes 5451808 | tf_op jit(solution)/shard_map/all_to_all | solution.py:55
  516.9 7.9 copy.54
  524.9 9.2 %reshape.193 = f32[44,176,176]{2,1,0:T(8,128)} reshape(f32[1,44,4,44,176]{4,3,2,1,0:T(8,128)} %copy.54) | data formatting | bytes 10903552 | tf_op jit(solution)/shard_map/reshape.16
  534.0 11.3 %fusion.49 = f32[176,44,176]{2,0,1:T(8,128)S(1)} fusion(f32[44,176,176]{2,1,0:T(8,128)} %reshape.193), kind=kOutput, calls=%fused_computation.53 | convolution fusion | flops 2878847488 | bytes 10903552 | tf_op jit(solution)/shard_map/pxyz,ky->pxkz/dot_general | solution.py:56
  545.3 10.0 %fusion.11 = f32[44,176,176]{2,1,0:T(8,128)} fusion(f32[176,44,176]{2,0,1:T(8,128)S(1)} %fusion.49), kind=kOutput, calls=%fused_computation.16 | convolution fusion | flops 2878847488 | bytes 10903552 | tf_op jit(solution)/shard_map/pxyz,kz->pxyk/dot_general | solution.py:59
  555.3 9.4 %reshape.195 = f32[1,44,30976]{2,1,0:T(8,128)} reshape(f32[44,176,176]{2,1,0:T(8,128)} %fusion.11) | data formatting | bytes 10903552 | tf_op jit(solution)/shard_map/reshape | solution.py:70
  564.7 0.0 copy-done
  564.7 9.9 %fusion.19 = (f32[1,44,30976]{2,1,0:T(8,128)}, f32[1,44,30976]{2,1,0:T(8,128)}) fusion(f32[1,44,30976]{2,1,0:T(8,128)} %reshape.195, bf16[1,44,30976]{2,1,0:T(8,128)(2,1)S(1)} %copy-done, f32[]{:T(128)S(6)} %convert.4, f32[1,44,30976]{2,1,0:T(8,128)} %reshape.199), kind=kLoop, calls=%fused_computation.26 | loop fusion | flops 8177664 | bytes 24532996 | tf_op jit(solution)/shard_map/mul | solution.py:74
  574.6 8.5 copy.55
  583.1 63.5 %collective-permute-start.2 = (f32[1,44,30976]{2,0,1:T(1,128)}, f32[1,44,30976]{2,0,1:T(1,128)}, u32[]{:S(2)}, u32[]{:S(2)}) collective-permute-start(f32[1,44,30976]{2,0,1:T(1,128)} %copy.55), channel_id=1, source_target_pairs={{0,28},{4,0},{8,4},{12,8},{16,12},{20,16},{24,20},{28,24},{1,29},{... | collective-permute-start | bytes 16355336 | tf_op jit(solution)/shard_map/ppermute | solution.py:12
  646.6 0.0 slice-done
  646.6 0.0 slice-done.1
  646.6 6.7 copy.63
  653.3 0.7 collective-permute-start.5
  654.0 1.4 collective-permute-start.1
  655.4 225.0 %collective-permute-start.4 = (bf16[1]{0:T(256)(128)(2,1)}, bf16[1]{0:T(256)(128)(2,1)}, u32[]{:S(2)}, u32[]{:S(2)}) collective-permute-start(bf16[1]{0:T(256)(128)(2,1)} %convert_element_type.71), channel_id=1, source_target_pairs={{0,8},{4,12},{8,16},{12,20},{16,24},{20,28},{24,0},{28,4},{1,9},{5... | collective-permute-start | bytes 14 | tf_op jit(solution)/shard_map/ppermute | solution.py:12
  880.9 0.3 collective-permute-done.4
  881.9 0.0 collective-permute-done.2
  881.9 0.0 collective-permute-done.5
  881.9 0.0 copy-done.2
  881.9 10.1 %fusion.25 = f32[1,44,30976]{2,1,0:T(8,128)S(1)} fusion(f32[1,44,30976]{2,1,0:T(8,128)} %reshape.195, bf16[1,44,30976]{2,1,0:T(8,128)(2,1)S(1)} %copy-done.2, f32[1,44,30976]{2,1,0:T(8,128)} %reshape.199, bf16[1,44,30976]{2,1,0:T(8,128)(2,1)} %copy-done.3, f32[1,44,30976]{2,0,1:T(1,128)} %collective-permute-done.5, ...), kind=kLoop, calls=%fused_computation.32 | loop fusion | flops 14992384 | bytes 32710664 | tf_op jit(solution)/shard_map/add | solution.py:91
  892.1 6.7 copy.65
  (10 shorter events, 0.0 us)
Async XLA Ops:
  0.0 71.5 %collective-permute-start = (bf16[1,44,30976]{2,1,0:T(8,128)(2,1)}, bf16[1,44,30976]{2,1,0:T(8,128)(2,1)S(1)}, u32[]{:S(2)}, u32[]{:S(2)}) collective-permute-start(bf16[1,44,30976]{2,1,0:T(8,128)(2,1)} %param.2), channel_id=1, source_target_pairs={{0,4},{4,8},{8,12},{12,16},{16,20},{20,24},{24,28},{28,0},{1,5},{5... | collective-permute-start | bytes 8177672 | tf_op jit(solution)/shard_map/ppermute | solution.py:12
  3.0 68.5 %collective-permute-start.3 = (bf16[1,44,30976]{2,1,0:T(8,128)(2,1)}, bf16[1,44,30976]{2,1,0:T(8,128)(2,1)S(1)}, u32[]{:S(2)}, u32[]{:S(2)}) collective-permute-start(bf16[1,44,30976]{2,1,0:T(8,128)(2,1)} %param.2), channel_id=1, source_target_pairs={{0,8},{4,12},{8,16},{12,20},{16,24},{20,28},{24,0},{28,4},{1,9},{5... | collective-permute-start | bytes 8177672 | tf_op jit(solution)/shard_map/ppermute | solution.py:12
  71.5 9.3 %copy-start.1 = (bf16[1,44,30976]{2,1,0:T(8,128)(2,1)}, bf16[1,44,30976]{2,1,0:T(8,128)(2,1)S(1)}, u32[]{:S(2)}) copy-start(bf16[1,44,30976]{2,1,0:T(8,128)(2,1)S(1)} %collective-permute-done) | copy-start | bytes 8177668
  71.5 9.3 %copy-start.3 = (bf16[1,44,30976]{2,1,0:T(8,128)(2,1)}, bf16[1,44,30976]{2,1,0:T(8,128)(2,1)S(1)}, u32[]{:S(2)}) copy-start(bf16[1,44,30976]{2,1,0:T(8,128)(2,1)S(1)} %collective-permute-done.3) | copy-start | bytes 8177668
  119.9 94.0 %all-to-all-start.2 = ((f32[1,44,176,176]{3,0,1,2:T(1,128)}), f32[1,44,176,176]{3,0,1,2:T(1,128)}, u32[]{:S(2)}, u32[]{:S(2)}) async-start(f32[1,44,176,176]{3,0,1,2:T(1,128)} %copy.57), calls=%async_computation.2 | async-start | bytes 15859712 | tf_op jit(solution)/shard_map/all_to_all | solution.py:48
  213.9 104.7 %all-to-all-start = ((f32[1,44,176,176]{3,0,1,2:T(1,128)}), f32[1,44,176,176]{3,0,1,2:T(1,128)}, u32[]{:S(2)}, u32[]{:S(2)}) async-start(f32[1,44,176,176]{3,0,1,2:T(1,128)} %copy.49), calls=%async_computation | async-start | bytes 15859712 | tf_op jit(solution)/shard_map/all_to_all | solution.py:48
  318.6 104.5 %all-to-all-start.3 = ((f32[1,176,44,176]{3,0,2,1:T(1,128)}), f32[1,176,44,176]{3,0,2,1:T(1,128)}, u32[]{:S(2)}, u32[]{:S(2)}) async-start(f32[1,176,44,176]{3,0,2,1:T(1,128)} %copy.61), calls=%async_computation.3 | async-start | bytes 15859712 | tf_op jit(solution)/shard_map/all_to_all | solution.py:55
  423.1 93.8 %all-to-all-start.1 = ((f32[1,176,44,176]{3,0,2,1:T(1,128)}), f32[1,176,44,176]{3,0,2,1:T(1,128)}, u32[]{:S(2)}, u32[]{:S(2)}) async-start(f32[1,176,44,176]{3,0,2,1:T(1,128)} %copy.53), calls=%async_computation.1 | async-start | bytes 15859712 | tf_op jit(solution)/shard_map/all_to_all | solution.py:55
  555.3 9.4 %copy-start = (bf16[1,44,30976]{2,1,0:T(8,128)(2,1)S(1)}, bf16[1,44,30976]{2,1,0:T(8,128)(2,1)}, u32[]{:S(2)}) copy-start(bf16[1,44,30976]{2,1,0:T(8,128)(2,1)} %param.2) | copy-start | bytes 8177668
  574.6 72.0 %slice-start = ((s8[5947392]{0:T(1024)(128)(4,1)}), s8[4194304]{0:T(1024)(128)(4,1)S(1)}, s32[]{:S(2)}) async-start(s8[5947392]{0:T(1024)(128)(4,1)} %bitcast.94), calls=%async_computation.4 | async-start | bytes 8388608
  574.6 72.0 %slice-start.1 = ((s8[5947392]{0:T(1024)(128)(4,1)}), s8[1753088]{0:T(1024)(128)(4,1)S(1)}, s32[]{:S(2)}) async-start(s8[5947392]{0:T(1024)(128)(4,1)} %bitcast.94), calls=%async_computation.5 | async-start | bytes 3506176
  583.1 298.8 %copy-start.2 = (bf16[1,44,30976]{2,1,0:T(8,128)(2,1)S(1)}, bf16[1,44,30976]{2,1,0:T(8,128)(2,1)}, u32[]{:S(2)}) copy-start(bf16[1,44,30976]{2,1,0:T(8,128)(2,1)} %copy-done.1) | copy-start | bytes 8177668
  583.1 298.8 %collective-permute-start.2 = (f32[1,44,30976]{2,0,1:T(1,128)}, f32[1,44,30976]{2,0,1:T(1,128)}, u32[]{:S(2)}, u32[]{:S(2)}) collective-permute-start(f32[1,44,30976]{2,0,1:T(1,128)} %copy.55), channel_id=1, source_target_pairs={{0,28},{4,0},{8,4},{12,8},{16,12},{20,16},{24,20},{28,24},{1,29},{... | collective-permute-start | bytes 16355336 | tf_op jit(solution)/shard_map/ppermute | solution.py:12
  653.3 228.6 %collective-permute-start.5 = (f32[1,44,30976]{2,0,1:T(1,128)}, f32[1,44,30976]{2,0,1:T(1,128)}, u32[]{:S(2)}, u32[]{:S(2)}) collective-permute-start(f32[1,44,30976]{2,0,1:T(1,128)} %copy.63), channel_id=1, source_target_pairs={{0,24},{4,28},{8,0},{12,4},{16,8},{20,12},{24,16},{28,20},{1,25},{... | collective-permute-start | bytes 16355336 | tf_op jit(solution)/shard_map/ppermute | solution.py:12
  654.0 226.4 %collective-permute-start.1 = (bf16[1]{0:T(256)(128)(2,1)}, bf16[1]{0:T(256)(128)(2,1)}, u32[]{:S(2)}, u32[]{:S(2)}) collective-permute-start(bf16[1]{0:T(256)(128)(2,1)} %convert_element_type.71), channel_id=1, source_target_pairs={{0,4},{4,8},{8,12},{12,16},{16,20},{20,24},{24,28},{28,0},{1,5},{5... | collective-permute-start | bytes 14 | tf_op jit(solution)/shard_map/ppermute | solution.py:12
  655.4 225.8 %collective-permute-start.4 = (bf16[1]{0:T(256)(128)(2,1)}, bf16[1]{0:T(256)(128)(2,1)}, u32[]{:S(2)}, u32[]{:S(2)}) collective-permute-start(bf16[1]{0:T(256)(128)(2,1)} %convert_element_type.71), channel_id=1, source_target_pairs={{0,8},{4,12},{8,16},{12,20},{16,24},{20,28},{24,0},{28,4},{1,9},{5... | collective-permute-start | bytes 14 | tf_op jit(solution)/shard_map/ppermute | solution.py:12
where the time goes:
time: 906 us; the launch traced here: 899 us
  starting transfers between devices  318 us (35%)
  matrix products  206 us (23%)
  local copies, waits for them, and re-layouts  184 us (20%)
  waiting for transfers between devices  157 us (17%)
  other arithmetic  30.9 us (3%)
    ppermute x6, starting transfers between devices, passed_along(): return lax.ppermute(value, axis, pairs)  295 us
    dot_general x2, matrix products, potentials(): jnp.einsum('pkyz,kx->pxyz', spectrum * kernel[None], cas_table, precision...  102 us
    ppermute x6, waiting for transfers between devices, passed_along(): return lax.ppermute(value, axis, pairs)  67.2 us
    all_to_all x2, waiting for transfers between devices, potentials(): lax.all_to_all(partial_field, 'fft', split_axis=2, concat_axis=1, tiled=T...  49.5 us
    all_to_all x2, waiting for transfers between devices, potentials(): lax.all_to_all(filtered, 'fft', split_axis=1, concat_axis=2, tiled=True)  40.2 us
    another operation x4, local copies, waits for them, and re-layouts  36.8 us
    all_to_all x4, local copies, waits for them, and re-layouts, potentials(): lax.all_to_all(partial_field, 'fft', split_axis=2, concat_axis=1, tiled=T...  33.4 us
    dot_general x2, matrix products, potentials(): jnp.einsum('pxyz,ky->pxkz', mixed_field, cas_table, precision=lax.Precisi...  22.4 us
  transfers between devices with their start and end apart: 10, of which 4 were waited for; matrix products, arithmetic and copies ran while one was open for 32% of the time, Pallas kernels for 0%

commit v1 on v0

v1 whole, which is shorter than its diff:
```python
import functools

import jax
import jax.numpy as jnp
import numpy as np
from jax import lax
from jax.experimental import pallas as pl
from jax.experimental.pallas import tpu as pltpu
from jax.sharding import PartitionSpec as P

LANES = 256
LEVELS = 32000.0
STEPS_PER_OCTAVE = 64.0
F32 = jnp.float32
BF16 = jnp.bfloat16
VMEM_BYTES = 60 * 1024 * 1024


def round_up(value, multiple):
    return -(-value // multiple) * multiple


def cas_table(grid_size):
    indices = np.arange(grid_size)
    phases = (indices[:, None] * indices[None, :] % grid_size) * (2.0 * np.pi / grid_size)
    return np.cos(phases) + np.sin(phases)


def high_low(table):
    table = table.astype(np.float32)
    high = table.astype(BF16)
    low = (table - high.astype(np.float32)).astype(BF16)
    return jnp.asarray(high), jnp.asarray(low)


def spread_rows(table, blocks, slab, block_rows):
    spread = np.zeros((blocks * block_rows, table.shape[1]))
    for block in range(blocks):
        spread[block * block_rows : block * block_rows + slab] = table[block * slab : (block + 1) * slab]
    return spread


def folded_squares(indices, grid_size):
    folded = jnp.minimum(indices, grid_size - indices).astype(F32)
    return folded * folded


def truncated_kernel(grid_size, slab, rows):
    indices = jnp.arange(grid_size, dtype=jnp.int32)
    squares = folded_squares(indices, grid_size)
    lanes = folded_squares(jnp.minimum(jnp.arange(LANES, dtype=jnp.int32), grid_size), grid_size)
    own_rows = lax.axis_index("fft") * slab + jnp.arange(rows, dtype=jnp.int32)
    row_squares = folded_squares(own_rows, grid_size)
    summed = row_squares[:, None, None] + squares[None, :, None] + lanes[None, None, :]
    safe_sum = jnp.maximum(summed, 1.0)
    radius = jnp.sqrt(safe_sum)
    profile = jnp.where(
        summed > 0.5, 2.0 * (1.0 - jnp.cos(jnp.pi * radius)) / (jnp.pi * jnp.pi * safe_sum), 1.0
    )
    return profile * (0.25 / float(grid_size) ** 1.5)


def parts_of(value):
    high = value.astype(BF16)
    return high, (value - high.astype(F32)).astype(BF16)


def dot(left, right):
    return jnp.dot(left, right, preferred_element_type=F32)


def times_table(value, table):
    high, low = parts_of(value)
    return dot(high, table[0]) + (dot(low, table[0]) + dot(high, table[1]))


def table_times(table, value):
    high, low = parts_of(value)
    return dot(table[0], high) + (dot(table[0], low) + dot(table[1], high))


def exponent_of(largest):
    return jnp.ceil(jnp.log2(jnp.maximum(largest, 1e-30)) * STEPS_PER_OCTAVE)


def step_of(exponent):
    return jnp.exp2(exponent * (1.0 / STEPS_PER_OCTAVE))


def coded(value, slab):
    exponent = exponent_of(jnp.max(jnp.abs(value), axis=-2, keepdims=True))
    scaled = jnp.round(value * (LEVELS / step_of(exponent)))
    row = lax.broadcasted_iota(jnp.int32, value.shape, value.ndim - 2)
    return jnp.where(row == slab, exponent, scaled)


def decoded(code, slab):
    return code * (step_of(code[..., slab : slab + 1, :]) * (1.0 / LEVELS))


def to_wire(code):
    return code.astype(jnp.int32).astype(jnp.int16)


def from_wire(wire):
    return wire.astype(jnp.int32).astype(F32)


def shared_lanes(first, second):
    lane = lax.broadcasted_iota(jnp.int32, first.shape, first.ndim - 1)
    return jnp.where(lane < 64, first, pltpu.roll(second, 64, second.ndim - 1))


def unshared(both):
    lane = lax.broadcasted_iota(jnp.int32, both.shape, both.ndim - 1)
    first = jnp.where(lane < 64, both, 0.0)
    second = jnp.where(lane < 64, pltpu.roll(both, 64, both.ndim - 1), 0.0)
    return first, second


def forward_kernel(slab, blocks, block_rows, a_ref, b_ref, zh, zl, yh, yl, out_ref, buf):
    planes, grid_size = a_ref.shape[0], a_ref.shape[1]
    half = out_ref.shape[1] // 3
    z_table, y_table = (zh[...], zl[...]), (yh[...], yl[...])

    @pl.loop(0, planes // 8)
    def _(chunk):
        rows = pl.ds(pl.multiple_of(chunk * 8, 8), 8)
        density = a_ref[rows].astype(F32) * b_ref[rows].astype(F32)
        along_z = times_table(density.reshape(8 * grid_size, grid_size), z_table)
        along_z = along_z.reshape(8, grid_size, LANES)
        along_y = jnp.stack([table_times(y_table, along_z[i]) for i in range(8)])
        buf[:, rows, :] = jnp.transpose(along_y, (1, 0, 2))

    for block in range(blocks):

        @pl.loop(0, half)
        def _(row):
            first = coded(buf[block * block_rows + row], slab)
            second = coded(buf[block * block_rows + half + row], slab)
            out_ref[block, row] = to_wire(first[:, :128])
            out_ref[block, half + row] = to_wire(second[:, :128])
            out_ref[block, 2 * half + row] = to_wire(shared_lanes(first[:, 128:], second[:, 128:]))


def filter_kernel(slab, in_ref, w_ref, fh, fl, ih, il, out_ref):
    blocks, half, planes = in_ref.shape[0], in_ref.shape[1] // 3, in_ref.shape[2]
    forward, inverse = (fh[...], fl[...]), (ih[...], il[...])

    @pl.loop(0, half)
    def _(row):
        upper = unshared(from_wire(in_ref[:, 2 * half + row]))
        codes = []
        for i in range(2):
            at = row + i * half
            code = jnp.concatenate([from_wire(in_ref[:, at]), upper[i]], axis=-1)
            field = decoded(code, slab).reshape(blocks * planes, LANES)
            spectrum = table_times(forward, field) * w_ref[at]
            filtered = table_times(inverse, spectrum).reshape(blocks, planes, LANES)
            code = coded(filtered, slab)
            out_ref[:, at] = to_wire(code[..., :128])
            codes.append(code[..., 128:])
        out_ref[:, 2 * half + row] = to_wire(shared_lanes(codes[0], codes[1]))


def back_kernel(slab, blocks, block_rows, with_swapped, *refs):
    if with_swapped:
        in_ref, a_ref, b_ref, occ, swapped, zh, zl, yh, yl, own_ref, ret_ref, buf, ret = refs
    else:
        in_ref, a_ref, b_ref, occ, zh, zl, yh, yl, own_ref, ret_ref, buf, ret = refs
    planes, grid_size = a_ref.shape[0], a_ref.shape[1]
    half = in_ref.shape[1] // 3
    halfx = (ret_ref.shape[0] - 2) // 3
    z_table, y_table = (zh[...], zl[...]), (yh[...], yl[...])
    home, visitor = -0.5 * occ[0], -0.5 * occ[1]

    for block in range(blocks):
        base = block * block_rows
        buf[base + 2 * half : base + block_rows] = jnp.zeros(
            (block_rows - 2 * half, planes, LANES), F32
        )

        @pl.loop(0, half)
        def _(row):
            upper = unshared(from_wire(in_ref[block, 2 * half + row]))
            for i in range(2):
                at = row + i * half
                code = jnp.concatenate([from_wire(in_ref[block, at]), upper[i]], axis=-1)
                buf[base + at] = decoded(code, slab)

    def chunk_at(chunk, largest):
        rows = pl.ds(pl.multiple_of(chunk * 8, 8), 8)
        mixed = jnp.transpose(buf[:, rows, :], (1, 0, 2))
        along_y = jnp.stack([table_times(y_table, mixed[i]) for i in range(8)])
        field = times_table(along_y.reshape(8 * grid_size, LANES), z_table)
        field = field.reshape(8, grid_size, LANES)[..., :grid_size]
        own_ref[rows] = field * b_ref[rows].astype(F32) * visitor
        terms = field * a_ref[rows].astype(F32) * home
        ret[rows] = terms
        if with_swapped:
            return largest
        return jnp.maximum(largest, jnp.max(jnp.abs(terms), axis=0))

    largest = lax.fori_loop(0, planes // 8, chunk_at, jnp.zeros((grid_size, grid_size), F32))

    if with_swapped:
        add_own, add_ret = occ[2], occ[3]
        step = plane_steps(swapped, halfx)

        def add_at(row, largest):
            upper = unshared(from_wire(swapped[2 * halfx + row]))
            for i in range(2):
                at = row + i * halfx
                code = jnp.concatenate([from_wire(swapped[at]), upper[i]], axis=-1)
                value = (code * step)[:, :grid_size]
                own_ref[at] = own_ref[at] + value * add_own
                total = ret[at] + value * add_ret
                ret[at] = total
                largest = jnp.maximum(largest, jnp.abs(total))
            return largest

        largest = lax.fori_loop(0, halfx, add_at, largest)

    exponent = exponent_of(widened(largest))
    scale = LEVELS / step_of(exponent)

    @pl.loop(0, halfx)
    def _(row):
        codes = []
        for i in range(2):
            code = jnp.round(widened(ret[row + i * halfx]) * scale)
            ret_ref[row + i * halfx] = to_wire(code[:, :128])
            codes.append(code[:, 128:])
        ret_ref[2 * halfx + row] = to_wire(shared_lanes(codes[0], codes[1]))

    ret_ref[3 * halfx] = to_wire(exponent[:, :128])
    ret_ref[3 * halfx + 1] = to_wire(exponent[:, 128:])


def widened(plane):
    pad = jnp.zeros((plane.shape[0], LANES - plane.shape[1]), F32)
    return jnp.concatenate([plane, pad], axis=-1)


def plane_steps(wire_ref, halfx):
    exponent = jnp.concatenate(
        [from_wire(wire_ref[3 * halfx]), from_wire(wire_ref[3 * halfx + 1])], axis=-1
    )
    return step_of(exponent) * (1.0 / LEVELS)


def total_kernel(first_ref, second_ref, arrived, out_ref):
    grid_size = first_ref.shape[1]
    halfx = (arrived.shape[0] - 2) // 3
    step = plane_steps(arrived, halfx)

    @pl.loop(0, halfx)
    def _(row):
        upper = unshared(from_wire(arrived[2 * halfx + row]))
        for i in range(2):
            at = row + i * halfx
            code = jnp.concatenate([from_wire(arrived[at]), upper[i]], axis=-1)
            out_ref[at] = first_ref[at] + second_ref[at] + (code * step)[:, :grid_size]


def call(kernel, out_shape, scratch, name, flops, *operands, smem=()):
    specs = [
        pl.BlockSpec(memory_space=pltpu.SMEM if at in smem else pltpu.VMEM)
        for at in range(len(operands))
    ]
    single = pl.BlockSpec(memory_space=pltpu.VMEM)
    bytes_moved = sum(o.size * o.dtype.itemsize for o in operands)
    return pl.pallas_call(
        kernel,
        out_shape=out_shape,
        in_specs=specs,
        out_specs=[single] * len(out_shape) if isinstance(out_shape, list) else single,
        scratch_shapes=scratch,
        compiler_params=pltpu.CompilerParams(vmem_limit_bytes=VMEM_BYTES),
        cost_estimate=pl.CostEstimate(flops=flops, bytes_accessed=bytes_moved, transcendentals=0),
        name=name,
    )(*operands)


def exchange(wire):
    return lax.all_to_all(wire, "fft", split_axis=0, concat_axis=0, tiled=True)


def shards(wavefunctions, band_occ):
    slab = wavefunctions.shape[1]
    blocks = lax.axis_size("fft")
    bands = lax.axis_size("band")
    grid_size = slab * blocks
    planes = round_up(slab + 1, 16)
    block_rows = round_up(slab, 8)
    half = (slab + 1) // 2
    ky_rows = blocks * block_rows

    table = cas_table(grid_size)
    lanes_table = np.zeros((grid_size, LANES))
    lanes_table[:, :grid_size] = table
    square_table = np.zeros((LANES, LANES))
    square_table[:grid_size, :grid_size] = table
    to_ky = spread_rows(table, blocks, slab, block_rows)
    to_x = spread_rows(table, blocks, slab, planes)
    z_forward, z_back = high_low(lanes_table), high_low(square_table)
    y_forward, y_back = high_low(to_ky), high_low(to_ky.T)
    x_forward, x_back = high_low(to_x.T), high_low(to_x)
    profile = truncated_kernel(grid_size, slab, 2 * half)

    occupied = band_occ.astype(BF16)
    upward = [(i, (i + 2) % bands) for i in range(bands)]
    downward = [(i, (i - 2) % bands) for i in range(bands)]
    swap = [(i, i ^ 1) for i in range(bands)]
    is_odd = lax.axis_index("band") % 2 == 1

    wide = lambda psi: jnp.pad(psi[0], ((0, planes - slab), (0, 0))).reshape(
        planes, grid_size, grid_size
    )
    far, far_occ = lax.ppermute((wavefunctions, occupied), "band", upward)
    near, near_occ = lax.ppermute(
        (jnp.where(is_odd, far, wavefunctions), jnp.where(is_odd, far_occ, occupied)), "band", swap
    )
    home = wide(wavefunctions)
    flops = 12 * planes * grid_size**3

    def forward(visitor):
        return call(
            functools.partial(forward_kernel, slab, blocks, block_rows),
            jax.ShapeDtypeStruct((blocks, 3 * half, planes, 128), jnp.int16),
            [pltpu.VMEM((ky_rows, planes, LANES), F32)],
            "density_to_ky_kz",
            flops,
            home,
            visitor,
            *z_forward,
            *y_forward,
        )

    def filtered(wire):
        return call(
            functools.partial(filter_kernel, slab),
            jax.ShapeDtypeStruct(wire.shape, jnp.int16),
            [],
            "filter_along_x",
            flops,
            wire,
            profile,
            *x_forward,
            *x_back,
        )

    def back(wire, visitor, factors, swapped=None):
        extra = [] if swapped is None else [swapped]
        return call(
            functools.partial(back_kernel, slab, blocks, block_rows, swapped is not None),
            [
                jax.ShapeDtypeStruct((planes, grid_size, grid_size), F32),
                jax.ShapeDtypeStruct((3 * half + 2, grid_size, 128), jnp.int16),
            ],
            [
                pltpu.VMEM((ky_rows, planes, LANES), F32),
                pltpu.VMEM((planes, grid_size, grid_size), F32),
            ],
            "potential_terms",
            flops,
            wire,
            home,
            visitor,
            factors,
            *extra,
            *z_back,
            *y_back,
            smem=(3,),
        )

    far_field, near_field = wide(far), wide(near)
    odd = is_odd.astype(F32)
    home_occ = occupied.astype(F32)[0]
    near_factors = jnp.stack([home_occ, near_occ.astype(F32)[0], 1.0 - odd, odd])
    far_factors = jnp.stack([home_occ, far_occ.astype(F32)[0], 1.0 - odd, odd])

    near_wire = exchange(forward(near_field))
    far_wire = exchange(forward(far_field))
    near_wire = exchange(filtered(near_wire))
    far_wire = exchange(filtered(far_wire))
    near_own, near_return = back(near_wire, near_field, near_factors)
    swapped = lax.ppermute(near_return, "band", swap)
    far_own, far_return = back(far_wire, far_field, far_factors, swapped)
    arrived = lax.ppermute(far_return, "band", downward)
    total = call(
        total_kernel,
        jax.ShapeDtypeStruct((planes, grid_size, grid_size), F32),
        [],
        "total_terms",
        3 * planes * grid_size**2,
        near_own,
        far_own,
        arrived,
    )
    return total[:slab].reshape(1, slab, grid_size * grid_size)


def solution(mesh):
    in_specs = (P("band", "fft", None), P("band"))
    out_specs = P("band", "fft", None)
    return jax.shard_map(shards, mesh=mesh, in_specs=in_specs, out_specs=out_specs, check_vma=False)
```

time: 906 us -> 545 us (0.60)
  starting transfers between devices: 318 us -> 22.4 us
  matrix products: 206 us -> 0 us
  Pallas kernels: 0 us -> 182 us
  local copies, waits for them, and re-layouts: 184 us -> 58.6 us
  waiting for transfers between devices: 157 us -> 240 us
    ppermute x6, starting transfers between devices: 295 us -> 6.31 us  [the longest x2 4.38 us: shards(): far, far_occ = lax.ppermute((wavefunctions, occupied), 'band', upward)]
    dot_general x12 -> x0, matrix products: 206 us -> none  [the longest x2 102 us: potentials(): jnp.einsum('pkyz,kx->pxyz', spectrum * kernel[None], cas_table, precision...]
    pallas_call x0 -> x7, Pallas kernels: none -> 182 us  [call(): pl.pallas_call(kernel, out_shape=out_shape, in_specs=specs, out_specs=[si...]
    ppermute x6, waiting for transfers between devices: 67.2 us -> 198 us  [the longest x2 70.8 us: shards(): far, far_occ = lax.ppermute((wavefunctions, occupied), 'band', upward)]
    all_to_all x6 -> x0, local copies, waits for them, and re-layouts: 49.3 us -> none  [the longest x4 33.4 us: potentials(): lax.all_to_all(partial_field, 'fft', split_axis=2, concat_axis=1, tiled=T...]
    all_to_all x4, waiting for transfers between devices: 89.7 us -> 42.8 us  [exchange(): return lax.all_to_all(wire, 'fft', split_axis=0, concat_axis=0, tiled=True)]
    transpose x4 -> x0, local copies, waits for them, and re-layouts: 38.3 us -> none  [the longest x2 19.4 us: potentials(): jnp.einsum('pkyz,kx->pxyz', spectrum * kernel[None], cas_table, precision...]
    another operation x4 -> x0, local copies, waits for them, and re-layouts: 36.8 us -> none
  transfers between devices with their start and end apart: 10 -> 10, of which waited for: 4 -> 8; matrix products, arithmetic and copies ran while one was open for 32% -> 10% of each run, Pallas kernels for 0% -> 15%
where the time goes in v1:
time: 545 us; the launch traced here: 544 us
  waiting for transfers between devices  240 us (44%)
  Pallas kernels  182 us (33%)
  local copies, waits for them, and re-layouts  58.6 us (11%)
  other arithmetic  37.9 us (7%)
  starting transfers between devices  22.4 us (4%)
    pallas_call x7, Pallas kernels, call(): pl.pallas_call(kernel, out_shape=out_shape, in_specs=specs, out_specs=[si...  182 us
    ppermute x2, waiting for transfers between devices, shards(): far, far_occ = lax.ppermute((wavefunctions, occupied), 'band', upward)  70.8 us
    ppermute x1, waiting for transfers between devices, shards(): arrived = lax.ppermute(far_return, 'band', downward)  68.2 us
    ppermute x2, waiting for transfers between devices, shards(): lax.ppermute((jnp.where(is_odd, far, wavefunctions), jnp.where(is_odd, fa...  58.1 us
    all_to_all x4, waiting for transfers between devices, exchange(): return lax.all_to_all(wire, 'fft', split_axis=0, concat_axis=0, tiled=True)  42.8 us
    mul x1, other arithmetic, truncated_kernel(): return profile * (0.25 / float(grid_size) ** 1.5)  31.8 us
    reshape x3, local copies, waits for them, and re-layouts, shards(): jnp.pad(psi[0], ((0, planes - slab), (0, 0)))  29.1 us
    all_to_all x4, starting transfers between devices, exchange(): return lax.all_to_all(wire, 'fft', split_axis=0, concat_axis=0, tiled=True)  16.1 us
  transfers between devices with their start and end apart: 10, of which 8 were waited for; matrix products, arithmetic and copies ran while one was open for 10% of the time, Pallas kernels for 15%

profile of v1, /device:TPU:0, one launch (start us, length us, event | category | flops | bytes accessed | tf_op | source)
XLA Modules:
  0.0 543.8 jit_solution(8230953794865837044)
XLA Ops:
  0.0 3.0 collective-permute-start
  3.0 0.0 copy-start.3
  3.0 66.6 %collective-permute-done = bf16[1,44,30976]{2,1,0:T(8,128)(2,1)S(1)} collective-permute-done((bf16[1,44,30976]{2,1,0:T(8,128)(2,1)}, bf16[1,44,30976]{2,1,0:T(8,128)(2,1)S(1)}, u32[]{:S(2)}, u32[]{:S(2)}) %collective-permute-start) | collective-permute-done | bytes 2725920 | tf_op jit(solution)/shard_map/ppermute | solution.py:320
  69.7 0.0 copy-start.4
  69.7 4.8 broadcast_select_fusion
  74.5 0.0 copy-done.4
  74.5 0.0 collective-permute-start.1
  74.5 0.0 copy-done.3
  74.5 0.2 pad.10
  74.7 9.7 %reshape.69.a_ref.refs_1_ = bf16[48,176,176]{2,1,0:T(8,128)(2,1)} reshape(bf16[48,30976]{1,0:T(8,128)(2,1)S(1)} %pad.10) | data formatting | bytes 5947392 | tf_op jit(solution)/shard_map/reshape | solution.py:317
  84.4 56.0 %collective-permute-done.1 = bf16[1,44,30976]{2,1,0:T(8,128)(2,1)} collective-permute-done((bf16[1,44,30976]{2,1,0:T(8,128)(2,1)}, bf16[1,44,30976]{2,1,0:T(8,128)(2,1)}, u32[]{:S(2)}, u32[]{:S(2)}) %collective-permute-start.1) | collective-permute-done | bytes 2725920 | tf_op jit(solution)/shard_map/ppermute | solution.py:321
  140.4 2.0 pad.11
  142.5 9.7 %reshape.70.b_ref.refs_2_ = bf16[48,176,176]{2,1,0:T(8,128)(2,1)} reshape(bf16[48,30976]{1,0:T(8,128)(2,1)S(1)} %pad.11) | data formatting | bytes 5947392 | tf_op jit(solution)/shard_map/reshape | solution.py:317
  152.2 29.6 %density_to_ky_kz.2 = s16[4,66,48,128]{3,2,1,0:T(8,128)(2,1)} custom-call(bf16[48,176,176]{2,1,0:T(8,128)(2,1)} %reshape.69.a_ref.refs_1_, bf16[48,176,176]{2,1,0:T(8,128)(2,1)} %reshape.70.b_ref.refs_2_, bf16[176,256]{1,0:T(8,128)(2,1)} %constant.61.clone.zh, bf16[176,256]{1,0:T(8,128)(2,1)} %constant.62.clone.zl, bf16[192,176]{1,0:T(8,128)(2,1)} %constant.65.clone.yh.ih, ...), custom_call_target="tpu_custom_call" | custom-call | flops 3140222976 | bytes 6262784 | tf_op jit(solution)/shard_map/density_to_ky_kz/pallas_call | solution.py:273
  181.7 3.7 all-to-all-start
  185.5 0.1 broadcast_add_fusion
  185.6 31.8 %fusion.8.w_ref = f32[44,176,256]{2,1,0:T(8,128)} fusion(f32[256]{0:T(256)S(1)} %fusion.12, f32[44,176]{1,0:T(8,128)S(1)} %broadcast_add_fusion), kind=kLoop, calls=%fused_computation.10 | loop fusion | flops 19824640 | bytes 7961856 | tf_op jit(solution)/shard_map/mul | solution.py:60
  217.3 6.1 %all-to-all-done.in_ref = s16[4,66,48,128]{3,2,1,0:T(8,128)(2,1)S(1)} async-done(((s16[4,66,48,128]{3,2,1,0:T(8,128)(2,1)}), s16[4,66,48,128]{3,2,1,0:T(8,128)(2,1)S(1)}, u32[]{:S(2)}, u32[]{:S(2)}) %all-to-all-start) | async-done | bytes 3244064 | tf_op jit(solution)/shard_map/all_to_all | solution.py:286
  223.4 0.0 copy-start.2
  223.4 1.7 copy-done.2
  225.1 24.2 %filter_along_x.2 = s16[4,66,48,128]{3,2,1,0:T(8,128)(2,1)} custom-call(s16[4,66,48,128]{3,2,1,0:T(8,128)(2,1)} %copy-done.2, f32[44,176,256]{2,1,0:T(8,128)} %fusion.8.w_ref, bf16[176,192]{1,0:T(8,128)(2,1)} %constant.67.clone.fh.refs_6_.refs_7_, bf16[176,192]{1,0:T(8,128)(2,1)} %constant.68.clone.fl.refs_7_.refs_8_, ...), custom_call_target="tpu_custom_call" | custom-call | flops 3140222976 | bytes 11444224 | tf_op jit(solution)/shard_map/filter_along_x/pallas_call | solution.py:273
  249.3 3.9 all-to-all-start.1
  253.2 3.7 pad.12
  256.9 9.7 %reshape.71.b_ref.refs_2_ = bf16[48,176,176]{2,1,0:T(8,128)(2,1)} reshape(bf16[48,30976]{1,0:T(8,128)(2,1)} %pad.12) | data formatting | bytes 5947392 | tf_op jit(solution)/shard_map/reshape | solution.py:317
  266.6 29.6 %density_to_ky_kz.3 = s16[4,66,48,128]{3,2,1,0:T(8,128)(2,1)} custom-call(bf16[48,176,176]{2,1,0:T(8,128)(2,1)} %reshape.69.a_ref.refs_1_, bf16[48,176,176]{2,1,0:T(8,128)(2,1)} %reshape.71.b_ref.refs_2_, bf16[176,256]{1,0:T(8,128)(2,1)} %constant.61.clone.zh, bf16[176,256]{1,0:T(8,128)(2,1)} %constant.62.clone.zl, bf16[192,176]{1,0:T(8,128)(2,1)} %constant.65.clone.yh.ih, ...), custom_call_target="tpu_custom_call" | custom-call | flops 3140222976 | bytes 6262784 | tf_op jit(solution)/shard_map/density_to_ky_kz/pallas_call | solution.py:273
  296.2 0.0 all-to-all-done.1.refs_0_
  296.2 0.0 copy-start
  296.2 4.8 all-to-all-start.2
  301.6 1.4 collective-permute-start.2
  303.0 4.1 collective-permute-done.2
  307.8 1.6 collective-permute-start.3
  309.4 2.1 collective-permute-done.3
  312.1 0.6 maximum_maximum_fusion.refs_3_
  312.7 0.0 copy-done
  312.7 28.3 %potential_terms.2 = (f32[48,176,176]{2,1,0:T(8,128)}, s16[68,176,128]{2,1,0:T(8,128)(2,1)}) custom-call(s16[4,66,48,128]{3,2,1,0:T(8,128)(2,1)} %copy-done, bf16[48,176,176]{2,1,0:T(8,128)(2,1)} %reshape.69.a_ref.refs_1_, bf16[48,176,176]{2,1,0:T(8,128)(2,1)} %reshape.70.b_ref.refs_2_, f32[4]{0:T(128)} %maximum_maximum_fusion.refs_3_, ...), custom_call_target="tpu_custom_call" | custom-call | flops 3140222976 | bytes 9588752 | tf_op jit(solution)/shard_map/potential_terms/pallas_call | solution.py:273
  341.1 0.3 collective-permute-start.4
  341.3 0.0 all-to-all-done.2.in_ref
  341.3 24.3 %filter_along_x.3 = s16[4,66,48,128]{3,2,1,0:T(8,128)(2,1)} custom-call(s16[4,66,48,128]{3,2,1,0:T(8,128)(2,1)} %all-to-all-done.2.in_ref, f32[44,176,256]{2,1,0:T(8,128)} %fusion.8.w_ref, bf16[176,192]{1,0:T(8,128)(2,1)} %constant.67.clone.fh.refs_6_.refs_7_, bf16[176,192]{1,0:T(8,128)(2,1)} %constant.68.clone.fl.refs_7_.refs_8_, ...), custom_call_target="tpu_custom_call" | custom-call | flops 3140222976 | bytes 11444224 | tf_op jit(solution)/shard_map/filter_along_x/pallas_call | solution.py:273
  365.7 3.7 all-to-all-start.3
  370.0 0.6 maximum_maximum_fusion.1.refs_3_
  370.6 36.7 %all-to-all-done.3.refs_0_ = s16[4,66,48,128]{3,2,1,0:T(8,128)(2,1)S(1)} async-done(((s16[4,66,48,128]{3,2,1,0:T(8,128)(2,1)}), s16[4,66,48,128]{3,2,1,0:T(8,128)(2,1)S(1)}, u32[]{:S(2)}, u32[]{:S(2)}) %all-to-all-start.3) | async-done | bytes 3244064 | tf_op jit(solution)/shard_map/all_to_all | solution.py:286
  407.3 0.0 copy-start.1
  407.3 0.6 collective-permute-done.4.refs_4_
  407.9 1.1 copy-done.1
  409.0 32.5 %potential_terms.3 = (f32[48,176,176]{2,1,0:T(8,128)}, s16[68,176,128]{2,1,0:T(8,128)(2,1)}) custom-call(s16[4,66,48,128]{3,2,1,0:T(8,128)(2,1)} %copy-done.1, bf16[48,176,176]{2,1,0:T(8,128)(2,1)} %reshape.69.a_ref.refs_1_, bf16[48,176,176]{2,1,0:T(8,128)(2,1)} %reshape.71.b_ref.refs_2_, f32[4]{0:T(128)} %maximum_maximum_fusion.1.refs_3_, ...), custom_call_target="tpu_custom_call" | custom-call | flops 3140222976 | bytes 12652560 | tf_op jit(solution)/shard_map/potential_terms/pallas_call | solution.py:273
  441.5 0.0 collective-permute-start.5
  441.5 68.2 %collective-permute-done.5.arrived = s16[68,176,128]{2,1,0:T(8,128)(2,1)S(1)} collective-permute-done((s16[68,176,128]{2,1,0:T(8,128)(2,1)}, s16[68,176,128]{2,1,0:T(8,128)(2,1)S(1)}, u32[]{:S(2)}, u32[]{:S(2)}) %collective-permute-start.5) | collective-permute-done | bytes 3063840 | tf_op jit(solution)/shard_map/ppermute | solution.py:390
  509.7 0.0 copy-start.5
  509.7 1.6 copy-done.5
  511.3 13.3 %total_terms.1 = f32[48,176,176]{2,1,0:T(8,128)} custom-call(f32[48,176,176]{2,1,0:T(8,128)} %get-tuple-element.9.first_ref, f32[48,176,176]{2,1,0:T(8,128)} %get-tuple-element.11.second_ref, s16[68,176,128]{2,1,0:T(8,128)(2,1)} %copy-done.5), custom_call_target="tpu_custom_call" | custom-call | flops 4460544 | bytes 14958592 | tf_op jit(solution)/shard_map/total_terms/pallas_call | solution.py:273
  524.6 6.9 %slice.4 = f32[44,176,176]{2,1,0:T(8,128)} slice(f32[48,176,176]{2,1,0:T(8,128)} %total_terms.1), slice={[0:44], [0:176], [0:176]} | slice | bytes 10903552 | tf_op jit(solution)/shard_map/slice | solution.py:401
  531.5 12.4 %reshape.73 = f32[1,44,30976]{2,0,1:T(1,128)} reshape(f32[44,176,176]{2,1,0:T(8,128)} %slice.4) | data formatting | bytes 10903552 | tf_op jit(solution)/shard_map/reshape | solution.py:401
  (3 shorter events, 0.0 us)
Async XLA Ops:
  0.0 69.7 %collective-permute-start = (bf16[1,44,30976]{2,1,0:T(8,128)(2,1)}, bf16[1,44,30976]{2,1,0:T(8,128)(2,1)S(1)}, u32[]{:S(2)}, u32[]{:S(2)}) collective-permute-start(bf16[1,44,30976]{2,1,0:T(8,128)(2,1)} %param.14), channel_id=1, source_target_pairs={{0,8},{4,12},{8,16},{12,20},{16,24},{20,28},{24,0},{28,4},{1,9},{5... | collective-permute-start | bytes 8177672 | tf_op jit(solution)/shard_map/ppermute | solution.py:320
  3.0 71.5 %copy-start.3 = (bf16[1,44,30976]{2,1,0:T(8,128)(2,1)S(1)}, bf16[1,44,30976]{2,1,0:T(8,128)(2,1)}, u32[]{:S(2)}) copy-start(bf16[1,44,30976]{2,1,0:T(8,128)(2,1)} %param.14) | copy-start | bytes 8177668
  69.7 4.9 copy-start.4
  74.5 65.9 %collective-permute-start.1 = (bf16[1,44,30976]{2,1,0:T(8,128)(2,1)}, bf16[1,44,30976]{2,1,0:T(8,128)(2,1)}, u32[]{:S(2)}, u32[]{:S(2)}) collective-permute-start(bf16[1,44,30976]{2,1,0:T(8,128)(2,1)} %broadcast_select_fusion), channel_id=1, source_target_pairs={{0,4},{4,0},{8,12},{12,8},{16,20},{20,16},{24,28},{28,24},{1,5},{5... | collective-permute-start | bytes 8177672 | tf_op jit(solution)/shard_map/ppermute | solution.py:321
  181.7 41.7 %all-to-all-start = ((s16[4,66,48,128]{3,2,1,0:T(8,128)(2,1)}), s16[4,66,48,128]{3,2,1,0:T(8,128)(2,1)S(1)}, u32[]{:S(2)}, u32[]{:S(2)}) async-start(s16[4,66,48,128]{3,2,1,0:T(8,128)(2,1)} %density_to_ky_kz.2), calls=%async_computation | async-start | bytes 6488064 | tf_op jit(solution)/shard_map/all_to_all | solution.py:286
  223.4 1.7 copy-start.2
  249.3 46.9 %all-to-all-start.1 = ((s16[4,66,48,128]{3,2,1,0:T(8,128)(2,1)}), s16[4,66,48,128]{3,2,1,0:T(8,128)(2,1)S(1)}, u32[]{:S(2)}, u32[]{:S(2)}) async-start(s16[4,66,48,128]{3,2,1,0:T(8,128)(2,1)} %filter_along_x.2), calls=%async_computation.1 | async-start | bytes 6488064 | tf_op jit(solution)/shard_map/all_to_all | solution.py:286
  296.2 16.5 %copy-start = (s16[4,66,48,128]{3,2,1,0:T(8,128)(2,1)}, s16[4,66,48,128]{3,2,1,0:T(8,128)(2,1)S(1)}, u32[]{:S(2)}) copy-start(s16[4,66,48,128]{3,2,1,0:T(8,128)(2,1)S(1)} %all-to-all-done.1.refs_0_) | copy-start | bytes 9732100
  296.2 45.1 %all-to-all-start.2 = ((s16[4,66,48,128]{3,2,1,0:T(8,128)(2,1)}), s16[4,66,48,128]{3,2,1,0:T(8,128)(2,1)}, u32[]{:S(2)}, u32[]{:S(2)}) async-start(s16[4,66,48,128]{3,2,1,0:T(8,128)(2,1)} %density_to_ky_kz.3), calls=%async_computation.2 | async-start | bytes 6488064 | tf_op jit(solution)/shard_map/all_to_all | solution.py:286
  301.6 5.5 %collective-permute-start.2 = (bf16[1]{0:T(256)(128)(2,1)}, bf16[1]{0:T(256)(128)(2,1)}, u32[]{:S(2)}, u32[]{:S(2)}) collective-permute-start(bf16[1]{0:T(256)(128)(2,1)} %convert_element_type.43), channel_id=1, source_target_pairs={{0,8},{4,12},{8,16},{12,20},{16,24},{20,28},{24,0},{28,4},{1,9},{5... | collective-permute-start | bytes 14 | tf_op jit(solution)/shard_map/ppermute | solution.py:320
  307.8 3.7 collective-permute-start.3
  341.1 66.9 %collective-permute-start.4 = (s16[68,176,128]{2,1,0:T(8,128)(2,1)}, s16[68,176,128]{2,1,0:T(8,128)(2,1)}, u32[]{:S(2)}, u32[]{:S(2)}) collective-permute-start(s16[68,176,128]{2,1,0:T(8,128)(2,1)} %get-tuple-element.10), channel_id=1, source_target_pairs={{0,4},{4,0},{8,12},{12,8},{16,20},{20,16},{24,28},{28,24},{1,5},{5... | collective-permute-start | bytes 9191432 | tf_op jit(solution)/shard_map/ppermute | solution.py:388
  365.7 41.7 %all-to-all-start.3 = ((s16[4,66,48,128]{3,2,1,0:T(8,128)(2,1)}), s16[4,66,48,128]{3,2,1,0:T(8,128)(2,1)S(1)}, u32[]{:S(2)}, u32[]{:S(2)}) async-start(s16[4,66,48,128]{3,2,1,0:T(8,128)(2,1)} %filter_along_x.3), calls=%async_computation.3 | async-start | bytes 6488064 | tf_op jit(solution)/shard_map/all_to_all | solution.py:286
  407.3 1.7 copy-start.1
  441.5 68.2 %collective-permute-start.5 = (s16[68,176,128]{2,1,0:T(8,128)(2,1)}, s16[68,176,128]{2,1,0:T(8,128)(2,1)S(1)}, u32[]{:S(2)}, u32[]{:S(2)}) collective-permute-start(s16[68,176,128]{2,1,0:T(8,128)(2,1)} %get-tuple-element.12), channel_id=1, source_target_pairs={{0,24},{4,28},{8,0},{12,4},{16,8},{20,12},{24,16},{28,20},{1,25},{... | collective-permute-start | bytes 9191432 | tf_op jit(solution)/shard_map/ppermute | solution.py:390
  509.7 1.6 copy-start.5

commit v2 on v1

--- a/solution.py
+++ b/solution.py
@@ -118,19 +118,50 @@
     return first, second
 
 
-def forward_kernel(slab, blocks, block_rows, a_ref, b_ref, zh, zl, yh, yl, out_ref, buf):
-    planes, grid_size = a_ref.shape[0], a_ref.shape[1]
+def group_slices(group_lanes, grid_size):
+    for row in range(group_lanes // grid_size):
+        first, offset = divmod(row * grid_size, 128)
+        yield row, first, offset, -(-(offset + grid_size) // 128)
+
+
+def forward_kernel(slab, blocks, block_rows, a_ref, b_ref, zh, zl, yh, yl, out_ref, dens, rows_z, rows_y, buf):
+    planes, cells = a_ref.shape
+    grid_size = rows_z.shape[0]
     half = out_ref.shape[1] // 3
+    group_lanes = 8 * grid_size
     z_table, y_table = (zh[...], zl[...]), (yh[...], yl[...])
 
-    @pl.loop(0, planes // 8)
+    @pl.loop(0, cells // group_lanes)
+    def _(group):
+        lanes = pl.ds(pl.multiple_of(group * group_lanes, 128), group_lanes)
+        dens[:, lanes] = a_ref[:, lanes].astype(F32) * b_ref[:, lanes].astype(F32)
+
+    @pl.loop(0, planes // 16)
     def _(chunk):
-        rows = pl.ds(pl.multiple_of(chunk * 8, 8), 8)
-        density = a_ref[rows].astype(F32) * b_ref[rows].astype(F32)
-        along_z = times_table(density.reshape(8 * grid_size, grid_size), z_table)
-        along_z = along_z.reshape(8, grid_size, LANES)
-        along_y = jnp.stack([table_times(y_table, along_z[i]) for i in range(8)])
-        buf[:, rows, :] = jnp.transpose(along_y, (1, 0, 2))
+        rows = pl.ds(pl.multiple_of(chunk * 16, 16), 16)
+
+        @pl.loop(0, cells // group_lanes)
+        def _(group):
+            lanes = pl.ds(pl.multiple_of(group * group_lanes, 128), group_lanes)
+            flat = dens[rows, lanes]
+            for row, first, offset, tiles in group_slices(group_lanes, grid_size):
+                window = flat[:, first * 128 : (first + tiles) * 128]
+                if offset:
+                    window = pltpu.roll(window, tiles * 128 - offset, 1)
+                rows_z[group * 8 + row] = window[:, :LANES]
+
+        @pl.loop(0, 2)
+        def _(part):
+            count = grid_size // 2
+            at = pl.ds(pl.multiple_of(part * count, 8), count)
+            along_z = times_table(rows_z[at].reshape(count * 16, LANES), z_table)
+            rows_y[:, at, :] = jnp.transpose(along_z.reshape(count, 16, LANES), (1, 0, 2))
+
+        @pl.loop(0, 2)
+        def _(part):
+            along_y = jnp.stack([table_times(y_table, rows_y[part * 8 + i]) for i in range(8)])
+            at = pl.ds(pl.multiple_of(chunk * 16 + part * 8, 8), 8)
+            buf[:, at, :] = jnp.transpose(along_y, (1, 0, 2))
 
     for block in range(blocks):
 
@@ -163,14 +194,13 @@
         out_ref[:, 2 * half + row] = to_wire(shared_lanes(codes[0], codes[1]))
 
 
-def back_kernel(slab, blocks, block_rows, with_swapped, *refs):
-    if with_swapped:
-        in_ref, a_ref, b_ref, occ, swapped, zh, zl, yh, yl, own_ref, ret_ref, buf, ret = refs
-    else:
-        in_ref, a_ref, b_ref, occ, zh, zl, yh, yl, own_ref, ret_ref, buf, ret = refs
-    planes, grid_size = a_ref.shape[0], a_ref.shape[1]
+def back_kernel(
+    slab, blocks, block_rows, in_ref, a_ref, b_ref, occ, zh, zl, yh, yl, own_ref, ret_ref, buf, rows_z, field
+):
+    planes, cells = a_ref.shape
+    grid_size = rows_z.shape[0]
     half = in_ref.shape[1] // 3
-    halfx = (ret_ref.shape[0] - 2) // 3
+    group_lanes = 8 * grid_size
     z_table, y_table = (zh[...], zl[...]), (yh[...], yl[...])
     home, visitor = -0.5 * occ[0], -0.5 * occ[1]
 
@@ -188,79 +218,37 @@
                 code = jnp.concatenate([from_wire(in_ref[block, at]), upper[i]], axis=-1)
                 buf[base + at] = decoded(code, slab)
 
-    def chunk_at(chunk, largest):
+    @pl.loop(0, planes // 8)
+    def _(chunk):
         rows = pl.ds(pl.multiple_of(chunk * 8, 8), 8)
         mixed = jnp.transpose(buf[:, rows, :], (1, 0, 2))
         along_y = jnp.stack([table_times(y_table, mixed[i]) for i in range(8)])
-        field = times_table(along_y.reshape(8 * grid_size, LANES), z_table)
-        field = field.reshape(8, grid_size, LANES)[..., :grid_size]
-        own_ref[rows] = field * b_ref[rows].astype(F32) * visitor
-        terms = field * a_ref[rows].astype(F32) * home
-        ret[rows] = terms
-        if with_swapped:
-            return largest
-        return jnp.maximum(largest, jnp.max(jnp.abs(terms), axis=0))
-
-    largest = lax.fori_loop(0, planes // 8, chunk_at, jnp.zeros((grid_size, grid_size), F32))
-
-    if with_swapped:
-        add_own, add_ret = occ[2], occ[3]
-        step = plane_steps(swapped, halfx)
-
-        def add_at(row, largest):
-            upper = unshared(from_wire(swapped[2 * halfx + row]))
-            for i in range(2):
-                at = row + i * halfx
-                code = jnp.concatenate([from_wire(swapped[at]), upper[i]], axis=-1)
-                value = (code * step)[:, :grid_size]
-                own_ref[at] = own_ref[at] + value * add_own
-                total = ret[at] + value * add_ret
-                ret[at] = total
-                largest = jnp.maximum(largest, jnp.abs(total))
-            return largest
-
-        largest = lax.fori_loop(0, halfx, add_at, largest)
-
-    exponent = exponent_of(widened(largest))
-    scale = LEVELS / step_of(exponent)
-
-    @pl.loop(0, halfx)
-    def _(row):
-        codes = []
-        for i in range(2):
-            code = jnp.round(widened(ret[row + i * halfx]) * scale)
-            ret_ref[row + i * halfx] = to_wire(code[:, :128])
-            codes.append(code[:, 128:])
-        ret_ref[2 * halfx + row] = to_wire(shared_lanes(codes[0], codes[1]))
-
-    ret_ref[3 * halfx] = to_wire(exponent[:, :128])
-    ret_ref[3 * halfx + 1] = to_wire(exponent[:, 128:])
-
-
-def widened(plane):
-    pad = jnp.zeros((plane.shape[0], LANES - plane.shape[1]), F32)
-    return jnp.concatenate([plane, pad], axis=-1)
-
-
-def plane_steps(wire_ref, halfx):
-    exponent = jnp.concatenate(
-        [from_wire(wire_ref[3 * halfx]), from_wire(wire_ref[3 * halfx + 1])], axis=-1
-    )
-    return step_of(exponent) * (1.0 / LEVELS)
-
-
-def total_kernel(first_ref, second_ref, arrived, out_ref):
-    grid_size = first_ref.shape[1]
-    halfx = (arrived.shape[0] - 2) // 3
-    step = plane_steps(arrived, halfx)
-
-    @pl.loop(0, halfx)
-    def _(row):
-        upper = unshared(from_wire(arrived[2 * halfx + row]))
-        for i in range(2):
-            at = row + i * halfx
-            code = jnp.concatenate([from_wire(arrived[at]), upper[i]], axis=-1)
-            out_ref[at] = first_ref[at] + second_ref[at] + (code * step)[:, :grid_size]
+        along_z = times_table(along_y.reshape(8 * grid_size, LANES), z_table)
+        rows_z[...] = jnp.transpose(along_z.reshape(8, grid_size, LANES), (1, 0, 2))
+
+        @pl.loop(0, cells // group_lanes)
+        def _(group):
+            tiles_of = [None] * (group_lanes // 128)
+            for row, first, offset, tiles in group_slices(group_lanes, grid_size):
+                window = rows_z[group * 8 + row]
+                if tiles * 128 > LANES:
+                    window = jnp.concatenate([window, jnp.zeros((8, tiles * 128 - LANES), F32)], axis=1)
+                if offset:
+                    window = pltpu.roll(window, offset, 1)
+                for tile in range(tiles):
+                    piece = window[:, tile * 128 : (tile + 1) * 128]
+                    before = tiles_of[first + tile]
+                    tiles_of[first + tile] = piece if before is None else before + piece
+            lanes = pl.ds(pl.multiple_of(group * group_lanes, 128), group_lanes)
+            field[rows, lanes] = jnp.concatenate(tiles_of, axis=1)
+
+    @pl.loop(0, cells // group_lanes)
+    def _(group):
+        lanes = pl.ds(pl.multiple_of(group * group_lanes, 128), group_lanes)
+        potential = field[:, lanes]
+        own_ref[:, lanes] = potential * b_ref[:, lanes].astype(F32) * visitor
+        terms = potential * a_ref[:, lanes].astype(F32) * home
+        ret_ref[:, lanes] = to_wire(coded(terms, slab))
 
 
 def call(kernel, out_shape, scratch, name, flops, *operands, smem=()):
@@ -297,13 +285,11 @@
     ky_rows = blocks * block_rows
 
     table = cas_table(grid_size)
-    lanes_table = np.zeros((grid_size, LANES))
-    lanes_table[:, :grid_size] = table
     square_table = np.zeros((LANES, LANES))
     square_table[:grid_size, :grid_size] = table
     to_ky = spread_rows(table, blocks, slab, block_rows)
     to_x = spread_rows(table, blocks, slab, planes)
-    z_forward, z_back = high_low(lanes_table), high_low(square_table)
+    z_back = high_low(square_table)
     y_forward, y_back = high_low(to_ky), high_low(to_ky.T)
     x_forward, x_back = high_low(to_x.T), high_low(to_x)
     profile = truncated_kernel(grid_size, slab, 2 * half)
@@ -314,26 +300,36 @@
     swap = [(i, i ^ 1) for i in range(bands)]
     is_odd = lax.axis_index("band") % 2 == 1
 
-    wide = lambda psi: jnp.pad(psi[0], ((0, planes - slab), (0, 0))).reshape(
-        planes, grid_size, grid_size
-    )
-    far, far_occ = lax.ppermute((wavefunctions, occupied), "band", upward)
-    near, near_occ = lax.ppermute(
-        (jnp.where(is_odd, far, wavefunctions), jnp.where(is_odd, far_occ, occupied)), "band", swap
-    )
-    home = wide(wavefunctions)
+    cells = grid_size * grid_size
+    home = jnp.pad(wavefunctions[0], ((0, planes - slab), (0, 0)))
+    home_first, home_second = home[:, : cells // 2], home[:, cells // 2 :]
+    far_occ = lax.ppermute(occupied, "band", upward)
+    near_occ = lax.ppermute(jnp.where(is_odd, far_occ, occupied), "band", swap)
+    far_first = lax.ppermute(home_first, "band", upward)
+    home_later, far_first = lax.optimization_barrier((home_second, far_first))
+    far_second = lax.ppermute(home_later, "band", upward)
+    near_first = lax.ppermute(jnp.where(is_odd, far_first, home_first), "band", swap)
+    near_second = lax.ppermute(jnp.where(is_odd, far_second, home_second), "band", swap)
+    far_field = jnp.concatenate([far_first, far_second], axis=1)
+    near_field = jnp.concatenate([near_first, near_second], axis=1)
+    far_field, profile = lax.optimization_barrier((far_field, profile))
     flops = 12 * planes * grid_size**3
 
     def forward(visitor):
         return call(
             functools.partial(forward_kernel, slab, blocks, block_rows),
             jax.ShapeDtypeStruct((blocks, 3 * half, planes, 128), jnp.int16),
-            [pltpu.VMEM((ky_rows, planes, LANES), F32)],
+            [
+                pltpu.VMEM((planes, cells), F32),
+                pltpu.VMEM((grid_size, 16, LANES), F32),
+                pltpu.VMEM((16, grid_size, LANES), F32),
+                pltpu.VMEM((ky_rows, planes, LANES), F32),
+            ],
             "density_to_ky_kz",
             flops,
             home,
             visitor,
-            *z_forward,
+            *z_back,
             *y_forward,
         )
 
@@ -350,17 +346,17 @@
             *x_back,
         )
 
-    def back(wire, visitor, factors, swapped=None):
-        extra = [] if swapped is None else [swapped]
+    def back(wire, visitor, factors):
         return call(
-            functools.partial(back_kernel, slab, blocks, block_rows, swapped is not None),
+            functools.partial(back_kernel, slab, blocks, block_rows),
             [
-                jax.ShapeDtypeStruct((planes, grid_size, grid_size), F32),
-                jax.ShapeDtypeStruct((3 * half + 2, grid_size, 128), jnp.int16),
+                jax.ShapeDtypeStruct((planes, cells), F32),
+                jax.ShapeDtypeStruct((planes, cells), jnp.int16),
             ],
             [
                 pltpu.VMEM((ky_rows, planes, LANES), F32),
-                pltpu.VMEM((planes, grid_size, grid_size), F32),
+                pltpu.VMEM((grid_size, 8, LANES), F32),
+                pltpu.VMEM((planes, cells), F32),
             ],
             "potential_terms",
             flops,
@@ -368,37 +364,30 @@
             home,
             visitor,
             factors,
-            *extra,
             *z_back,
             *y_back,
             smem=(3,),
         )
 
-    far_field, near_field = wide(far), wide(near)
-    odd = is_odd.astype(F32)
     home_occ = occupied.astype(F32)[0]
-    near_factors = jnp.stack([home_occ, near_occ.astype(F32)[0], 1.0 - odd, odd])
-    far_factors = jnp.stack([home_occ, far_occ.astype(F32)[0], 1.0 - odd, odd])
-
+    near_factors = jnp.stack([home_occ, near_occ.astype(F32)[0]])
+    far_factors = jnp.stack([home_occ, far_occ.astype(F32)[0]])
+
+    far_wire = exchange(forward(far_field))
     near_wire = exchange(forward(near_field))
-    far_wire = exchange(forward(far_field))
+    far_wire = exchange(filtered(far_wire))
     near_wire = exchange(filtered(near_wire))
-    far_wire = exchange(filtered(far_wire))
+    far_own, far_return = back(far_wire, far_field, far_factors)
+    far_arrived = lax.ppermute(far_return, "band", downward)
     near_own, near_return = back(near_wire, near_field, near_factors)
-    swapped = lax.ppermute(near_return, "band", swap)
-    far_own, far_return = back(far_wire, far_field, far_factors, swapped)
-    arrived = lax.ppermute(far_return, "band", downward)
-    total = call(
-        total_kernel,
-        jax.ShapeDtypeStruct((planes, grid_size, grid_size), F32),
-        [],
-        "total_terms",
-        3 * planes * grid_size**2,
-        near_own,
-        far_own,
-        arrived,
-    )
-    return total[:slab].reshape(1, slab, grid_size * grid_size)
+    near_arrived = lax.ppermute(near_return, "band", [(i, (i - 1) % bands) for i in range(bands)])
+
+    def terms_of(arrived):
+        code = arrived.astype(F32)
+        return code[:slab] * (step_of(code[slab : slab + 1]) * (1.0 / LEVELS))
+
+    total = far_own[:slab] + near_own[:slab] + terms_of(far_arrived) + terms_of(near_arrived)
+    return total[None]
 
 
 def solution(mesh):

time: 545 us -> 462 us (0.85)
  waiting for transfers between devices: 240 us -> 172 us
  local copies, waits for them, and re-layouts: 58.6 us -> 20.8 us
  other arithmetic: 37.9 us -> 47.1 us
  Pallas kernels: 182 us -> 190 us
  starting transfers between devices: 22.4 us -> 27.9 us
    ppermute x6 -> x8, waiting for transfers between devices: 198 us -> 144 us  [the longest x1 56.5 us: shards(): lax.ppermute(near_return, 'band', [(i, (i - 1) % bands) for i in range(ba...]
    reshape x4 -> x0, local copies, waits for them, and re-layouts: 41.4 us -> none  [the longest x3 29.1 us: shards(): jnp.pad(psi[0], ((0, planes - slab), (0, 0)))]
    all_to_all x4, waiting for transfers between devices: 42.8 us -> 27.7 us  [exchange(): return lax.all_to_all(wire, 'fft', split_axis=0, concat_axis=0, tiled=True)]
    pallas_call x7 -> x6, Pallas kernels: 182 us -> 190 us  [call(): pl.pallas_call(kernel, out_shape=out_shape, in_specs=specs, out_specs=[si...]
    broadcast_in_dim x0 -> x1, local copies, waits for them, and re-layouts: none -> 6.66 us  [shards(): return total[None]]
    ppermute x6 -> x8, starting transfers between devices: 6.31 us -> 12.1 us  [the longest x1 3.11 us: shards(): near_occ = lax.ppermute(jnp.where(is_odd, far_occ, occupied), 'band', swap)]
  transfers between devices with their start and end apart: 10 -> 12, of which waited for: 8 -> 8; matrix products, arithmetic and copies ran while one was open for 10% -> 10% of each run, Pallas kernels for 15% -> 41%
where the time goes in v2:
time: 462 us; the launch traced here: 461 us
  Pallas kernels  190 us (41%)
  waiting for transfers between devices  172 us (37%)
  other arithmetic  47.1 us (10%)
  starting transfers between devices  27.9 us (6%)
  local copies, waits for them, and re-layouts  20.8 us (5%)
    pallas_call x6, Pallas kernels, call(): pl.pallas_call(kernel, out_shape=out_shape, in_specs=specs, out_specs=[si...  190 us
    ppermute x1, waiting for transfers between devices, shards(): lax.ppermute(near_return, 'band', [(i, (i - 1) % bands) for i in range(ba...  56.5 us
    ppermute x1, waiting for transfers between devices, shards(): far_first = lax.ppermute(home_first, 'band', upward)  34.9 us
    mul x1, other arithmetic, truncated_kernel(): return profile * (0.25 / float(grid_size) ** 1.5)  31.8 us
    all_to_all x4, waiting for transfers between devices, exchange(): return lax.all_to_all(wire, 'fft', split_axis=0, concat_axis=0, tiled=True)  27.7 us
    ppermute x1, waiting for transfers between devices, shards(): far_arrived = lax.ppermute(far_return, 'band', downward)  25.9 us
    ppermute x1, waiting for transfers between devices, shards(): lax.ppermute(jnp.where(is_odd, far_second, home_second), 'band', swap)  20.7 us
    all_to_all x4, starting transfers between devices, exchange(): return lax.all_to_all(wire, 'fft', split_axis=0, concat_axis=0, tiled=True)  15.8 us
  transfers between devices with their start and end apart: 12, of which 8 were waited for; matrix products, arithmetic and copies ran while one was open for 10% of the time, Pallas kernels for 41%

profile of v2, /device:TPU:0, one launch (start us, length us, event | category | flops | bytes accessed | tf_op | source)
XLA Modules:
  0.0 460.8 jit_solution(1827909983812762982)
XLA Ops:
  0.0 0.0 copy-start
  0.0 3.8 pad_slice_fusion
  3.8 3.0 collective-permute-start
  6.8 34.9 %collective-permute-done = bf16[48,15488]{1,0:T(8,128)(2,1)} collective-permute-done((bf16[48,15488]{1,0:T(8,128)(2,1)}, bf16[48,15488]{1,0:T(8,128)(2,1)}, u32[]{:S(2)}, u32[]{:S(2)}) %collective-permute-start) | collective-permute-done | bytes 1486880 | tf_op jit(solution)/shard_map/ppermute | solution.py:308
  41.7 0.0 collective-permute-start.1
  41.7 0.1 broadcast_add_fusion
  41.8 0.0 copy-done
  41.8 1.8 pad.4.a_ref
  43.6 31.8 %fusion.8.w_ref = f32[44,176,256]{2,1,0:T(8,128)} fusion(f32[256]{0:T(256)S(1)} %fusion.21, f32[44,176]{1,0:T(8,128)S(1)} %broadcast_add_fusion), kind=kLoop, calls=%fused_computation.10 | loop fusion | flops 19824640 | bytes 7961856 | tf_op jit(solution)/shard_map/mul | solution.py:60
  75.3 2.2 collective-permute-done.1
  77.6 2.3 broadcast_select_fusion
  79.9 3.1 collective-permute-start.3
  83.0 0.0 collective-permute-start.4
  83.0 3.7 pad_maximum_fusion.b_ref
  86.7 32.3 %density_to_ky_kz.2 = s16[4,66,48,128]{3,2,1,0:T(8,128)(2,1)} custom-call(bf16[48,30976]{1,0:T(8,128)(2,1)} %pad.4.a_ref, bf16[48,30976]{1,0:T(8,128)(2,1)} %pad_maximum_fusion.b_ref, bf16[256,256]{1,0:T(8,128)(2,1)} %constant.64.clone.zh, bf16[256,256]{1,0:T(8,128)(2,1)} %constant.65.clone.zl, bf16[192,176]{1,0:T(8,128)(2,1)} %constant.66.clone.yh.ih, ...), custom_call_target="tpu_custom_call" | custom-call | flops 3140222976 | bytes 6344704 | tf_op jit(solution)/shard_map/density_to_ky_kz/pallas_call | solution.py:261
  119.0 3.7 all-to-all-start
  122.7 0.0 collective-permute-done.3
  122.7 2.6 constant_dynamic-update-slice_fusion.1
  125.3 20.7 %collective-permute-done.4 = bf16[48,15488]{1,0:T(8,128)(2,1)} collective-permute-done((bf16[48,15488]{1,0:T(8,128)(2,1)}, bf16[48,15488]{1,0:T(8,128)(2,1)}, u32[]{:S(2)}, u32[]{:S(2)}) %collective-permute-start.4) | collective-permute-done | bytes 1486880 | tf_op jit(solution)/shard_map/ppermute | solution.py:312
  146.0 2.6 constant_dynamic-update-slice_fusion.b_ref
  148.6 32.3 %density_to_ky_kz.3 = s16[4,66,48,128]{3,2,1,0:T(8,128)(2,1)} custom-call(bf16[48,30976]{1,0:T(8,128)(2,1)} %pad.4.a_ref, bf16[48,30976]{1,0:T(8,128)(2,1)} %constant_dynamic-update-slice_fusion.b_ref, bf16[256,256]{1,0:T(8,128)(2,1)} %constant.64.clone.zh, bf16[256,256]{1,0:T(8,128)(2,1)} %constant.65.clone.zl, bf16[192,176]{1,0:T(8,128)(2,1)} %constant.66.clone.yh.ih, ...), custom_call_target="tpu_custom_call" | custom-call | flops 3140222976 | bytes 6344704 | tf_op jit(solution)/shard_map/density_to_ky_kz/pallas_call | solution.py:261
  180.8 0.0 all-to-all-done.in_ref
  180.9 0.0 copy-start.1
  180.9 4.7 %all-to-all-start.2 = ((s16[4,66,48,128]{3,2,1,0:T(8,128)(2,1)}), s16[4,66,48,128]{3,2,1,0:T(8,128)(2,1)}, u32[]{:S(2)}, u32[]{:S(2)}) async-start(s16[4,66,48,128]{3,2,1,0:T(8,128)(2,1)} %density_to_ky_kz.3), calls=%async_computation.2 | async-start | bytes 6488064 | tf_op jit(solution)/shard_map/all_to_all | solution.py:274
  185.5 0.0 copy-done.1
  185.6 24.1 %filter_along_x.2 = s16[4,66,48,128]{3,2,1,0:T(8,128)(2,1)} custom-call(s16[4,66,48,128]{3,2,1,0:T(8,128)(2,1)} %copy-done.1, f32[44,176,256]{2,1,0:T(8,128)} %fusion.8.w_ref, bf16[176,192]{1,0:T(8,128)(2,1)} %constant.68.clone.fh.yh, bf16[176,192]{1,0:T(8,128)(2,1)} %constant.69.clone.fl.yl, bf16[192,176]{1,0:T(8,128)(2,1)} %constant.66.clone.yh.ih, ...), custom_call_target="tpu_custom_call" | custom-call | flops 3140222976 | bytes 11444224 | tf_op jit(solution)/shard_map/filter_along_x/pallas_call | solution.py:261
  209.7 13.9 %all-to-all-done.2.in_ref = s16[4,66,48,128]{3,2,1,0:T(8,128)(2,1)} async-done(((s16[4,66,48,128]{3,2,1,0:T(8,128)(2,1)}), s16[4,66,48,128]{3,2,1,0:T(8,128)(2,1)}, u32[]{:S(2)}, u32[]{:S(2)}) %all-to-all-start.2) | async-done | bytes 3244064 | tf_op jit(solution)/shard_map/all_to_all | solution.py:274
  223.6 3.7 all-to-all-start.1
  227.3 24.1 %filter_along_x.3 = s16[4,66,48,128]{3,2,1,0:T(8,128)(2,1)} custom-call(s16[4,66,48,128]{3,2,1,0:T(8,128)(2,1)} %all-to-all-done.2.in_ref, f32[44,176,256]{2,1,0:T(8,128)} %fusion.8.w_ref, bf16[176,192]{1,0:T(8,128)(2,1)} %constant.68.clone.fh.yh, bf16[176,192]{1,0:T(8,128)(2,1)} %constant.69.clone.fl.yl, bf16[192,176]{1,0:T(8,128)(2,1)} %constant.66.clone.yh.ih, ...), custom_call_target="tpu_custom_call" | custom-call | flops 3140222976 | bytes 11444224 | tf_op jit(solution)/shard_map/filter_along_x/pallas_call | solution.py:261
  251.4 13.8 %all-to-all-done.1.in_ref = s16[4,66,48,128]{3,2,1,0:T(8,128)(2,1)S(1)} async-done(((s16[4,66,48,128]{3,2,1,0:T(8,128)(2,1)}), s16[4,66,48,128]{3,2,1,0:T(8,128)(2,1)S(1)}, u32[]{:S(2)}, u32[]{:S(2)}) %all-to-all-start.1) | async-done | bytes 3244064 | tf_op jit(solution)/shard_map/all_to_all | solution.py:274
  265.3 0.0 copy-start.3
  265.3 1.7 copy-done.3
  266.9 3.7 all-to-all-start.3
  271.3 1.5 collective-permute-start.2
  272.8 4.0 collective-permute-done.2
  277.5 3.1 collective-permute-start.5
  281.3 0.6 pad_maximum_fusion.1.occ
  281.9 0.0 collective-permute-done.5
  282.5 0.6 pad_maximum_fusion.2.occ
  283.1 38.7 %potential_terms.2 = (f32[48,30976]{1,0:T(8,128)}, s16[48,30976]{1,0:T(8,128)(2,1)}) custom-call(s16[4,66,48,128]{3,2,1,0:T(8,128)(2,1)} %copy-done.3, bf16[48,30976]{1,0:T(8,128)(2,1)} %pad.4.a_ref, bf16[48,30976]{1,0:T(8,128)(2,1)} %pad_maximum_fusion.b_ref, f32[2]{0:T(128)} %pad_maximum_fusion.1.occ, bf16[256,256]{1,0:T(8,128)(2,1)} %constant.64.clone.zh, ...), custom_call_target="tpu_custom_call" | custom-call | flops 3140222976 | bytes 9588744 | tf_op jit(solution)/shard_map/potential_terms/pallas_call | solution.py:261
  321.8 0.7 collective-permute-start.6
  322.5 0.0 all-to-all-done.3.in_ref
  322.5 0.0 copy-start.2
  322.5 1.7 copy-done.2
  324.2 38.8 %potential_terms.3 = (f32[48,30976]{1,0:T(8,128)}, s16[48,30976]{1,0:T(8,128)(2,1)}) custom-call(s16[4,66,48,128]{3,2,1,0:T(8,128)(2,1)} %copy-done.2, bf16[48,30976]{1,0:T(8,128)(2,1)} %pad.4.a_ref, bf16[48,30976]{1,0:T(8,128)(2,1)} %constant_dynamic-update-slice_fusion.b_ref, f32[2]{0:T(128)} %pad_maximum_fusion.2.occ, ...), custom_call_target="tpu_custom_call" | custom-call | flops 3140222976 | bytes 9588744 | tf_op jit(solution)/shard_map/potential_terms/pallas_call | solution.py:261
  363.1 0.5 collective-permute-start.7
  363.6 25.9 %collective-permute-done.6 = s16[48,30976]{1,0:T(8,128)(2,1)} collective-permute-done((s16[48,30976]{1,0:T(8,128)(2,1)}, s16[48,30976]{1,0:T(8,128)(2,1)}, u32[]{:S(2)}, u32[]{:S(2)}) %collective-permute-start.6) | collective-permute-done | bytes 2973728 | tf_op jit(solution)/shard_map/ppermute | solution.py:381
  389.5 0.0 slice-start
  389.5 2.8 convert_element_type.48
  392.2 0.5 fusion.17
  392.7 0.0 slice-start.1
  392.7 56.5 %collective-permute-done.7 = s16[48,30976]{1,0:T(8,128)(2,1)S(1)} collective-permute-done((s16[48,30976]{1,0:T(8,128)(2,1)}, s16[48,30976]{1,0:T(8,128)(2,1)S(1)}, u32[]{:S(2)}, u32[]{:S(2)}) %collective-permute-start.7) | collective-permute-done | bytes 2973728 | tf_op jit(solution)/shard_map/ppermute | solution.py:383
  449.2 0.8 convert_element_type.49
  450.0 0.5 fusion.14
  450.5 0.0 slice-done
  450.5 0.0 slice-done.1
  450.5 3.6 fusion.10
  454.1 6.7 %copy.13 = f32[1,44,30976]{2,0,1:T(1,128)} copy(f32[1,44,30976]{2,1,0:T(8,128)S(1)} %fusion.10) | data formatting | bytes 10903552 | tf_op jit(solution)/shard_map/broadcast_in_dim | solution.py:390
  (4 shorter events, 0.0 us)
Async XLA Ops:
  0.0 41.8 %copy-start = (bf16[1,44,30976]{2,1,0:T(8,128)(2,1)S(1)}, bf16[1,44,30976]{2,1,0:T(8,128)(2,1)}, u32[]{:S(2)}) copy-start(bf16[1,44,30976]{2,1,0:T(8,128)(2,1)} %param.12) | copy-start | bytes 8177668
  3.8 37.9 %collective-permute-start = (bf16[48,15488]{1,0:T(8,128)(2,1)}, bf16[48,15488]{1,0:T(8,128)(2,1)}, u32[]{:S(2)}, u32[]{:S(2)}) collective-permute-start(bf16[48,15488]{1,0:T(8,128)(2,1)} %get-tuple-element.23), channel_id=1, source_target_pairs={{0,8},{4,12},{8,16},{12,20},{16,24},{20,28},{24,0},{28,4},{1,9},{5... | collective-permute-start | bytes 4460552 | tf_op jit(solution)/shard_map/ppermute | solution.py:308
  41.7 35.9 %collective-permute-start.1 = (bf16[48,15488]{1,0:T(8,128)(2,1)}, bf16[48,15488]{1,0:T(8,128)(2,1)}, u32[]{:S(2)}, u32[]{:S(2)}) collective-permute-start(bf16[48,15488]{1,0:T(8,128)(2,1)} %get-tuple-element.14), channel_id=1, source_target_pairs={{0,8},{4,12},{8,16},{12,20},{16,24},{20,28},{24,0},{28,4},{1,9},{5... | collective-permute-start | bytes 4460552 | tf_op jit(solution)/shard_map/ppermute | solution.py:310
  79.9 42.8 %collective-permute-start.3 = (bf16[48,15488]{1,0:T(8,128)(2,1)}, bf16[48,15488]{1,0:T(8,128)(2,1)}, u32[]{:S(2)}, u32[]{:S(2)}) collective-permute-start(bf16[48,15488]{1,0:T(8,128)(2,1)} %get-tuple-element.22), channel_id=1, source_target_pairs={{0,4},{4,0},{8,12},{12,8},{16,20},{20,16},{24,28},{28,24},{1,5},{5... | collective-permute-start | bytes 4460552 | tf_op jit(solution)/shard_map/ppermute | solution.py:311
  83.0 63.0 %collective-permute-start.4 = (bf16[48,15488]{1,0:T(8,128)(2,1)}, bf16[48,15488]{1,0:T(8,128)(2,1)}, u32[]{:S(2)}, u32[]{:S(2)}) collective-permute-start(bf16[48,15488]{1,0:T(8,128)(2,1)} %get-tuple-element.21), channel_id=1, source_target_pairs={{0,4},{4,0},{8,12},{12,8},{16,20},{20,16},{24,28},{28,24},{1,5},{5... | collective-permute-start | bytes 4460552 | tf_op jit(solution)/shard_map/ppermute | solution.py:312
  119.0 61.9 %all-to-all-start = ((s16[4,66,48,128]{3,2,1,0:T(8,128)(2,1)}), s16[4,66,48,128]{3,2,1,0:T(8,128)(2,1)S(1)}, u32[]{:S(2)}, u32[]{:S(2)}) async-start(s16[4,66,48,128]{3,2,1,0:T(8,128)(2,1)} %density_to_ky_kz.2), calls=%async_computation | async-start | bytes 6488064 | tf_op jit(solution)/shard_map/all_to_all | solution.py:274
  180.9 4.7 %copy-start.1 = (s16[4,66,48,128]{3,2,1,0:T(8,128)(2,1)}, s16[4,66,48,128]{3,2,1,0:T(8,128)(2,1)S(1)}, u32[]{:S(2)}) copy-start(s16[4,66,48,128]{3,2,1,0:T(8,128)(2,1)S(1)} %all-to-all-done.in_ref) | copy-start | bytes 9732100
  180.9 42.7 %all-to-all-start.2 = ((s16[4,66,48,128]{3,2,1,0:T(8,128)(2,1)}), s16[4,66,48,128]{3,2,1,0:T(8,128)(2,1)}, u32[]{:S(2)}, u32[]{:S(2)}) async-start(s16[4,66,48,128]{3,2,1,0:T(8,128)(2,1)} %density_to_ky_kz.3), calls=%async_computation.2 | async-start | bytes 6488064 | tf_op jit(solution)/shard_map/all_to_all | solution.py:274
  223.6 41.7 %all-to-all-start.1 = ((s16[4,66,48,128]{3,2,1,0:T(8,128)(2,1)}), s16[4,66,48,128]{3,2,1,0:T(8,128)(2,1)S(1)}, u32[]{:S(2)}, u32[]{:S(2)}) async-start(s16[4,66,48,128]{3,2,1,0:T(8,128)(2,1)} %filter_along_x.2), calls=%async_computation.1 | async-start | bytes 6488064 | tf_op jit(solution)/shard_map/all_to_all | solution.py:274
  265.3 1.7 copy-start.3
  266.9 55.6 %all-to-all-start.3 = ((s16[4,66,48,128]{3,2,1,0:T(8,128)(2,1)}), s16[4,66,48,128]{3,2,1,0:T(8,128)(2,1)S(1)}, u32[]{:S(2)}, u32[]{:S(2)}) async-start(s16[4,66,48,128]{3,2,1,0:T(8,128)(2,1)} %filter_along_x.3), calls=%async_computation.3 | async-start | bytes 6488064 | tf_op jit(solution)/shard_map/all_to_all | solution.py:274
  271.3 5.5 %collective-permute-start.2 = (bf16[1]{0:T(256)(128)(2,1)}, bf16[1]{0:T(256)(128)(2,1)}, u32[]{:S(2)}, u32[]{:S(2)}) collective-permute-start(bf16[1]{0:T(256)(128)(2,1)} %convert_element_type.44), channel_id=1, source_target_pairs={{0,8},{4,12},{8,16},{12,20},{16,24},{20,28},{24,0},{28,4},{1,9},{5... | collective-permute-start | bytes 14 | tf_op jit(solution)/shard_map/ppermute | solution.py:306
  277.5 4.4 collective-permute-start.5
  321.8 67.7 %collective-permute-start.6 = (s16[48,30976]{1,0:T(8,128)(2,1)}, s16[48,30976]{1,0:T(8,128)(2,1)}, u32[]{:S(2)}, u32[]{:S(2)}) collective-permute-start(s16[48,30976]{1,0:T(8,128)(2,1)} %get-tuple-element.19), channel_id=1, source_target_pairs={{0,24},{4,28},{8,0},{12,4},{16,8},{20,12},{24,16},{28,20},{1,25},{... | collective-permute-start | bytes 8921096 | tf_op jit(solution)/shard_map/ppermute | solution.py:381
  322.5 1.7 copy-start.2
  363.1 86.1 %collective-permute-start.7 = (s16[48,30976]{1,0:T(8,128)(2,1)}, s16[48,30976]{1,0:T(8,128)(2,1)S(1)}, u32[]{:S(2)}, u32[]{:S(2)}) collective-permute-start(s16[48,30976]{1,0:T(8,128)(2,1)} %get-tuple-element.20), channel_id=1, source_target_pairs={{0,28},{4,0},{8,4},{12,8},{16,12},{20,16},{24,20},{28,24},{1,29},{... | collective-permute-start | bytes 8921096 | tf_op jit(solution)/shard_map/ppermute | solution.py:383
  389.5 61.0 %slice-start = ((s8[5947392]{0:T(1024)(128)(4,1)}), s8[4194304]{0:T(1024)(128)(4,1)S(1)}, s32[]{:S(2)}) async-start(s8[5947392]{0:T(1024)(128)(4,1)} %bitcast.7), calls=%async_computation.4 | async-start | bytes 8388608
  392.7 57.8 %slice-start.1 = ((s8[5947392]{0:T(1024)(128)(4,1)}), s8[1753088]{0:T(1024)(128)(4,1)S(1)}, s32[]{:S(2)}) async-start(s8[5947392]{0:T(1024)(128)(4,1)} %bitcast.7), calls=%async_computation.5 | async-start | bytes 3506176

commit v3 on v2

--- a/solution.py
+++ b/solution.py
@@ -26,11 +26,11 @@
     return np.cos(phases) + np.sin(phases)
 
 
-def high_low(table):
+def high_low(table, axis):
     table = table.astype(np.float32)
     high = table.astype(BF16)
     low = (table - high.astype(np.float32)).astype(BF16)
-    return jnp.asarray(high), jnp.asarray(low)
+    return jnp.asarray(np.concatenate([high, high, low], axis=axis))
 
 
 def spread_rows(table, blocks, slab, block_rows):
@@ -71,12 +71,12 @@
 
 def times_table(value, table):
     high, low = parts_of(value)
-    return dot(high, table[0]) + (dot(low, table[0]) + dot(high, table[1]))
+    return dot(jnp.concatenate([high, low, high], axis=1), table)
 
 
 def table_times(table, value):
     high, low = parts_of(value)
-    return dot(table[0], high) + (dot(table[0], low) + dot(table[1], high))
+    return dot(table, jnp.concatenate([high, low, high], axis=0))
 
 
 def exponent_of(largest):
@@ -124,12 +124,12 @@
         yield row, first, offset, -(-(offset + grid_size) // 128)
 
 
-def forward_kernel(slab, blocks, block_rows, a_ref, b_ref, zh, zl, yh, yl, out_ref, dens, rows_z, rows_y, buf):
+def forward_kernel(slab, blocks, block_rows, a_ref, b_ref, z_ref, y_ref, out_ref, dens, rows_z, rows_y, buf):
     planes, cells = a_ref.shape
     grid_size = rows_z.shape[0]
     half = out_ref.shape[1] // 3
     group_lanes = 8 * grid_size
-    z_table, y_table = (zh[...], zl[...]), (yh[...], yl[...])
+    z_table, y_table = z_ref[...], y_ref[...]
 
     @pl.loop(0, cells // group_lanes)
     def _(group):
@@ -140,7 +140,7 @@
     def _(chunk):
         rows = pl.ds(pl.multiple_of(chunk * 16, 16), 16)
 
-        @pl.loop(0, cells // group_lanes)
+        @pl.loop(0, cells // group_lanes, unroll=2)
         def _(group):
             lanes = pl.ds(pl.multiple_of(group * group_lanes, 128), group_lanes)
             flat = dens[rows, lanes]
@@ -163,10 +163,9 @@
             at = pl.ds(pl.multiple_of(chunk * 16 + part * 8, 8), 8)
             buf[:, at, :] = jnp.transpose(along_y, (1, 0, 2))
 
-    for block in range(blocks):
-
-        @pl.loop(0, half)
-        def _(row):
+    @pl.loop(0, half)
+    def _(row):
+        for block in range(blocks):
             first = coded(buf[block * block_rows + row], slab)
             second = coded(buf[block * block_rows + half + row], slab)
             out_ref[block, row] = to_wire(first[:, :128])
@@ -174,11 +173,11 @@
             out_ref[block, 2 * half + row] = to_wire(shared_lanes(first[:, 128:], second[:, 128:]))
 
 
-def filter_kernel(slab, in_ref, w_ref, fh, fl, ih, il, out_ref):
+def filter_kernel(slab, in_ref, w_ref, forward_ref, inverse_ref, out_ref):
     blocks, half, planes = in_ref.shape[0], in_ref.shape[1] // 3, in_ref.shape[2]
-    forward, inverse = (fh[...], fl[...]), (ih[...], il[...])
-
-    @pl.loop(0, half)
+    forward, inverse = forward_ref[...], inverse_ref[...]
+
+    @pl.loop(0, half, unroll=2)
     def _(row):
         upper = unshared(from_wire(in_ref[:, 2 * half + row]))
         codes = []
@@ -195,13 +194,13 @@
 
 
 def back_kernel(
-    slab, blocks, block_rows, in_ref, a_ref, b_ref, occ, zh, zl, yh, yl, own_ref, ret_ref, buf, rows_z, field
+    slab, blocks, block_rows, in_ref, a_ref, b_ref, occ, z_ref, y_ref, own_ref, ret_ref, buf, rows_z, field
 ):
     planes, cells = a_ref.shape
     grid_size = rows_z.shape[0]
     half = in_ref.shape[1] // 3
     group_lanes = 8 * grid_size
-    z_table, y_table = (zh[...], zl[...]), (yh[...], yl[...])
+    z_table, y_table = z_ref[...], y_ref[...]
     home, visitor = -0.5 * occ[0], -0.5 * occ[1]
 
     for block in range(blocks):
@@ -210,8 +209,10 @@
             (block_rows - 2 * half, planes, LANES), F32
         )
 
-        @pl.loop(0, half)
-        def _(row):
+    @pl.loop(0, half)
+    def _(row):
+        for block in range(blocks):
+            base = block * block_rows
             upper = unshared(from_wire(in_ref[block, 2 * half + row]))
             for i in range(2):
                 at = row + i * half
@@ -226,7 +227,7 @@
         along_z = times_table(along_y.reshape(8 * grid_size, LANES), z_table)
         rows_z[...] = jnp.transpose(along_z.reshape(8, grid_size, LANES), (1, 0, 2))
 
-        @pl.loop(0, cells // group_lanes)
+        @pl.loop(0, cells // group_lanes, unroll=2)
         def _(group):
             tiles_of = [None] * (group_lanes // 128)
             for row, first, offset, tiles in group_slices(group_lanes, grid_size):
@@ -289,9 +290,9 @@
     square_table[:grid_size, :grid_size] = table
     to_ky = spread_rows(table, blocks, slab, block_rows)
     to_x = spread_rows(table, blocks, slab, planes)
-    z_back = high_low(square_table)
-    y_forward, y_back = high_low(to_ky), high_low(to_ky.T)
-    x_forward, x_back = high_low(to_x.T), high_low(to_x)
+    z_table = high_low(square_table, 0)
+    y_forward, y_back = high_low(to_ky, 1), high_low(to_ky.T, 1)
+    x_forward, x_back = high_low(to_x.T, 1), high_low(to_x, 1)
     profile = truncated_kernel(grid_size, slab, 2 * half)
 
     occupied = band_occ.astype(BF16)
@@ -329,8 +330,8 @@
             flops,
             home,
             visitor,
-            *z_back,
-            *y_forward,
+            z_table,
+            y_forward,
         )
 
     def filtered(wire):
@@ -342,8 +343,8 @@
             flops,
             wire,
             profile,
-            *x_forward,
-            *x_back,
+            x_forward,
+            x_back,
         )
 
     def back(wire, visitor, factors):
@@ -364,8 +365,8 @@
             home,
             visitor,
             factors,
-            *z_back,
-            *y_back,
+            z_table,
+            y_back,
             smem=(3,),
         )
 

time: 462 us -> 443 us (0.959)
  Pallas kernels: 190 us -> 143 us
  waiting for transfers between devices: 172 us -> 201 us
    pallas_call x6, Pallas kernels: 190 us -> 143 us  [call(): pl.pallas_call(kernel, out_shape=out_shape, in_specs=specs, out_specs=[si...]
    all_to_all x4, waiting for transfers between devices: 27.7 us -> 39 us  [exchange(): return lax.all_to_all(wire, 'fft', split_axis=0, concat_axis=0, tiled=True)]
    ppermute x1, waiting for transfers between devices: 25.9 us -> 35.1 us  [shards(): far_arrived = lax.ppermute(far_return, 'band', downward)]
    ppermute x1, waiting for transfers between devices: 20.7 us -> 26.6 us  [shards(): lax.ppermute(jnp.where(is_odd, far_second, home_second), 'band', swap)]
  transfers between devices with their start and end apart: 12 -> 12, of which waited for: 8 -> 9; matrix products, arithmetic and copies ran while one was open for 10% -> 11% of each run, Pallas kernels for 41% -> 32%
where the time goes in v3:
time: 443 us
  waiting for transfers between devices  201 us (45%)
  Pallas kernels  143 us (32%)
  other arithmetic  47.1 us (11%)
  starting transfers between devices  27.8 us (6%)
  local copies, waits for them, and re-layouts  20.8 us (5%)
    pallas_call x6, Pallas kernels, call(): pl.pallas_call(kernel, out_shape=out_shape, in_specs=specs, out_specs=[si...  143 us
    ppermute x1, waiting for transfers between devices, shards(): lax.ppermute(near_return, 'band', [(i, (i - 1) % bands) for i in range(ba...  56.5 us
    all_to_all x4, waiting for transfers between devices, exchange(): return lax.all_to_all(wire, 'fft', split_axis=0, concat_axis=0, tiled=True)  39 us
    ppermute x1, waiting for transfers between devices, shards(): far_arrived = lax.ppermute(far_return, 'band', downward)  35.1 us
    ppermute x1, waiting for transfers between devices, shards(): far_first = lax.ppermute(home_first, 'band', upward)  34.9 us
    mul x1, other arithmetic, truncated_kernel(): return profile * (0.25 / float(grid_size) ** 1.5)  31.8 us
    ppermute x1, waiting for transfers between devices, shards(): lax.ppermute(jnp.where(is_odd, far_second, home_second), 'band', swap)  26.6 us
    all_to_all x4, starting transfers between devices, exchange(): return lax.all_to_all(wire, 'fft', split_axis=0, concat_axis=0, tiled=True)  15.8 us
  transfers between devices with their start and end apart: 12, of which 9 were waited for; matrix products, arithmetic and copies ran while one was open for 11% of the time, Pallas kernels for 32%

profile of v3, /device:TPU:0, one launch (start us, length us, event | category | flops | bytes accessed | tf_op | source)
XLA Modules:
  0.0 442.7 jit_solution(9562289928117334476)
XLA Ops:
  0.0 0.0 copy-start
  0.0 3.8 pad_slice_fusion
  3.8 3.0 collective-permute-start
  6.8 34.9 %collective-permute-done = bf16[48,15488]{1,0:T(8,128)(2,1)} collective-permute-done((bf16[48,15488]{1,0:T(8,128)(2,1)}, bf16[48,15488]{1,0:T(8,128)(2,1)}, u32[]{:S(2)}, u32[]{:S(2)}) %collective-permute-start) | collective-permute-done | bytes 1486880 | tf_op jit(solution)/shard_map/ppermute | solution.py:309
  41.7 0.0 collective-permute-start.1
  41.7 0.1 broadcast_add_fusion
  41.8 0.0 copy-done
  41.8 1.8 pad.4.a_ref
  43.6 31.8 %fusion.8.w_ref = f32[44,176,256]{2,1,0:T(8,128)} fusion(f32[256]{0:T(256)S(1)} %fusion.21, f32[44,176]{1,0:T(8,128)S(1)} %broadcast_add_fusion), kind=kLoop, calls=%fused_computation.10 | loop fusion | flops 19824640 | bytes 7961856 | tf_op jit(solution)/shard_map/mul | solution.py:60
  75.3 2.2 collective-permute-done.1
  77.6 2.3 broadcast_select_fusion
  79.9 3.1 collective-permute-start.3
  83.0 0.0 collective-permute-start.4
  83.0 3.7 pad_maximum_fusion.b_ref
  86.7 23.4 %density_to_ky_kz.2 = s16[4,66,48,128]{3,2,1,0:T(8,128)(2,1)} custom-call(bf16[48,30976]{1,0:T(8,128)(2,1)} %pad.4.a_ref, bf16[48,30976]{1,0:T(8,128)(2,1)} %pad_maximum_fusion.b_ref, bf16[768,256]{1,0:T(8,128)(2,1)} %constant.58.clone.z_ref, bf16[192,528]{1,0:T(8,128)(2,1)} %constant.59.clone.y_ref.inverse_ref), custom_call_target="tpu_custom_call" | custom-call | flops 3140222976 | bytes 6543360 | tf_op jit(solution)/shard_map/density_to_ky_kz/pallas_call | solution.py:262
  110.1 3.7 all-to-all-start
  113.8 3.0 collective-permute-done.3
  116.8 2.6 constant_dynamic-update-slice_fusion.1
  119.4 26.6 %collective-permute-done.4 = bf16[48,15488]{1,0:T(8,128)(2,1)} collective-permute-done((bf16[48,15488]{1,0:T(8,128)(2,1)}, bf16[48,15488]{1,0:T(8,128)(2,1)}, u32[]{:S(2)}, u32[]{:S(2)}) %collective-permute-start.4) | collective-permute-done | bytes 1486880 | tf_op jit(solution)/shard_map/ppermute | solution.py:313
  146.0 2.6 constant_dynamic-update-slice_fusion.b_ref
  148.6 23.4 %density_to_ky_kz.3 = s16[4,66,48,128]{3,2,1,0:T(8,128)(2,1)} custom-call(bf16[48,30976]{1,0:T(8,128)(2,1)} %pad.4.a_ref, bf16[48,30976]{1,0:T(8,128)(2,1)} %constant_dynamic-update-slice_fusion.b_ref, bf16[768,256]{1,0:T(8,128)(2,1)} %constant.58.clone.z_ref, bf16[192,528]{1,0:T(8,128)(2,1)} %constant.59.clone.y_ref.inverse_ref), custom_call_target="tpu_custom_call" | custom-call | flops 3140222976 | bytes 6543360 | tf_op jit(solution)/shard_map/density_to_ky_kz/pallas_call | solution.py:262
  172.0 0.0 all-to-all-done.in_ref
  172.0 0.0 copy-start.1
  172.0 4.7 %all-to-all-start.2 = ((s16[4,66,48,128]{3,2,1,0:T(8,128)(2,1)}), s16[4,66,48,128]{3,2,1,0:T(8,128)(2,1)}, u32[]{:S(2)}, u32[]{:S(2)}) async-start(s16[4,66,48,128]{3,2,1,0:T(8,128)(2,1)} %density_to_ky_kz.3), calls=%async_computation.2 | async-start | bytes 6488064 | tf_op jit(solution)/shard_map/all_to_all | solution.py:275
  176.7 0.0 copy-done.1
  176.7 18.5 %filter_along_x.2 = s16[4,66,48,128]{3,2,1,0:T(8,128)(2,1)} custom-call(s16[4,66,48,128]{3,2,1,0:T(8,128)(2,1)} %copy-done.1, f32[44,176,256]{2,1,0:T(8,128)} %fusion.8.w_ref, bf16[176,576]{1,0:T(8,128)(2,1)} %constant.60.clone.forward_ref.y_ref, bf16[192,528]{1,0:T(8,128)(2,1)} %constant.59.clone.y_ref.inverse_ref), custom_call_target="tpu_custom_call" | custom-call | flops 3140222976 | bytes 11579392 | tf_op jit(solution)/shard_map/filter_along_x/pallas_call | solution.py:262
  195.2 19.5 %all-to-all-done.2.in_ref = s16[4,66,48,128]{3,2,1,0:T(8,128)(2,1)} async-done(((s16[4,66,48,128]{3,2,1,0:T(8,128)(2,1)}), s16[4,66,48,128]{3,2,1,0:T(8,128)(2,1)}, u32[]{:S(2)}, u32[]{:S(2)}) %all-to-all-start.2) | async-done | bytes 3244064 | tf_op jit(solution)/shard_map/all_to_all | solution.py:275
  214.7 3.7 all-to-all-start.1
  218.4 18.5 %filter_along_x.3 = s16[4,66,48,128]{3,2,1,0:T(8,128)(2,1)} custom-call(s16[4,66,48,128]{3,2,1,0:T(8,128)(2,1)} %all-to-all-done.2.in_ref, f32[44,176,256]{2,1,0:T(8,128)} %fusion.8.w_ref, bf16[176,576]{1,0:T(8,128)(2,1)} %constant.60.clone.forward_ref.y_ref, bf16[192,528]{1,0:T(8,128)(2,1)} %constant.59.clone.y_ref.inverse_ref), custom_call_target="tpu_custom_call" | custom-call | flops 3140222976 | bytes 11579392 | tf_op jit(solution)/shard_map/filter_along_x/pallas_call | solution.py:262
  236.9 19.5 %all-to-all-done.1.in_ref = s16[4,66,48,128]{3,2,1,0:T(8,128)(2,1)S(1)} async-done(((s16[4,66,48,128]{3,2,1,0:T(8,128)(2,1)}), s16[4,66,48,128]{3,2,1,0:T(8,128)(2,1)S(1)}, u32[]{:S(2)}, u32[]{:S(2)}) %all-to-all-start.1) | async-done | bytes 3244064 | tf_op jit(solution)/shard_map/all_to_all | solution.py:275
  256.4 0.0 copy-start.3
  256.4 1.7 copy-done.3
  258.0 3.7 all-to-all-start.3
  262.4 1.5 collective-permute-start.2
  263.9 4.0 collective-permute-done.2
  268.6 3.1 collective-permute-start.5
  272.4 0.6 pad_maximum_fusion.1.occ
  273.0 0.0 collective-permute-done.5
  273.6 0.6 pad_maximum_fusion.2.occ
  274.2 29.6 %potential_terms.2 = (f32[48,30976]{1,0:T(8,128)}, s16[48,30976]{1,0:T(8,128)(2,1)}) custom-call(s16[4,66,48,128]{3,2,1,0:T(8,128)(2,1)} %copy-done.3, bf16[48,30976]{1,0:T(8,128)(2,1)} %pad.4.a_ref, bf16[48,30976]{1,0:T(8,128)(2,1)} %pad_maximum_fusion.b_ref, f32[2]{0:T(128)} %pad_maximum_fusion.1.occ, bf16[768,256]{1,0:T(8,128)(2,1)} %constant.58.clone.z_ref, ...), custom_call_target="tpu_custom_call" | custom-call | flops 3140222976 | bytes 9787400 | tf_op jit(solution)/shard_map/potential_terms/pallas_call | solution.py:262
  303.8 0.7 collective-permute-start.6
  304.5 0.0 all-to-all-done.3.in_ref
  304.5 0.0 copy-start.2
  304.5 1.7 copy-done.2
  306.2 29.7 %potential_terms.3 = (f32[48,30976]{1,0:T(8,128)}, s16[48,30976]{1,0:T(8,128)(2,1)}) custom-call(s16[4,66,48,128]{3,2,1,0:T(8,128)(2,1)} %copy-done.2, bf16[48,30976]{1,0:T(8,128)(2,1)} %pad.4.a_ref, bf16[48,30976]{1,0:T(8,128)(2,1)} %constant_dynamic-update-slice_fusion.b_ref, f32[2]{0:T(128)} %pad_maximum_fusion.2.occ, ...), custom_call_target="tpu_custom_call" | custom-call | flops 3140222976 | bytes 9787400 | tf_op jit(solution)/shard_map/potential_terms/pallas_call | solution.py:262
  335.8 0.5 collective-permute-start.7
  336.4 35.1 %collective-permute-done.6 = s16[48,30976]{1,0:T(8,128)(2,1)} collective-permute-done((s16[48,30976]{1,0:T(8,128)(2,1)}, s16[48,30976]{1,0:T(8,128)(2,1)}, u32[]{:S(2)}, u32[]{:S(2)}) %collective-permute-start.6) | collective-permute-done | bytes 2973728 | tf_op jit(solution)/shard_map/ppermute | solution.py:382
  371.4 0.0 slice-start
  371.4 2.8 convert_element_type.48
  374.2 0.5 fusion.17
  374.7 0.0 slice-start.1
  374.7 56.5 %collective-permute-done.7 = s16[48,30976]{1,0:T(8,128)(2,1)S(1)} collective-permute-done((s16[48,30976]{1,0:T(8,128)(2,1)}, s16[48,30976]{1,0:T(8,128)(2,1)S(1)}, u32[]{:S(2)}, u32[]{:S(2)}) %collective-permute-start.7) | collective-permute-done | bytes 2973728 | tf_op jit(solution)/shard_map/ppermute | solution.py:384
  431.1 0.8 convert_element_type.49
  431.9 0.5 fusion.14
  432.4 0.0 slice-done
  432.4 0.0 slice-done.1
  432.4 3.6 fusion.10
  436.1 6.7 %copy.8 = f32[1,44,30976]{2,0,1:T(1,128)} copy(f32[1,44,30976]{2,1,0:T(8,128)S(1)} %fusion.10) | data formatting | bytes 10903552 | tf_op jit(solution)/shard_map/broadcast_in_dim | solution.py:391
  (4 shorter events, 0.0 us)
Async XLA Ops:
  0.0 41.8 %copy-start = (bf16[1,44,30976]{2,1,0:T(8,128)(2,1)S(1)}, bf16[1,44,30976]{2,1,0:T(8,128)(2,1)}, u32[]{:S(2)}) copy-start(bf16[1,44,30976]{2,1,0:T(8,128)(2,1)} %param.7) | copy-start | bytes 8177668
  3.8 37.9 %collective-permute-start = (bf16[48,15488]{1,0:T(8,128)(2,1)}, bf16[48,15488]{1,0:T(8,128)(2,1)}, u32[]{:S(2)}, u32[]{:S(2)}) collective-permute-start(bf16[48,15488]{1,0:T(8,128)(2,1)} %get-tuple-element.23), channel_id=1, source_target_pairs={{0,8},{4,12},{8,16},{12,20},{16,24},{20,28},{24,0},{28,4},{1,9},{5... | collective-permute-start | bytes 4460552 | tf_op jit(solution)/shard_map/ppermute | solution.py:309
  41.7 35.9 %collective-permute-start.1 = (bf16[48,15488]{1,0:T(8,128)(2,1)}, bf16[48,15488]{1,0:T(8,128)(2,1)}, u32[]{:S(2)}, u32[]{:S(2)}) collective-permute-start(bf16[48,15488]{1,0:T(8,128)(2,1)} %get-tuple-element.14), channel_id=1, source_target_pairs={{0,8},{4,12},{8,16},{12,20},{16,24},{20,28},{24,0},{28,4},{1,9},{5... | collective-permute-start | bytes 4460552 | tf_op jit(solution)/shard_map/ppermute | solution.py:311
  79.9 36.9 %collective-permute-start.3 = (bf16[48,15488]{1,0:T(8,128)(2,1)}, bf16[48,15488]{1,0:T(8,128)(2,1)}, u32[]{:S(2)}, u32[]{:S(2)}) collective-permute-start(bf16[48,15488]{1,0:T(8,128)(2,1)} %get-tuple-element.22), channel_id=1, source_target_pairs={{0,4},{4,0},{8,12},{12,8},{16,20},{20,16},{24,28},{28,24},{1,5},{5... | collective-permute-start | bytes 4460552 | tf_op jit(solution)/shard_map/ppermute | solution.py:312
  83.0 63.0 %collective-permute-start.4 = (bf16[48,15488]{1,0:T(8,128)(2,1)}, bf16[48,15488]{1,0:T(8,128)(2,1)}, u32[]{:S(2)}, u32[]{:S(2)}) collective-permute-start(bf16[48,15488]{1,0:T(8,128)(2,1)} %get-tuple-element.21), channel_id=1, source_target_pairs={{0,4},{4,0},{8,12},{12,8},{16,20},{20,16},{24,28},{28,24},{1,5},{5... | collective-permute-start | bytes 4460552 | tf_op jit(solution)/shard_map/ppermute | solution.py:313
  110.1 61.9 %all-to-all-start = ((s16[4,66,48,128]{3,2,1,0:T(8,128)(2,1)}), s16[4,66,48,128]{3,2,1,0:T(8,128)(2,1)S(1)}, u32[]{:S(2)}, u32[]{:S(2)}) async-start(s16[4,66,48,128]{3,2,1,0:T(8,128)(2,1)} %density_to_ky_kz.2), calls=%async_computation | async-start | bytes 6488064 | tf_op jit(solution)/shard_map/all_to_all | solution.py:275
  172.0 4.7 %copy-start.1 = (s16[4,66,48,128]{3,2,1,0:T(8,128)(2,1)}, s16[4,66,48,128]{3,2,1,0:T(8,128)(2,1)S(1)}, u32[]{:S(2)}) copy-start(s16[4,66,48,128]{3,2,1,0:T(8,128)(2,1)S(1)} %all-to-all-done.in_ref) | copy-start | bytes 9732100
  172.0 42.7 %all-to-all-start.2 = ((s16[4,66,48,128]{3,2,1,0:T(8,128)(2,1)}), s16[4,66,48,128]{3,2,1,0:T(8,128)(2,1)}, u32[]{:S(2)}, u32[]{:S(2)}) async-start(s16[4,66,48,128]{3,2,1,0:T(8,128)(2,1)} %density_to_ky_kz.3), calls=%async_computation.2 | async-start | bytes 6488064 | tf_op jit(solution)/shard_map/all_to_all | solution.py:275
  214.7 41.7 %all-to-all-start.1 = ((s16[4,66,48,128]{3,2,1,0:T(8,128)(2,1)}), s16[4,66,48,128]{3,2,1,0:T(8,128)(2,1)S(1)}, u32[]{:S(2)}, u32[]{:S(2)}) async-start(s16[4,66,48,128]{3,2,1,0:T(8,128)(2,1)} %filter_along_x.2), calls=%async_computation.1 | async-start | bytes 6488064 | tf_op jit(solution)/shard_map/all_to_all | solution.py:275
  256.4 1.7 copy-start.3
  258.0 46.4 %all-to-all-start.3 = ((s16[4,66,48,128]{3,2,1,0:T(8,128)(2,1)}), s16[4,66,48,128]{3,2,1,0:T(8,128)(2,1)S(1)}, u32[]{:S(2)}, u32[]{:S(2)}) async-start(s16[4,66,48,128]{3,2,1,0:T(8,128)(2,1)} %filter_along_x.3), calls=%async_computation.3 | async-start | bytes 6488064 | tf_op jit(solution)/shard_map/all_to_all | solution.py:275
  262.4 5.5 %collective-permute-start.2 = (bf16[1]{0:T(256)(128)(2,1)}, bf16[1]{0:T(256)(128)(2,1)}, u32[]{:S(2)}, u32[]{:S(2)}) collective-permute-start(bf16[1]{0:T(256)(128)(2,1)} %convert_element_type.44), channel_id=1, source_target_pairs={{0,8},{4,12},{8,16},{12,20},{16,24},{20,28},{24,0},{28,4},{1,9},{5... | collective-permute-start | bytes 14 | tf_op jit(solution)/shard_map/ppermute | solution.py:307
  268.6 4.4 collective-permute-start.5
  303.8 67.7 %collective-permute-start.6 = (s16[48,30976]{1,0:T(8,128)(2,1)}, s16[48,30976]{1,0:T(8,128)(2,1)}, u32[]{:S(2)}, u32[]{:S(2)}) collective-permute-start(s16[48,30976]{1,0:T(8,128)(2,1)} %get-tuple-element.19), channel_id=1, source_target_pairs={{0,24},{4,28},{8,0},{12,4},{16,8},{20,12},{24,16},{28,20},{1,25},{... | collective-permute-start | bytes 8921096 | tf_op jit(solution)/shard_map/ppermute | solution.py:382
  304.5 1.7 copy-start.2
  335.8 95.3 %collective-permute-start.7 = (s16[48,30976]{1,0:T(8,128)(2,1)}, s16[48,30976]{1,0:T(8,128)(2,1)S(1)}, u32[]{:S(2)}, u32[]{:S(2)}) collective-permute-start(s16[48,30976]{1,0:T(8,128)(2,1)} %get-tuple-element.20), channel_id=1, source_target_pairs={{0,28},{4,0},{8,4},{12,8},{16,12},{20,16},{24,20},{28,24},{1,29},{... | collective-permute-start | bytes 8921096 | tf_op jit(solution)/shard_map/ppermute | solution.py:384
  371.4 61.0 %slice-start = ((s8[5947392]{0:T(1024)(128)(4,1)}), s8[4194304]{0:T(1024)(128)(4,1)S(1)}, s32[]{:S(2)}) async-start(s8[5947392]{0:T(1024)(128)(4,1)} %bitcast.7), calls=%async_computation.4 | async-start | bytes 8388608
  374.7 57.7 %slice-start.1 = ((s8[5947392]{0:T(1024)(128)(4,1)}), s8[1753088]{0:T(1024)(128)(4,1)S(1)}, s32[]{:S(2)}) async-start(s8[5947392]{0:T(1024)(128)(4,1)} %bitcast.7), calls=%async_computation.5 | async-start | bytes 3506176

commit v4 on v3

v4 whole, which is shorter than its diff:
```python
import functools

import jax
import jax.numpy as jnp
import numpy as np
from jax import lax
from jax.experimental import pallas as pl
from jax.experimental.pallas import tpu as pltpu
from jax.sharding import PartitionSpec as P

LANES = 256
CHUNK = 15
ROWS = 16
LEVELS = 32000.0
STEPS_PER_OCTAVE = 64.0
F32 = jnp.float32
BF16 = jnp.bfloat16
VMEM_BYTES = 60 * 1024 * 1024


def round_up(value, multiple):
    return -(-value // multiple) * multiple


def cas_table(grid_size):
    indices = np.arange(grid_size)
    phases = (indices[:, None] * indices[None, :] % grid_size) * (2.0 * np.pi / grid_size)
    return np.cos(phases) + np.sin(phases)


def high_low(table, axis):
    table = table.astype(np.float32)
    high = table.astype(BF16)
    low = (table - high.astype(np.float32)).astype(BF16)
    return jnp.asarray(np.concatenate([high, high, low], axis=axis))


def spread_rows(table, blocks, slab, block_rows):
    spread = np.zeros((blocks * block_rows, table.shape[1]))
    for block in range(blocks):
        spread[block * block_rows : block * block_rows + slab] = table[block * slab : (block + 1) * slab]
    return spread


def spread_planes(table, blocks, slab):
    planes = round_up(slab, CHUNK) // CHUNK * ROWS
    spread = np.zeros((blocks * planes, table.shape[1]))
    for plane in range(blocks * slab):
        block, own = divmod(plane, slab)
        spread[block * planes + own // CHUNK * ROWS + own % CHUNK] = table[plane]
    return spread


def folded_squares(indices, grid_size):
    folded = jnp.minimum(indices, grid_size - indices).astype(F32)
    return folded * folded


def sine_of_half_turns(turns):
    angle = turns * jnp.pi
    square = angle * angle
    series = jnp.full_like(square, 1.0 / 6227020800.0)
    for factor in (-1.0 / 39916800.0, 1.0 / 362880.0, -1.0 / 5040.0, 1.0 / 120.0, -1.0 / 6.0, 1.0):
        series = series * square + factor
    return angle * series


def truncated_kernel(grid_size, slab, rows):
    lanes = folded_squares(jnp.minimum(jnp.arange(LANES, dtype=jnp.int32), grid_size), grid_size)
    folded = jnp.arange(round_up(grid_size // 2 + 1, 8), dtype=jnp.int32).astype(F32)
    squares = folded * folded
    own_rows = lax.axis_index("fft") * slab + jnp.arange(rows, dtype=jnp.int32)
    row_squares = folded_squares(own_rows, grid_size)
    summed = row_squares[:, None, None] + squares[None, :, None] + lanes[None, None, :]
    safe_sum = jnp.maximum(summed, 1.0)
    half_radius = 0.5 * jnp.sqrt(safe_sum)
    sine = sine_of_half_turns(half_radius - jnp.round(half_radius))
    profile = jnp.where(summed > 0.5, 4.0 * sine * sine / (jnp.pi * jnp.pi * safe_sum), 1.0)
    return profile * (0.25 / float(grid_size) ** 1.5)


def parts_of(value):
    high = value.astype(BF16)
    return high, (value - high.astype(F32)).astype(BF16)


def dot(left, right):
    return jnp.dot(left, right, preferred_element_type=F32)


def times_table(value, table):
    high, low = parts_of(value)
    return dot(jnp.concatenate([high, low, high], axis=1), table)


def table_times(table, value):
    high, low = parts_of(value)
    return dot(table, jnp.concatenate([high, low, high], axis=0))


def exponent_of(largest):
    return jnp.ceil(jnp.log2(jnp.maximum(largest, 1e-30)) * STEPS_PER_OCTAVE)


def step_of(exponent):
    return jnp.exp2(exponent * (1.0 / STEPS_PER_OCTAVE))


def coded(value):
    exponent = exponent_of(jnp.max(jnp.abs(value), axis=-2, keepdims=True))
    scaled = jnp.round(value * (LEVELS / step_of(exponent)))
    row = lax.broadcasted_iota(jnp.int32, value.shape, value.ndim - 2)
    return jnp.where(row == CHUNK, exponent, scaled)


def decoded(code):
    return code * (step_of(code[..., CHUNK:, :]) * (1.0 / LEVELS))


def to_wire(code):
    return code.astype(jnp.int32).astype(jnp.int16)


def from_wire(wire):
    return wire.astype(jnp.int32).astype(F32)


def shared_lanes(first, second):
    lane = lax.broadcasted_iota(jnp.int32, first.shape, first.ndim - 1)
    return jnp.where(lane < 64, first, pltpu.roll(second, 64, second.ndim - 1))


def unshared(both):
    lane = lax.broadcasted_iota(jnp.int32, both.shape, both.ndim - 1)
    first = jnp.where(lane < 64, both, 0.0)
    second = jnp.where(lane < 64, pltpu.roll(both, 64, both.ndim - 1), 0.0)
    return first, second


def group_slices(group_lanes, grid_size):
    for row in range(group_lanes // grid_size):
        first, offset = divmod(row * grid_size, 128)
        yield row, first, offset, -(-(offset + grid_size) // 128)


def forward_kernel(blocks, block_rows, a_ref, b_ref, z_ref, y_ref, out_ref, rows_z, rows_y, buf):
    cells = a_ref.shape[1]
    grid_size = rows_z.shape[0]
    half = out_ref.shape[1] // 3
    group_lanes = 8 * grid_size
    z_table, y_table = z_ref[...], y_ref[...]

    @pl.loop(0, cells // group_lanes, unroll=2)
    def _(group):
        lanes = pl.ds(pl.multiple_of(group * group_lanes, 128), group_lanes)
        flat = a_ref[:, lanes].astype(F32) * b_ref[:, lanes].astype(F32)
        for row, first, offset, tiles in group_slices(group_lanes, grid_size):
            window = flat[:, first * 128 : (first + tiles) * 128]
            if offset:
                window = pltpu.roll(window, tiles * 128 - offset, 1)
            rows_z[group * 8 + row] = window[:, :LANES]

    @pl.loop(0, 2)
    def _(part):
        count = grid_size // 2
        at = pl.ds(pl.multiple_of(part * count, 8), count)
        along_z = times_table(rows_z[at].reshape(count * ROWS, LANES), z_table)
        rows_y[:, at, :] = jnp.transpose(along_z.reshape(count, ROWS, LANES), (1, 0, 2))

    @pl.loop(0, 2)
    def _(part):
        along_y = jnp.stack([table_times(y_table, rows_y[part * 8 + i]) for i in range(8)])
        at = pl.ds(pl.multiple_of(part * 8, 8), 8)
        buf[:, at, :] = jnp.transpose(along_y, (1, 0, 2))

    @pl.loop(0, half)
    def _(row):
        for block in range(blocks):
            first = coded(buf[block * block_rows + row])
            second = coded(buf[block * block_rows + half + row])
            out_ref[block, row] = to_wire(first[:, :128])
            out_ref[block, half + row] = to_wire(second[:, :128])
            out_ref[block, 2 * half + row] = to_wire(shared_lanes(first[:, 128:], second[:, 128:]))


def filter_kernel(chunks, *refs):
    in_refs, (w_ref, forward_ref, inverse_ref, out_ref) = refs[:chunks], refs[chunks:]
    blocks, half = out_ref.shape[0], out_ref.shape[1] // 3
    middle = forward_ref.shape[0] // 2
    forward, inverse = forward_ref[...], inverse_ref[...]

    @pl.loop(0, half, unroll=2)
    def _(row):
        upper = [unshared(from_wire(ref[:, 2 * half + row])) for ref in in_refs]
        codes = []
        for i in range(2):
            at = row + i * half
            fields = [
                decoded(jnp.concatenate([from_wire(ref[:, at]), upper[chunk][i]], axis=-1))
                for chunk, ref in enumerate(in_refs)
            ]
            field = jnp.concatenate(fields, axis=1).reshape(blocks * chunks * ROWS, LANES)
            lower_w = w_ref[at, :middle]
            rows = lax.broadcasted_iota(jnp.int32, lower_w.shape, 0)
            upper_w = jnp.where(rows == 0, w_ref[at, middle : middle + 1], lower_w)
            spectrum = table_times(forward, field) * jnp.concatenate([lower_w, upper_w], axis=0)
            filtered = table_times(inverse, spectrum).reshape(blocks, chunks, ROWS, LANES)
            code = coded(filtered).reshape(blocks, chunks * ROWS, LANES)
            out_ref[:, at] = to_wire(code[..., :128])
            codes.append(code[..., 128:])
        out_ref[:, 2 * half + row] = to_wire(shared_lanes(codes[0], codes[1]))


def back_kernel(blocks, block_rows, in_ref, a_ref, b_ref, occ, z_ref, y_ref, own_ref, ret_ref, buf, rows_z, field):
    cells = a_ref.shape[1]
    grid_size = rows_z.shape[0]
    half = in_ref.shape[1] // 3
    group_lanes = 8 * grid_size
    z_table, y_table = z_ref[...], y_ref[...]
    home, visitor = -0.5 * occ[0], -0.5 * occ[1]

    for block in range(blocks):
        base = block * block_rows
        buf[base + 2 * half : base + block_rows] = jnp.zeros((block_rows - 2 * half, ROWS, LANES), F32)

    @pl.loop(0, half)
    def _(row):
        for block in range(blocks):
            base = block * block_rows
            upper = unshared(from_wire(in_ref[block, 2 * half + row]))
            for i in range(2):
                at = row + i * half
                code = jnp.concatenate([from_wire(in_ref[block, at]), upper[i]], axis=-1)
                buf[base + at] = decoded(code)

    @pl.loop(0, 2)
    def _(part):
        rows = pl.ds(pl.multiple_of(part * 8, 8), 8)
        mixed = jnp.transpose(buf[:, rows, :], (1, 0, 2))
        along_y = jnp.stack([table_times(y_table, mixed[i]) for i in range(8)])
        along_z = times_table(along_y.reshape(8 * grid_size, LANES), z_table)
        rows_z[...] = jnp.transpose(along_z.reshape(8, grid_size, LANES), (1, 0, 2))

        @pl.loop(0, cells // group_lanes, unroll=2)
        def _(group):
            tiles_of = [None] * (group_lanes // 128)
            for row, first, offset, tiles in group_slices(group_lanes, grid_size):
                window = rows_z[group * 8 + row]
                if tiles * 128 > LANES:
                    window = jnp.concatenate([window, jnp.zeros((8, tiles * 128 - LANES), F32)], axis=1)
                if offset:
                    window = pltpu.roll(window, offset, 1)
                for tile in range(tiles):
                    piece = window[:, tile * 128 : (tile + 1) * 128]
                    before = tiles_of[first + tile]
                    tiles_of[first + tile] = piece if before is None else before + piece
            lanes = pl.ds(pl.multiple_of(group * group_lanes, 128), group_lanes)
            field[rows, lanes] = jnp.concatenate(tiles_of, axis=1)

    @pl.loop(0, cells // group_lanes)
    def _(group):
        lanes = pl.ds(pl.multiple_of(group * group_lanes, 128), group_lanes)
        potential = field[:, lanes]
        own_ref[:, lanes] = potential * b_ref[:, lanes].astype(F32) * visitor
        terms = potential * a_ref[:, lanes].astype(F32) * home
        ret_ref[:, lanes] = to_wire(coded(terms))


def total_kernel(chunks, *refs):
    out_ref = refs[-1]
    slab = out_ref.shape[1]
    for chunk in range(chunks):
        first, second, third, fourth = refs[4 * chunk : 4 * chunk + 4]
        total = first[...] + second[...]
        total = total + decoded(from_wire(third[...])) + decoded(from_wire(fourth[...]))
        start = chunk * CHUNK
        stop = min(start + CHUNK, slab)
        out_ref[0, start:stop] = total[: stop - start]


def call(kernel, out_shape, scratch, name, flops, operands, in_specs=None):
    single = pl.BlockSpec(memory_space=pltpu.VMEM)
    bytes_moved = sum(o.size * o.dtype.itemsize for o in operands)
    return pl.pallas_call(
        kernel,
        grid=(1,) if in_specs else (),
        out_shape=out_shape,
        in_specs=in_specs or [single] * len(operands),
        out_specs=[single] * len(out_shape) if isinstance(out_shape, list) else single,
        scratch_shapes=scratch,
        compiler_params=pltpu.CompilerParams(vmem_limit_bytes=VMEM_BYTES),
        cost_estimate=pl.CostEstimate(flops=flops, bytes_accessed=bytes_moved, transcendentals=0),
        name=name,
    )(*operands)


def exchange(wire):
    return lax.all_to_all(wire, "fft", split_axis=0, concat_axis=0, tiled=True)


def shards(wavefunctions, band_occ):
    _, slab, cells = wavefunctions.shape
    blocks = lax.axis_size("fft")
    bands = lax.axis_size("band")
    grid_size = slab * blocks
    chunks = round_up(slab, CHUNK) // CHUNK
    planes = chunks * ROWS
    block_rows = round_up(slab, 8)
    half = (slab + 1) // 2
    ky_rows = blocks * block_rows

    table = cas_table(grid_size)
    square_table = np.zeros((LANES, LANES))
    square_table[:grid_size, :grid_size] = table
    to_ky = spread_rows(table, blocks, slab, block_rows)
    middle = grid_size // 2
    kx_order = np.concatenate([np.arange(middle), [middle], grid_size - np.arange(1, middle)])
    to_x = spread_planes(table[:, kx_order], blocks, slab)
    z_table = high_low(square_table, 0)
    y_forward, y_back = high_low(to_ky, 1), high_low(to_ky.T, 1)
    x_forward, x_back = high_low(to_x.T, 1), high_low(to_x, 1)
    profile = truncated_kernel(grid_size, slab, 2 * half)

    occupied = band_occ.astype(BF16)
    upward = [(i, (i + 2) % bands) for i in range(bands)]
    downward = [(i, (i - 2) % bands) for i in range(bands)]
    downward_one = [(i, (i - 1) % bands) for i in range(bands)]
    swap = [(i, i ^ 1) for i in range(bands)]
    is_odd = lax.axis_index("band") % 2 == 1

    def chunk_of(chunk):
        piece = wavefunctions[0, chunk * CHUNK : (chunk + 1) * CHUNK]
        return jnp.pad(piece, ((0, ROWS - piece.shape[0]), (0, 0)))

    home = [chunk_of(chunk) for chunk in range(chunks)]
    far_occ = lax.ppermute(occupied, "band", upward)
    near_occ = lax.ppermute(jnp.where(is_odd, far_occ, occupied), "band", swap)
    far, near = [], []
    for chunk in range(chunks):
        sent = home[chunk]
        if far:
            sent, far[-1] = lax.optimization_barrier((sent, far[-1]))
        far.append(lax.ppermute(sent, "band", upward))
    far[0], profile = lax.optimization_barrier((far[0], profile))
    for chunk in range(chunks):
        near.append(lax.ppermute(jnp.where(is_odd, far[chunk], home[chunk]), "band", swap))
    flops = 12 * ROWS * grid_size**3

    def forward(chunk, visitor):
        return call(
            functools.partial(forward_kernel, blocks, block_rows),
            jax.ShapeDtypeStruct((blocks, 3 * half, ROWS, 128), jnp.int16),
            [
                pltpu.VMEM((grid_size, ROWS, LANES), F32),
                pltpu.VMEM((ROWS, grid_size, LANES), F32),
                pltpu.VMEM((ky_rows, ROWS, LANES), F32),
            ],
            "density_to_ky_kz",
            flops,
            [home[chunk], visitor[chunk], z_table, y_forward],
        )

    def filtered(wires):
        return call(
            functools.partial(filter_kernel, chunks),
            jax.ShapeDtypeStruct((blocks, 3 * half, planes, 128), jnp.int16),
            [],
            "filter_along_x",
            chunks * flops,
            [*wires, profile, x_forward, x_back],
        )

    def back(wire, chunk, visitor, factors):
        whole = pl.BlockSpec(memory_space=pltpu.VMEM)
        piece = pl.BlockSpec((blocks, 3 * half, ROWS, 128), lambda i: (0, 0, chunk, 0))
        return call(
            functools.partial(back_kernel, blocks, block_rows),
            [
                jax.ShapeDtypeStruct((ROWS, cells), F32),
                jax.ShapeDtypeStruct((ROWS, cells), jnp.int16),
            ],
            [
                pltpu.VMEM((ky_rows, ROWS, LANES), F32),
                pltpu.VMEM((grid_size, 8, LANES), F32),
                pltpu.VMEM((ROWS, cells), F32),
            ],
            "potential_terms",
            flops,
            [wire, home[chunk], visitor[chunk], factors, z_table, y_back],
            [piece, whole, whole, pl.BlockSpec(memory_space=pltpu.SMEM), whole, whole],
        )

    home_occ = occupied.astype(F32)[0]
    near_factors = jnp.stack([home_occ, near_occ.astype(F32)[0]])
    far_factors = jnp.stack([home_occ, far_occ.astype(F32)[0]])

    far_wires = [exchange(forward(chunk, far)) for chunk in range(chunks)]
    near_wires = [exchange(forward(chunk, near)) for chunk in range(chunks)]
    far_wire = exchange(filtered(far_wires))
    near_wire = exchange(filtered(near_wires))
    far_parts = [back(far_wire, chunk, far, far_factors) for chunk in range(chunks)]
    near_parts = [back(near_wire, chunk, near, near_factors) for chunk in range(chunks)]
    operands = []
    for (far_own, far_return), (near_own, near_return) in zip(far_parts, near_parts):
        far_arrived = lax.ppermute(far_return, "band", downward)
        near_arrived = lax.ppermute(near_return, "band", downward_one)
        operands += [far_own, near_own, far_arrived, near_arrived]
    width = 16 * grid_size
    spec = pl.BlockSpec((ROWS, width), lambda i: (0, i))
    return pl.pallas_call(
        functools.partial(total_kernel, chunks),
        grid=(cells // width,),
        out_shape=jax.ShapeDtypeStruct((1, slab, cells), F32),
        in_specs=[spec] * len(operands),
        out_specs=pl.BlockSpec((1, slab, width), lambda i: (0, 0, i)),
        compiler_params=pltpu.CompilerParams(vmem_limit_bytes=VMEM_BYTES),
        name="total_terms",
    )(*operands)


def solution(mesh):
    in_specs = (P("band", "fft", None), P("band"))
    out_specs = P("band", "fft", None)
    return jax.shard_map(shards, mesh=mesh, in_specs=in_specs, out_specs=out_specs, check_vma=False)
```

time: 443 us -> 388 us (0.88)
  waiting for transfers between devices: 201 us -> 111 us
  Pallas kernels: 143 us -> 188 us
  other arithmetic: 47.1 us -> 11.4 us
  starting transfers between devices: 27.8 us -> 54.6 us
    pallas_call x6 -> x15, Pallas kernels: 143 us -> 188 us  [the longest x14 175 us: call(): pl.pallas_call(kernel, grid=(1,) if in_specs else (), out_shape=out_shape...]
    ppermute x5 -> x9, waiting for transfers between devices: 123 us -> 81.5 us  [the longest x3 48 us: shards(): near_arrived = lax.ppermute(near_return, 'band', downward_one)]
    ppermute x1 -> x3, waiting for transfers between devices: 35.1 us -> 0.01 us  [shards(): far_arrived = lax.ppermute(far_return, 'band', downward)]
    mul x1, other arithmetic: 31.8 us -> 6.22 us  [truncated_kernel(): return profile * (0.25 / float(grid_size) ** 1.5)]
    all_to_all x4 -> x8, starting transfers between devices: 15.8 us -> 31.8 us  [exchange(): return lax.all_to_all(wire, 'fft', split_axis=0, concat_axis=0, tiled=True)]
    all_to_all x4 -> x8, waiting for transfers between devices: 39 us -> 24.8 us  [exchange(): return lax.all_to_all(wire, 'fft', split_axis=0, concat_axis=0, tiled=True)]
    ppermute x5 -> x9, starting transfers between devices: 6.69 us -> 17.3 us  [the longest x3 7.67 us: shards(): lax.ppermute(jnp.where(is_odd, far[chunk], home[chunk]), 'band', swap)]
    pallas_call x0 -> x1, local copies, waits for them, and re-layouts: none -> 7.62 us  [shards(): pl.pallas_call(functools.partial(total_kernel, chunks), grid=(cells // wi...]
  transfers between devices with their start and end apart: 12 -> 22, of which waited for: 9 -> 12; matrix products, arithmetic and copies ran while one was open for 11% -> 3% of each run, Pallas kernels for 32% -> 45%
where the time goes in v4:
time: 388 us; the launch traced here: 386 us
  Pallas kernels  188 us (48%)
  waiting for transfers between devices  111 us (29%)
  starting transfers between devices  54.6 us (14%)
  local copies, waits for them, and re-layouts  17.8 us (5%)
  other arithmetic  11.4 us (3%)
    pallas_call x14, Pallas kernels, call(): pl.pallas_call(kernel, grid=(1,) if in_specs else (), out_shape=out_shape...  175 us
    ppermute x3, waiting for transfers between devices, shards(): near_arrived = lax.ppermute(near_return, 'band', downward_one)  48 us
    all_to_all x8, starting transfers between devices, exchange(): return lax.all_to_all(wire, 'fft', split_axis=0, concat_axis=0, tiled=True)  31.8 us
    ppermute x3, waiting for transfers between devices, shards(): far.append(lax.ppermute(sent, 'band', upward))  25.6 us
    all_to_all x8, waiting for transfers between devices, exchange(): return lax.all_to_all(wire, 'fft', split_axis=0, concat_axis=0, tiled=True)  24.8 us
    pallas_call x1, Pallas kernels, shards(): pl.pallas_call(functools.partial(total_kernel, chunks), grid=(cells // wi...  12.9 us
    ppermute x3, waiting for transfers between devices, shards(): lax.ppermute(jnp.where(is_odd, far[chunk], home[chunk]), 'band', swap)  7.92 us
  transfers between devices with their start and end apart: 22, of which 12 were waited for; matrix products, arithmetic and copies ran while one was open for 3% of the time, Pallas kernels for 45%

profile of v4, /device:TPU:0, one launch (start us, length us, event | category | flops | bytes accessed | tf_op | source)
XLA Modules:
  0.0 385.6 jit_solution(6118008820054380952)
XLA Ops:
  0.0 1.9 slice_bitcast_fusion.1
  1.9 0.1 pad.11.a_ref
  2.0 3.1 collective-permute-start
  5.2 0.1 pad.12.a_ref
  5.3 0.1 broadcast_add_fusion
  5.3 6.2 %fusion.5.refs_3_ = f32[44,96,256]{2,1,0:T(8,128)} fusion(f32[256]{0:T(256)S(1)} %fusion.22, f32[44,96]{1,0:T(8,128)S(1)} %broadcast_add_fusion), kind=kLoop, calls=%fused_computation.9 | loop fusion | flops 29196288 | bytes 4343296 | tf_op jit(solution)/shard_map/mul | solution.py:79
  11.6 17.6 %collective-permute-done.b_ref = bf16[16,30976]{1,0:T(8,128)(2,1)} collective-permute-done((bf16[16,30976]{1,0:T(8,128)(2,1)S(1)}, bf16[16,30976]{1,0:T(8,128)(2,1)}, u32[]{:S(2)}, u32[]{:S(2)}) %collective-permute-start) | collective-permute-done | bytes 991264 | tf_op jit(solution)/shard_map/ppermute | solution.py:343
  29.2 1.3 broadcast_select_fusion.2
  30.5 2.7 collective-permute-start.4
  33.2 10.3 %density_to_ky_kz.6 = s16[4,66,16,128]{3,2,1,0:T(8,128)(2,1)} custom-call(bf16[16,30976]{1,0:T(8,128)(2,1)} %copy-done.2, bf16[16,30976]{1,0:T(8,128)(2,1)} %collective-permute-done.b_ref, bf16[768,256]{1,0:T(8,128)(2,1)} %constant.66.clone.z_ref, bf16[192,528]{1,0:T(8,128)(2,1)} %constant.67.clone.y_ref), custom_call_target="tpu_custom_call" | custom-call | flops 1046740992 | bytes 2578432 | tf_op jit(solution)/shard_map/density_to_ky_kz/pallas_call | solution.py:284
  43.5 4.3 %all-to-all-start = ((s16[4,66,16,128]{3,2,1,0:T(8,128)(2,1)}), s16[4,66,16,128]{3,2,1,0:T(8,128)(2,1)}, u32[]{:S(2)}, u32[]{:S(2)}) async-start(s16[4,66,16,128]{3,2,1,0:T(8,128)(2,1)} %density_to_ky_kz.6), calls=%async_computation | async-start | bytes 2162688 | tf_op jit(solution)/shard_map/all_to_all | solution.py:298
  47.8 1.6 slice_bitcast_fusion
  49.4 0.1 pad.13.a_ref
  49.5 4.7 %collective-permute-done.1.b_ref = bf16[16,30976]{1,0:T(8,128)(2,1)} collective-permute-done((bf16[16,30976]{1,0:T(8,128)(2,1)S(1)}, bf16[16,30976]{1,0:T(8,128)(2,1)}, u32[]{:S(2)}, u32[]{:S(2)}) %collective-permute-start.1) | collective-permute-done | bytes 991264 | tf_op jit(solution)/shard_map/ppermute | solution.py:343
  54.2 10.3 %density_to_ky_kz.7 = s16[4,66,16,128]{3,2,1,0:T(8,128)(2,1)} custom-call(bf16[16,30976]{1,0:T(8,128)(2,1)} %copy-done.3, bf16[16,30976]{1,0:T(8,128)(2,1)} %collective-permute-done.1.b_ref, bf16[768,256]{1,0:T(8,128)(2,1)} %constant.66.clone.z_ref, bf16[192,528]{1,0:T(8,128)(2,1)} %constant.67.clone.y_ref), custom_call_target="tpu_custom_call" | custom-call | flops 1046740992 | bytes 2578432 | tf_op jit(solution)/shard_map/density_to_ky_kz/pallas_call | solution.py:284
  64.5 4.4 %all-to-all-start.1 = ((s16[4,66,16,128]{3,2,1,0:T(8,128)(2,1)}), s16[4,66,16,128]{3,2,1,0:T(8,128)(2,1)}, u32[]{:S(2)}, u32[]{:S(2)}) async-start(s16[4,66,16,128]{3,2,1,0:T(8,128)(2,1)} %density_to_ky_kz.7), calls=%async_computation.1 | async-start | bytes 2162688 | tf_op jit(solution)/shard_map/all_to_all | solution.py:298
  68.9 0.1 collective-permute-start.2
  69.0 10.3 %density_to_ky_kz.9 = s16[4,66,16,128]{3,2,1,0:T(8,128)(2,1)} custom-call(bf16[16,30976]{1,0:T(8,128)(2,1)} %copy-done.2, bf16[16,30976]{1,0:T(8,128)(2,1)} %collective-permute-done.4.b_ref, bf16[768,256]{1,0:T(8,128)(2,1)} %constant.66.clone.z_ref, bf16[192,528]{1,0:T(8,128)(2,1)} %constant.67.clone.y_ref), custom_call_target="tpu_custom_call" | custom-call | flops 1046740992 | bytes 2578432 | tf_op jit(solution)/shard_map/density_to_ky_kz/pallas_call | solution.py:284
  79.4 4.4 %all-to-all-done.1.refs_1_ = s16[4,66,16,128]{3,2,1,0:T(8,128)(2,1)} async-done(((s16[4,66,16,128]{3,2,1,0:T(8,128)(2,1)}), s16[4,66,16,128]{3,2,1,0:T(8,128)(2,1)}, u32[]{:S(2)}, u32[]{:S(2)}) %all-to-all-start.1) | async-done | bytes 1081376 | tf_op jit(solution)/shard_map/all_to_all | solution.py:298
  83.8 4.2 %all-to-all-start.4 = ((s16[4,66,16,128]{3,2,1,0:T(8,128)(2,1)}), s16[4,66,16,128]{3,2,1,0:T(8,128)(2,1)}, u32[]{:S(2)}, u32[]{:S(2)}) async-start(s16[4,66,16,128]{3,2,1,0:T(8,128)(2,1)} %density_to_ky_kz.9), calls=%async_computation.4 | async-start | bytes 2162688 | tf_op jit(solution)/shard_map/all_to_all | solution.py:298
  88.1 1.2 broadcast_select_fusion.1
  89.3 2.5 collective-permute-start.5
  91.8 3.4 collective-permute-done.2.b_ref
  95.1 10.3 %density_to_ky_kz.8 = s16[4,66,16,128]{3,2,1,0:T(8,128)(2,1)} custom-call(bf16[16,30976]{1,0:T(8,128)(2,1)} %copy-done.4, bf16[16,30976]{1,0:T(8,128)(2,1)} %collective-permute-done.2.b_ref, bf16[768,256]{1,0:T(8,128)(2,1)} %constant.66.clone.z_ref, bf16[192,528]{1,0:T(8,128)(2,1)} %constant.67.clone.y_ref), custom_call_target="tpu_custom_call" | custom-call | flops 1046740992 | bytes 2578432 | tf_op jit(solution)/shard_map/density_to_ky_kz/pallas_call | solution.py:284
  105.5 3.7 all-to-all-start.2
  109.2 1.3 broadcast_select_fusion
  110.5 2.5 collective-permute-start.6
  113.0 1.7 collective-permute-done.5.b_ref
  114.7 1.0 copy-done.11
  115.7 10.4 %density_to_ky_kz.10 = s16[4,66,16,128]{3,2,1,0:T(8,128)(2,1)} custom-call(bf16[16,30976]{1,0:T(8,128)(2,1)} %copy-done.3, bf16[16,30976]{1,0:T(8,128)(2,1)} %copy-done.11, bf16[768,256]{1,0:T(8,128)(2,1)} %constant.66.clone.z_ref, bf16[192,528]{1,0:T(8,128)(2,1)} %constant.67.clone.y_ref), custom_call_target="tpu_custom_call" | custom-call | flops 1046740992 | bytes 2578432 | tf_op jit(solution)/shard_map/density_to_ky_kz/pallas_call | solution.py:284
  126.1 3.5 all-to-all-start.5
  129.6 6.2 %collective-permute-done.6.b_ref = bf16[16,30976]{1,0:T(8,128)(2,1)S(1)} collective-permute-done((bf16[16,30976]{1,0:T(8,128)(2,1)}, bf16[16,30976]{1,0:T(8,128)(2,1)S(1)}, u32[]{:S(2)}, u32[]{:S(2)}) %collective-permute-start.6) | collective-permute-done | bytes 991264 | tf_op jit(solution)/shard_map/ppermute | solution.py:346
  135.8 1.0 copy-done.12
  136.8 10.3 %density_to_ky_kz.11 = s16[4,66,16,128]{3,2,1,0:T(8,128)(2,1)} custom-call(bf16[16,30976]{1,0:T(8,128)(2,1)} %copy-done.4, bf16[16,30976]{1,0:T(8,128)(2,1)} %copy-done.12, bf16[768,256]{1,0:T(8,128)(2,1)} %constant.66.clone.z_ref, bf16[192,528]{1,0:T(8,128)(2,1)} %constant.67.clone.y_ref), custom_call_target="tpu_custom_call" | custom-call | flops 1046740992 | bytes 2578432 | tf_op jit(solution)/shard_map/density_to_ky_kz/pallas_call | solution.py:284
  147.1 4.3 %all-to-all-start.6 = ((s16[4,66,16,128]{3,2,1,0:T(8,128)(2,1)}), s16[4,66,16,128]{3,2,1,0:T(8,128)(2,1)}, u32[]{:S(2)}, u32[]{:S(2)}) async-start(s16[4,66,16,128]{3,2,1,0:T(8,128)(2,1)} %density_to_ky_kz.11), calls=%async_computation.6 | async-start | bytes 2162688 | tf_op jit(solution)/shard_map/all_to_all | solution.py:298
  151.4 17.6 %filter_along_x.2 = s16[4,66,48,128]{3,2,1,0:T(8,128)(2,1)} custom-call(s16[4,66,16,128]{3,2,1,0:T(8,128)(2,1)} %all-to-all-done.refs_0_, s16[4,66,16,128]{3,2,1,0:T(8,128)(2,1)} %all-to-all-done.1.refs_1_, s16[4,66,16,128]{3,2,1,0:T(8,128)(2,1)} %copy-done.9, f32[44,96,256]{2,1,0:T(8,128)} %fusion.5.refs_3_, bf16[176,576]{1,0:T(8,128)(2,1)} %constant.69.clone.refs_4_, ...), custom_call_target="tpu_custom_call" | custom-call | flops 3140222976 | bytes 7974912 | tf_op jit(solution)/shard_map/filter_along_x/pallas_call | solution.py:284
  169.0 3.7 all-to-all-start.3
  172.8 17.6 %filter_along_x.3 = s16[4,66,48,128]{3,2,1,0:T(8,128)(2,1)} custom-call(s16[4,66,16,128]{3,2,1,0:T(8,128)(2,1)} %all-to-all-done.4.refs_0_, s16[4,66,16,128]{3,2,1,0:T(8,128)(2,1)} %copy-done.10, s16[4,66,16,128]{3,2,1,0:T(8,128)(2,1)} %all-to-all-done.6.refs_2_, f32[44,96,256]{2,1,0:T(8,128)} %fusion.5.refs_3_, bf16[176,576]{1,0:T(8,128)(2,1)} %constant.69.clone.refs_4_, ...), custom_call_target="tpu_custom_call" | custom-call | flops 3140222976 | bytes 7974912 | tf_op jit(solution)/shard_map/filter_along_x/pallas_call | solution.py:284
  190.4 20.4 %all-to-all-done.3.in_ref = s16[4,66,48,128]{3,2,1,0:T(8,128)(2,1)S(1)} async-done(((s16[4,66,48,128]{3,2,1,0:T(8,128)(2,1)}), s16[4,66,48,128]{3,2,1,0:T(8,128)(2,1)S(1)}, u32[]{:S(2)}, u32[]{:S(2)}) %all-to-all-start.3) | async-done | bytes 3244064 | tf_op jit(solution)/shard_map/all_to_all | solution.py:298
  210.7 1.7 copy-done.1
  212.4 3.7 all-to-all-start.7
  216.8 1.4 collective-permute-start.3
  218.1 4.0 %collective-permute-done.3 = bf16[1]{0:T(256)(128)(2,1)} collective-permute-done((bf16[1]{0:T(256)(128)(2,1)}, bf16[1]{0:T(256)(128)(2,1)}, u32[]{:S(2)}, u32[]{:S(2)}) %collective-permute-start.3) | collective-permute-done | bytes 34 | tf_op jit(solution)/shard_map/ppermute | solution.py:336
  222.8 0.7 pad_maximum_fusion.occ
  223.5 13.0 %potential_terms.10 = (f32[16,30976]{1,0:T(8,128)}, s16[16,30976]{1,0:T(8,128)(2,1)}) custom-call(s16[4,66,48,128]{3,2,1,0:T(8,128)(2,1)} %copy-done.1, bf16[16,30976]{1,0:T(8,128)(2,1)} %copy-done.4, bf16[16,30976]{1,0:T(8,128)(2,1)} %collective-permute-done.2.b_ref, f32[2]{0:T(128)} %pad_maximum_fusion.occ, bf16[768,256]{1,0:T(8,128)(2,1)} %constant.66.clone.z_ref, ...), custom_call_target="tpu_custom_call" | custom-call | flops 1046740992 | bytes 5822472 | tf_op jit(solution)/shard_map/potential_terms/pallas_call | solution.py:284
  237.2 3.1 collective-permute-start.7
  240.2 0.6 collective-permute-done.7
  241.4 0.6 pad_maximum_fusion.1.occ
  242.0 13.0 %potential_terms.8 = (f32[16,30976]{1,0:T(8,128)}, s16[16,30976]{1,0:T(8,128)(2,1)}) custom-call(s16[4,66,48,128]{3,2,1,0:T(8,128)(2,1)} %copy-done.1, bf16[16,30976]{1,0:T(8,128)(2,1)} %copy-done.3, bf16[16,30976]{1,0:T(8,128)(2,1)} %collective-permute-done.1.b_ref, f32[2]{0:T(128)} %pad_maximum_fusion.occ, bf16[768,256]{1,0:T(8,128)(2,1)} %constant.66.clone.z_ref, ...), custom_call_target="tpu_custom_call" | custom-call | flops 1046740992 | bytes 5822472 | tf_op jit(solution)/shard_map/potential_terms/pallas_call | solution.py:284
  255.0 12.9 %potential_terms.6 = (f32[16,30976]{1,0:T(8,128)}, s16[16,30976]{1,0:T(8,128)(2,1)}) custom-call(s16[4,66,48,128]{3,2,1,0:T(8,128)(2,1)} %copy-done.1, bf16[16,30976]{1,0:T(8,128)(2,1)} %copy-done.2, bf16[16,30976]{1,0:T(8,128)(2,1)} %collective-permute-done.b_ref, f32[2]{0:T(128)} %pad_maximum_fusion.occ, bf16[768,256]{1,0:T(8,128)(2,1)} %constant.66.clone.z_ref, ...), custom_call_target="tpu_custom_call" | custom-call | flops 1046740992 | bytes 5822472 | tf_op jit(solution)/shard_map/potential_terms/pallas_call | solution.py:284
  268.0 1.1 collective-permute-start.8
  269.1 1.7 copy-done
  270.8 13.0 %potential_terms.11 = (f32[16,30976]{1,0:T(8,128)}, s16[16,30976]{1,0:T(8,128)(2,1)}) custom-call(s16[4,66,48,128]{3,2,1,0:T(8,128)(2,1)} %copy-done, bf16[16,30976]{1,0:T(8,128)(2,1)} %copy-done.4, bf16[16,30976]{1,0:T(8,128)(2,1)} %copy-done.12, f32[2]{0:T(128)} %pad_maximum_fusion.1.occ, bf16[768,256]{1,0:T(8,128)(2,1)} %constant.66.clone.z_ref, ...), custom_call_target="tpu_custom_call" | custom-call | flops 1046740992 | bytes 5822472 | tf_op jit(solution)/shard_map/potential_terms/pallas_call | solution.py:284
  283.8 5.0 %collective-permute-start.13 = (s16[16,30976]{1,0:T(8,128)(2,1)}, s16[16,30976]{1,0:T(8,128)(2,1)S(1)}, u32[]{:S(2)}, u32[]{:S(2)}) collective-permute-start(s16[16,30976]{1,0:T(8,128)(2,1)} %get-tuple-element.40), channel_id=1, source_target_pairs={{0,28},{4,0},{8,4},{12,8},{16,12},{20,16},{24,20},{28,24},{1,29},{... | collective-permute-start | bytes 2973704 | tf_op jit(solution)/shard_map/ppermute | solution.py:406
  288.8 13.0 %potential_terms.7 = (f32[16,30976]{1,0:T(8,128)}, s16[16,30976]{1,0:T(8,128)(2,1)}) custom-call(s16[4,66,48,128]{3,2,1,0:T(8,128)(2,1)} %copy-done, bf16[16,30976]{1,0:T(8,128)(2,1)} %copy-done.2, bf16[16,30976]{1,0:T(8,128)(2,1)} %collective-permute-done.4.b_ref, f32[2]{0:T(128)} %pad_maximum_fusion.1.occ, bf16[768,256]{1,0:T(8,128)(2,1)} %constant.66.clone.z_ref, ...), custom_call_target="tpu_custom_call" | custom-call | flops 1046740992 | bytes 5822472 | tf_op jit(solution)/shard_map/potential_terms/pallas_call | solution.py:284
  301.8 0.3 collective-permute-start.9
  302.0 12.9 %potential_terms.9 = (f32[16,30976]{1,0:T(8,128)}, s16[16,30976]{1,0:T(8,128)(2,1)}) custom-call(s16[4,66,48,128]{3,2,1,0:T(8,128)(2,1)} %copy-done, bf16[16,30976]{1,0:T(8,128)(2,1)} %copy-done.3, bf16[16,30976]{1,0:T(8,128)(2,1)} %copy-done.11, f32[2]{0:T(128)} %pad_maximum_fusion.1.occ, bf16[768,256]{1,0:T(8,128)(2,1)} %constant.66.clone.z_ref, ...), custom_call_target="tpu_custom_call" | custom-call | flops 1046740992 | bytes 5822472 | tf_op jit(solution)/shard_map/potential_terms/pallas_call | solution.py:284
  314.9 1.2 collective-permute-start.11
  316.1 6.7 %collective-permute-done.13.refs_11_ = s16[16,30976]{1,0:T(8,128)(2,1)S(1)} collective-permute-done((s16[16,30976]{1,0:T(8,128)(2,1)}, s16[16,30976]{1,0:T(8,128)(2,1)S(1)}, u32[]{:S(2)}, u32[]{:S(2)}) %collective-permute-start.13) | collective-permute-done | bytes 991264 | tf_op jit(solution)/shard_map/ppermute | solution.py:406
  322.9 21.2 %collective-permute-done.9.refs_3_ = s16[16,30976]{1,0:T(8,128)(2,1)S(1)} collective-permute-done((s16[16,30976]{1,0:T(8,128)(2,1)}, s16[16,30976]{1,0:T(8,128)(2,1)S(1)}, u32[]{:S(2)}, u32[]{:S(2)}) %collective-permute-start.9) | collective-permute-done | bytes 991264 | tf_op jit(solution)/shard_map/ppermute | solution.py:406
  344.1 20.0 %collective-permute-done.11.refs_7_ = s16[16,30976]{1,0:T(8,128)(2,1)S(1)} collective-permute-done((s16[16,30976]{1,0:T(8,128)(2,1)}, s16[16,30976]{1,0:T(8,128)(2,1)S(1)}, u32[]{:S(2)}, u32[]{:S(2)}) %collective-permute-start.11) | collective-permute-done | bytes 991264 | tf_op jit(solution)/shard_map/ppermute | solution.py:406
  364.1 0.9 copy-done.15
  365.1 12.9 %total_terms.1 = f32[1,44,30976]{2,1,0:T(8,128)} custom-call(f32[16,30976]{1,0:T(8,128)} %get-tuple-element.29.refs_0_, f32[16,30976]{1,0:T(8,128)} %get-tuple-element.30.refs_1_, s16[16,30976]{1,0:T(8,128)(2,1)} %collective-permute-done.8.refs_2_, s16[16,30976]{1,0:T(8,128)(2,1)} %copy-done.14, f32[16,30976]{1,0:T(8,128)} %get-tuple-element.33.refs_4_, ...), custom_call_target="tpu_custom_call" | custom-call | tf_op jit(solution)/shard_map/total_terms/pallas_call | solution.py:410
  378.0 7.6 %copy.8 = f32[1,44,30976]{2,0,1:T(1,128)} copy(f32[1,44,30976]{2,1,0:T(8,128)} %total_terms.1) | data formatting | bytes 10903552 | tf_op jit(solution)/shard_map/total_terms/pallas_call | solution.py:410
  (43 shorter events, 0.1 us)
Async XLA Ops:
  1.9 3.2 copy-start.7
  1.9 28.5 %copy-start.5 = (bf16[15,30976]{1,0:T(8,128)(2,1)}, bf16[15,30976]{1,0:T(8,128)(2,1)S(1)}, u32[]{:S(2)}) copy-start(bf16[15,30976]{1,0:T(8,128)(2,1)S(1)} %get-tuple-element.41) | copy-start | bytes 2787844
  2.0 28.4 %copy-start.2 = (bf16[16,30976]{1,0:T(8,128)(2,1)}, bf16[16,30976]{1,0:T(8,128)(2,1)S(1)}, u32[]{:S(2)}) copy-start(bf16[16,30976]{1,0:T(8,128)(2,1)S(1)} %pad.11.a_ref) | copy-start | bytes 2973700
  2.0 27.1 %collective-permute-start = (bf16[16,30976]{1,0:T(8,128)(2,1)S(1)}, bf16[16,30976]{1,0:T(8,128)(2,1)}, u32[]{:S(2)}, u32[]{:S(2)}) collective-permute-start(bf16[16,30976]{1,0:T(8,128)(2,1)S(1)} %pad.11.a_ref), channel_id=1, source_target_pairs={{0,8},{4,12},{8,16},{12,20},{16,24},{20,28},{24,0},{28,4},{1,9},{5... | collective-permute-start | bytes 2973704 | tf_op jit(solution)/shard_map/ppermute | solution.py:343
  5.2 24.0 %copy-start.8 = (bf16[15,30976]{1,0:T(8,128)(2,1)S(1)}, bf16[15,30976]{1,0:T(8,128)(2,1)}, u32[]{:S(2)}) copy-start(bf16[15,30976]{1,0:T(8,128)(2,1)} %copy-done.7) | copy-start | bytes 2787844
  5.3 38.3 %copy-start.3 = (bf16[16,30976]{1,0:T(8,128)(2,1)}, bf16[16,30976]{1,0:T(8,128)(2,1)S(1)}, u32[]{:S(2)}) copy-start(bf16[16,30976]{1,0:T(8,128)(2,1)S(1)} %pad.12.a_ref) | copy-start | bytes 2973700
  29.2 25.0 %collective-permute-start.1 = (bf16[16,30976]{1,0:T(8,128)(2,1)S(1)}, bf16[16,30976]{1,0:T(8,128)(2,1)}, u32[]{:S(2)}, u32[]{:S(2)}) collective-permute-start(bf16[16,30976]{1,0:T(8,128)(2,1)S(1)} %pad.12.a_ref), channel_id=1, source_target_pairs={{0,8},{4,12},{8,16},{12,20},{16,24},{20,28},{24,0},{28,4},{1,9},{5... | collective-permute-start | bytes 2973704 | tf_op jit(solution)/shard_map/ppermute | solution.py:343
  30.5 38.5 %collective-permute-start.4 = (bf16[16,30976]{1,0:T(8,128)(2,1)}, bf16[16,30976]{1,0:T(8,128)(2,1)}, u32[]{:S(2)}, u32[]{:S(2)}) collective-permute-start(bf16[16,30976]{1,0:T(8,128)(2,1)} %broadcast_select_fusion.2), channel_id=1, source_target_pairs={{0,4},{4,0},{8,12},{12,8},{16,20},{20,16},{24,28},{28,24},{1,5},{5... | collective-permute-start | bytes 2973704 | tf_op jit(solution)/shard_map/ppermute | solution.py:346
  43.5 21.0 %all-to-all-start = ((s16[4,66,16,128]{3,2,1,0:T(8,128)(2,1)}), s16[4,66,16,128]{3,2,1,0:T(8,128)(2,1)}, u32[]{:S(2)}, u32[]{:S(2)}) async-start(s16[4,66,16,128]{3,2,1,0:T(8,128)(2,1)} %density_to_ky_kz.6), calls=%async_computation | async-start | bytes 2162688 | tf_op jit(solution)/shard_map/all_to_all | solution.py:298
  49.5 29.8 %copy-start.4 = (bf16[16,30976]{1,0:T(8,128)(2,1)}, bf16[16,30976]{1,0:T(8,128)(2,1)S(1)}, u32[]{:S(2)}) copy-start(bf16[16,30976]{1,0:T(8,128)(2,1)S(1)} %pad.13.a_ref) | copy-start | bytes 2973700
  64.5 23.5 %copy-start.6 = (bf16[15,30976]{1,0:T(8,128)(2,1)S(1)}, bf16[15,30976]{1,0:T(8,128)(2,1)}, u32[]{:S(2)}) copy-start(bf16[15,30976]{1,0:T(8,128)(2,1)} %copy-done.5) | copy-start | bytes 2787844
  64.5 19.3 %all-to-all-start.1 = ((s16[4,66,16,128]{3,2,1,0:T(8,128)(2,1)}), s16[4,66,16,128]{3,2,1,0:T(8,128)(2,1)}, u32[]{:S(2)}, u32[]{:S(2)}) async-start(s16[4,66,16,128]{3,2,1,0:T(8,128)(2,1)} %density_to_ky_kz.7), calls=%async_computation.1 | async-start | bytes 2162688 | tf_op jit(solution)/shard_map/all_to_all | solution.py:298
  68.9 26.2 %collective-permute-start.2 = (bf16[16,30976]{1,0:T(8,128)(2,1)S(1)}, bf16[16,30976]{1,0:T(8,128)(2,1)}, u32[]{:S(2)}, u32[]{:S(2)}) collective-permute-start(bf16[16,30976]{1,0:T(8,128)(2,1)S(1)} %pad.13.a_ref), channel_id=1, source_target_pairs={{0,8},{4,12},{8,16},{12,20},{16,24},{20,28},{24,0},{28,4},{1,9},{5... | collective-permute-start | bytes 2973704 | tf_op jit(solution)/shard_map/ppermute | solution.py:343
  83.8 21.7 %all-to-all-start.4 = ((s16[4,66,16,128]{3,2,1,0:T(8,128)(2,1)}), s16[4,66,16,128]{3,2,1,0:T(8,128)(2,1)}, u32[]{:S(2)}, u32[]{:S(2)}) async-start(s16[4,66,16,128]{3,2,1,0:T(8,128)(2,1)} %density_to_ky_kz.9), calls=%async_computation.4 | async-start | bytes 2162688 | tf_op jit(solution)/shard_map/all_to_all | solution.py:298
  89.3 25.4 %collective-permute-start.5 = (bf16[16,30976]{1,0:T(8,128)(2,1)}, bf16[16,30976]{1,0:T(8,128)(2,1)S(1)}, u32[]{:S(2)}, u32[]{:S(2)}) collective-permute-start(bf16[16,30976]{1,0:T(8,128)(2,1)} %broadcast_select_fusion.1), channel_id=1, source_target_pairs={{0,4},{4,0},{8,12},{12,8},{16,20},{20,16},{24,28},{28,24},{1,5},{5... | collective-permute-start | bytes 2973704 | tf_op jit(solution)/shard_map/ppermute | solution.py:346
  105.5 20.6 %all-to-all-start.2 = ((s16[4,66,16,128]{3,2,1,0:T(8,128)(2,1)}), s16[4,66,16,128]{3,2,1,0:T(8,128)(2,1)S(1)}, u32[]{:S(2)}, u32[]{:S(2)}) async-start(s16[4,66,16,128]{3,2,1,0:T(8,128)(2,1)} %density_to_ky_kz.8), calls=%async_computation.2 | async-start | bytes 2162688 | tf_op jit(solution)/shard_map/all_to_all | solution.py:298
  110.5 25.3 %collective-permute-start.6 = (bf16[16,30976]{1,0:T(8,128)(2,1)}, bf16[16,30976]{1,0:T(8,128)(2,1)S(1)}, u32[]{:S(2)}, u32[]{:S(2)}) collective-permute-start(bf16[16,30976]{1,0:T(8,128)(2,1)} %broadcast_select_fusion), channel_id=1, source_target_pairs={{0,4},{4,0},{8,12},{12,8},{16,20},{20,16},{24,28},{28,24},{1,5},{5... | collective-permute-start | bytes 2973704 | tf_op jit(solution)/shard_map/ppermute | solution.py:346
  114.7 1.0 copy-start.11
  126.1 25.3 %copy-start.9 = (s16[4,66,16,128]{3,2,1,0:T(8,128)(2,1)}, s16[4,66,16,128]{3,2,1,0:T(8,128)(2,1)S(1)}, u32[]{:S(2)}) copy-start(s16[4,66,16,128]{3,2,1,0:T(8,128)(2,1)S(1)} %all-to-all-done.2.refs_2_) | copy-start | bytes 3244036
  126.1 21.1 %all-to-all-start.5 = ((s16[4,66,16,128]{3,2,1,0:T(8,128)(2,1)}), s16[4,66,16,128]{3,2,1,0:T(8,128)(2,1)S(1)}, u32[]{:S(2)}, u32[]{:S(2)}) async-start(s16[4,66,16,128]{3,2,1,0:T(8,128)(2,1)} %density_to_ky_kz.10), calls=%async_computation.5 | async-start | bytes 2162688 | tf_op jit(solution)/shard_map/all_to_all | solution.py:298
  135.8 1.0 copy-start.12
  147.1 21.9 %copy-start.10 = (s16[4,66,16,128]{3,2,1,0:T(8,128)(2,1)}, s16[4,66,16,128]{3,2,1,0:T(8,128)(2,1)S(1)}, u32[]{:S(2)}) copy-start(s16[4,66,16,128]{3,2,1,0:T(8,128)(2,1)S(1)} %all-to-all-done.5.refs_1_) | copy-start | bytes 3244036
  147.1 21.9 %all-to-all-start.6 = ((s16[4,66,16,128]{3,2,1,0:T(8,128)(2,1)}), s16[4,66,16,128]{3,2,1,0:T(8,128)(2,1)}, u32[]{:S(2)}, u32[]{:S(2)}) async-start(s16[4,66,16,128]{3,2,1,0:T(8,128)(2,1)} %density_to_ky_kz.11), calls=%async_computation.6 | async-start | bytes 2162688 | tf_op jit(solution)/shard_map/all_to_all | solution.py:298
  169.0 41.7 %all-to-all-start.3 = ((s16[4,66,48,128]{3,2,1,0:T(8,128)(2,1)}), s16[4,66,48,128]{3,2,1,0:T(8,128)(2,1)S(1)}, u32[]{:S(2)}, u32[]{:S(2)}) async-start(s16[4,66,48,128]{3,2,1,0:T(8,128)(2,1)} %filter_along_x.2), calls=%async_computation.3 | async-start | bytes 6488064 | tf_op jit(solution)/shard_map/all_to_all | solution.py:298
  210.7 1.7 copy-start.1
  212.4 56.7 %all-to-all-start.7 = ((s16[4,66,48,128]{3,2,1,0:T(8,128)(2,1)}), s16[4,66,48,128]{3,2,1,0:T(8,128)(2,1)S(1)}, u32[]{:S(2)}, u32[]{:S(2)}) async-start(s16[4,66,48,128]{3,2,1,0:T(8,128)(2,1)} %filter_along_x.3), calls=%async_computation.7 | async-start | bytes 6488064 | tf_op jit(solution)/shard_map/all_to_all | solution.py:298
  216.8 5.3 %collective-permute-start.3 = (bf16[1]{0:T(256)(128)(2,1)}, bf16[1]{0:T(256)(128)(2,1)}, u32[]{:S(2)}, u32[]{:S(2)}) collective-permute-start(bf16[1]{0:T(256)(128)(2,1)} %convert_element_type.41), channel_id=1, source_target_pairs={{0,8},{4,12},{8,16},{12,20},{16,24},{20,28},{24,0},{28,4},{1,9},{5... | collective-permute-start | bytes 14 | tf_op jit(solution)/shard_map/ppermute | solution.py:336
  236.5 78.5 %collective-permute-start.12 = (s16[16,30976]{1,0:T(8,128)(2,1)}, s16[16,30976]{1,0:T(8,128)(2,1)}, u32[]{:S(2)}, u32[]{:S(2)}) collective-permute-start(s16[16,30976]{1,0:T(8,128)(2,1)} %get-tuple-element.39), channel_id=1, source_target_pairs={{0,24},{4,28},{8,0},{12,4},{16,8},{20,12},{24,16},{28,20},{1,25},{... | collective-permute-start | bytes 2973704 | tf_op jit(solution)/shard_map/ppermute | solution.py:405
  237.2 3.7 collective-permute-start.7
  255.0 61.1 %collective-permute-start.10 = (s16[16,30976]{1,0:T(8,128)(2,1)}, s16[16,30976]{1,0:T(8,128)(2,1)}, u32[]{:S(2)}, u32[]{:S(2)}) collective-permute-start(s16[16,30976]{1,0:T(8,128)(2,1)} %get-tuple-element.35), channel_id=1, source_target_pairs={{0,24},{4,28},{8,0},{12,4},{16,8},{20,12},{24,16},{28,20},{1,25},{... | collective-permute-start | bytes 2973704 | tf_op jit(solution)/shard_map/ppermute | solution.py:405
  268.0 48.1 %collective-permute-start.8 = (s16[16,30976]{1,0:T(8,128)(2,1)}, s16[16,30976]{1,0:T(8,128)(2,1)}, u32[]{:S(2)}, u32[]{:S(2)}) collective-permute-start(s16[16,30976]{1,0:T(8,128)(2,1)} %get-tuple-element.31), channel_id=1, source_target_pairs={{0,24},{4,28},{8,0},{12,4},{16,8},{20,12},{24,16},{28,20},{1,25},{... | collective-permute-start | bytes 2973704 | tf_op jit(solution)/shard_map/ppermute | solution.py:405
  269.1 1.7 copy-start
  283.8 39.1 %collective-permute-start.13 = (s16[16,30976]{1,0:T(8,128)(2,1)}, s16[16,30976]{1,0:T(8,128)(2,1)S(1)}, u32[]{:S(2)}, u32[]{:S(2)}) collective-permute-start(s16[16,30976]{1,0:T(8,128)(2,1)} %get-tuple-element.40), channel_id=1, source_target_pairs={{0,28},{4,0},{8,4},{12,8},{16,12},{20,16},{24,20},{28,24},{1,29},{... | collective-permute-start | bytes 2973704 | tf_op jit(solution)/shard_map/ppermute | solution.py:406
  301.8 42.3 %collective-permute-start.9 = (s16[16,30976]{1,0:T(8,128)(2,1)}, s16[16,30976]{1,0:T(8,128)(2,1)S(1)}, u32[]{:S(2)}, u32[]{:S(2)}) collective-permute-start(s16[16,30976]{1,0:T(8,128)(2,1)} %get-tuple-element.32), channel_id=1, source_target_pairs={{0,28},{4,0},{8,4},{12,8},{16,12},{20,16},{24,20},{28,24},{1,29},{... | collective-permute-start | bytes 2973704 | tf_op jit(solution)/shard_map/ppermute | solution.py:406
  314.9 49.2 %collective-permute-start.11 = (s16[16,30976]{1,0:T(8,128)(2,1)}, s16[16,30976]{1,0:T(8,128)(2,1)S(1)}, u32[]{:S(2)}, u32[]{:S(2)}) collective-permute-start(s16[16,30976]{1,0:T(8,128)(2,1)} %get-tuple-element.36), channel_id=1, source_target_pairs={{0,28},{4,0},{8,4},{12,8},{16,12},{20,16},{24,20},{28,24},{1,29},{... | collective-permute-start | bytes 2973704 | tf_op jit(solution)/shard_map/ppermute | solution.py:406
  322.9 41.3 %copy-start.13 = (s16[16,30976]{1,0:T(8,128)(2,1)}, s16[16,30976]{1,0:T(8,128)(2,1)S(1)}, u32[]{:S(2)}) copy-start(s16[16,30976]{1,0:T(8,128)(2,1)S(1)} %collective-permute-done.13.refs_11_) | copy-start | bytes 2973700
  344.1 20.0 %copy-start.14 = (s16[16,30976]{1,0:T(8,128)(2,1)}, s16[16,30976]{1,0:T(8,128)(2,1)S(1)}, u32[]{:S(2)}) copy-start(s16[16,30976]{1,0:T(8,128)(2,1)S(1)} %collective-permute-done.9.refs_3_) | copy-start | bytes 2973700
  364.1 1.0 copy-start.15

commit v5 on v4

--- a/solution.py
+++ b/solution.py
@@ -217,7 +217,7 @@
     half = in_ref.shape[1] // 3
     group_lanes = 8 * grid_size
     z_table, y_table = z_ref[...], y_ref[...]
-    home, visitor = -0.5 * occ[0], -0.5 * occ[1]
+    home = -0.5 * occ[0]
 
     for block in range(blocks):
         base = block * block_rows
@@ -261,21 +261,17 @@
     def _(group):
         lanes = pl.ds(pl.multiple_of(group * group_lanes, 128), group_lanes)
         potential = field[:, lanes]
-        own_ref[:, lanes] = potential * b_ref[:, lanes].astype(F32) * visitor
+        visitor = b_ref[:, lanes].astype(F32)
+        own_ref[:, lanes] = potential * visitor * (-0.5 * visitor[CHUNK:])
         terms = potential * a_ref[:, lanes].astype(F32) * home
         ret_ref[:, lanes] = to_wire(coded(terms))
 
 
-def total_kernel(chunks, *refs):
+def total_kernel(far_own, near_own, far_arrived, near_arrived, *refs):
     out_ref = refs[-1]
-    slab = out_ref.shape[1]
-    for chunk in range(chunks):
-        first, second, third, fourth = refs[4 * chunk : 4 * chunk + 4]
-        total = first[...] + second[...]
-        total = total + decoded(from_wire(third[...])) + decoded(from_wire(fourth[...]))
-        start = chunk * CHUNK
-        stop = min(start + CHUNK, slab)
-        out_ref[0, start:stop] = total[: stop - start]
+    total = far_own[...] + near_own[...]
+    total = total + decoded(from_wire(far_arrived[...])) + decoded(from_wire(near_arrived[...]))
+    out_ref[:, 0, :] = total[: out_ref.shape[0]]
 
 
 def call(kernel, out_shape, scratch, name, flops, operands, in_specs=None):
@@ -324,6 +320,8 @@
     occupied = band_occ.astype(BF16)
     upward = [(i, (i + 2) % bands) for i in range(bands)]
     downward = [(i, (i - 2) % bands) for i in range(bands)]
+    odd_downward = [pair for pair in downward if pair[0] % 2 == 1]
+    even_downward = [pair for pair in downward if pair[0] % 2 == 0]
     downward_one = [(i, (i - 1) % bands) for i in range(bands)]
     swap = [(i, i ^ 1) for i in range(bands)]
     is_odd = lax.axis_index("band") % 2 == 1
@@ -333,17 +331,17 @@
         return jnp.pad(piece, ((0, ROWS - piece.shape[0]), (0, 0)))
 
     home = [chunk_of(chunk) for chunk in range(chunks)]
-    far_occ = lax.ppermute(occupied, "band", upward)
-    near_occ = lax.ppermute(jnp.where(is_odd, far_occ, occupied), "band", swap)
+    spare_row = jnp.arange(ROWS, dtype=jnp.int32)[:, None] == CHUNK
+    carrying = [jnp.where(spare_row, occupied, piece) for piece in home]
     far, near = [], []
     for chunk in range(chunks):
-        sent = home[chunk]
+        sent = carrying[chunk]
         if far:
             sent, far[-1] = lax.optimization_barrier((sent, far[-1]))
         far.append(lax.ppermute(sent, "band", upward))
     far[0], profile = lax.optimization_barrier((far[0], profile))
     for chunk in range(chunks):
-        near.append(lax.ppermute(jnp.where(is_odd, far[chunk], home[chunk]), "band", swap))
+        near.append(lax.ppermute(jnp.where(is_odd, far[chunk], carrying[chunk]), "band", swap))
     flops = 12 * ROWS * grid_size**3
 
     def forward(chunk, visitor):
@@ -390,32 +388,45 @@
             [piece, whole, whole, pl.BlockSpec(memory_space=pltpu.SMEM), whole, whole],
         )
 
-    home_occ = occupied.astype(F32)[0]
-    near_factors = jnp.stack([home_occ, near_occ.astype(F32)[0]])
-    far_factors = jnp.stack([home_occ, far_occ.astype(F32)[0]])
+    factors = occupied.astype(F32)
 
     far_wires = [exchange(forward(chunk, far)) for chunk in range(chunks)]
     near_wires = [exchange(forward(chunk, near)) for chunk in range(chunks)]
     far_wire = exchange(filtered(far_wires))
     near_wire = exchange(filtered(near_wires))
-    far_parts = [back(far_wire, chunk, far, far_factors) for chunk in range(chunks)]
-    near_parts = [back(near_wire, chunk, near, near_factors) for chunk in range(chunks)]
-    operands = []
-    for (far_own, far_return), (near_own, near_return) in zip(far_parts, near_parts):
-        far_arrived = lax.ppermute(far_return, "band", downward)
-        near_arrived = lax.ppermute(near_return, "band", downward_one)
-        operands += [far_own, near_own, far_arrived, near_arrived]
+    def returned(chunk, terms):
+        route = chunk % 3
+        if route == 0:
+            crossed = lax.ppermute(terms, "band", swap)
+            return jnp.where(is_odd, lax.ppermute(crossed, "band", odd_downward), crossed)
+        if route == 1:
+            lowered = lax.ppermute(terms, "band", even_downward)
+            return lax.ppermute(jnp.where(is_odd, terms, lowered), "band", swap)
+        return lax.ppermute(terms, "band", downward_one)
+
+    far_parts, near_parts = [], []
+    for wire, visitor, parts in ((far_wire, far, far_parts), (near_wire, near, near_parts)):
+        for chunk in range(chunks):
+            parts.append(back(wire, chunk, visitor, factors))
+            factors, *parts[-1] = lax.optimization_barrier((factors, *parts[-1]))
     width = 16 * grid_size
     spec = pl.BlockSpec((ROWS, width), lambda i: (0, i))
-    return pl.pallas_call(
-        functools.partial(total_kernel, chunks),
-        grid=(cells // width,),
-        out_shape=jax.ShapeDtypeStruct((1, slab, cells), F32),
-        in_specs=[spec] * len(operands),
-        out_specs=pl.BlockSpec((1, slab, width), lambda i: (0, 0, i)),
-        compiler_params=pltpu.CompilerParams(vmem_limit_bytes=VMEM_BYTES),
-        name="total_terms",
-    )(*operands)
+    result = None
+    for chunk in range(chunks):
+        (far_own, far_return), (near_own, near_return) = far_parts[chunk], near_parts[chunk]
+        operands = [far_own, near_own, lax.ppermute(far_return, "band", downward), returned(chunk, near_return)]
+        started = [] if result is None else [result]
+        result = pl.pallas_call(
+            total_kernel,
+            grid=(cells // width,),
+            out_shape=jax.ShapeDtypeStruct((slab, 1, cells), F32),
+            in_specs=[spec] * 4 + [pl.BlockSpec(memory_space=pl.ANY)] * len(started),
+            out_specs=pl.BlockSpec((min(CHUNK, slab), 1, width), functools.partial(lambda at, i: (at, 0, i), chunk)),
+            input_output_aliases={4: 0} if started else {},
+            compiler_params=pltpu.CompilerParams(vmem_limit_bytes=VMEM_BYTES),
+            name="total_terms",
+        )(*operands, *started)
+    return result.reshape(1, slab, cells)
 
 
 def solution(mesh):

time: 388 us -> 437 us (1.13)
  starting transfers between devices: 54.6 us -> 110 us
  waiting for transfers between devices: 111 us -> 91.9 us
  Pallas kernels: 188 us -> 200 us
  other arithmetic: 11.4 us -> 18.7 us
    ppermute x11, starting transfers between devices: 19.7 us -> 76 us  [the longest x1 61.9 us: returned(): return lax.ppermute(jnp.where(is_odd, terms, lowered), 'band', swap)]
    ppermute x11, waiting for transfers between devices: 60.5 us -> 42.6 us  [the longest x1 28 us: returned(): return lax.ppermute(jnp.where(is_odd, terms, lowered), 'band', swap)]
    pallas_call x1 -> x3, Pallas kernels: 12.9 us -> 24.8 us  [shards(): pl.pallas_call(total_kernel, grid=(cells // width,), out_shape=jax.ShapeD...]
    pallas_call x1 -> x0, local copies, waits for them, and re-layouts: 7.62 us -> none  [shards(): pl.pallas_call(functools.partial(total_kernel, chunks), grid=(cells // wi...]
    select_n x3 -> x5, other arithmetic: 3.79 us -> 8.3 us  [the longest x3 3.41 us: shards(): jnp.where(is_odd, far[chunk], carrying[chunk])]
    unnamed x32 -> x24, local copies, waits for them, and re-layouts: 6.34 us -> 9.17 us
  transfers between devices with their start and end apart: 22 -> 22, of which waited for: 12 -> 9; matrix products, arithmetic and copies ran while one was open for 3% -> 5% of each run, Pallas kernels for 45% -> 38%
where the time goes in v5:
time: 437 us; the launch traced here: 436 us
  Pallas kernels  200 us (46%)
  starting transfers between devices  110 us (25%)
  waiting for transfers between devices  91.9 us (21%)
  other arithmetic  18.7 us (4%)
  local copies, waits for them, and re-layouts  13.7 us (3%)
    pallas_call x14, Pallas kernels, call(): pl.pallas_call(kernel, grid=(1,) if in_specs else (), out_shape=out_shape...  176 us
    ppermute x1, starting transfers between devices, returned(): return lax.ppermute(jnp.where(is_odd, terms, lowered), 'band', swap)  61.9 us
    all_to_all x8, starting transfers between devices, exchange(): return lax.all_to_all(wire, 'fft', split_axis=0, concat_axis=0, tiled=True)  31 us
    ppermute x1, waiting for transfers between devices, returned(): return lax.ppermute(jnp.where(is_odd, terms, lowered), 'band', swap)  28 us
    all_to_all x8, waiting for transfers between devices, exchange(): return lax.all_to_all(wire, 'fft', split_axis=0, concat_axis=0, tiled=True)  24.9 us
    pallas_call x3, Pallas kernels, shards(): pl.pallas_call(total_kernel, grid=(cells // width,), out_shape=jax.ShapeD...  24.8 us
    ppermute x3, waiting for transfers between devices, shards(): far.append(lax.ppermute(sent, 'band', upward))  24.4 us
    unnamed x24, local copies, waits for them, and re-layouts  9.17 us
  transfers between devices with their start and end apart: 22, of which 9 were waited for; matrix products, arithmetic and copies ran while one was open for 5% of the time, Pallas kernels for 38%

profile of v5, /device:TPU:0, one launch (start us, length us, event | category | flops | bytes accessed | tf_op | source)
XLA Modules:
  0.0 435.7 jit_solution(8513245555428938903)
XLA Ops:
  0.7 1.9 slice_bitcast_fusion.1
  2.6 1.7 fusion.26
  4.3 3.0 collective-permute-start
  7.3 2.6 slice_bitcast_fusion
  10.0 0.1 broadcast_add_fusion
  10.0 6.2 %fusion.5.refs_3_ = f32[44,96,256]{2,1,0:T(8,128)} fusion(f32[256]{0:T(256)S(1)} %fusion.22, f32[44,96]{1,0:T(8,128)S(1)} %broadcast_add_fusion), kind=kLoop, calls=%fused_computation.9 | loop fusion | flops 29196288 | bytes 4343296 | tf_op jit(solution)/shard_map/mul | solution.py:79
  16.3 15.0 %collective-permute-done.b_ref = bf16[16,30976]{1,0:T(8,128)(2,1)S(1)} collective-permute-done((bf16[16,30976]{1,0:T(8,128)(2,1)S(1)}, bf16[16,30976]{1,0:T(8,128)(2,1)S(1)}, u32[]{:S(2)}, u32[]{:S(2)}) %collective-permute-start) | collective-permute-done | bytes 991264 | tf_op jit(solution)/shard_map/ppermute | solution.py:341
  31.3 1.2 broadcast_select_fusion.7
  32.5 1.5 collective-permute-start.3
  34.0 10.4 %density_to_ky_kz.6 = s16[4,66,16,128]{3,2,1,0:T(8,128)(2,1)} custom-call(bf16[16,30976]{1,0:T(8,128)(2,1)} %get-tuple-element.83.a_ref, bf16[16,30976]{1,0:T(8,128)(2,1)} %copy-done.2, bf16[768,256]{1,0:T(8,128)(2,1)} %constant.68.clone.z_ref, bf16[192,528]{1,0:T(8,128)(2,1)} %constant.69.clone.y_ref), custom_call_target="tpu_custom_call" | custom-call | flops 1046740992 | bytes 2578432 | tf_op jit(solution)/shard_map/density_to_ky_kz/pallas_call | solution.py:280
  44.4 3.5 all-to-all-start
  47.9 2.4 fusion.25
  50.3 6.0 %collective-permute-done.1.b_ref = bf16[16,30976]{1,0:T(8,128)(2,1)} collective-permute-done((bf16[16,30976]{1,0:T(8,128)(2,1)S(1)}, bf16[16,30976]{1,0:T(8,128)(2,1)}, u32[]{:S(2)}, u32[]{:S(2)}) %collective-permute-start.1) | collective-permute-done | bytes 991264 | tf_op jit(solution)/shard_map/ppermute | solution.py:341
  56.3 10.4 %density_to_ky_kz.7 = s16[4,66,16,128]{3,2,1,0:T(8,128)(2,1)} custom-call(bf16[16,30976]{1,0:T(8,128)(2,1)} %get-tuple-element.79.a_ref, bf16[16,30976]{1,0:T(8,128)(2,1)} %collective-permute-done.1.b_ref, bf16[768,256]{1,0:T(8,128)(2,1)} %constant.68.clone.z_ref, bf16[192,528]{1,0:T(8,128)(2,1)} %constant.69.clone.y_ref), custom_call_target="tpu_custom_call" | custom-call | flops 1046740992 | bytes 2578432 | tf_op jit(solution)/shard_map/density_to_ky_kz/pallas_call | solution.py:280
  66.7 1.0 copy-done.4
  67.6 4.2 all-to-all-start.1
  71.9 0.1 collective-permute-start.2
  72.0 10.3 %density_to_ky_kz.9 = s16[4,66,16,128]{3,2,1,0:T(8,128)(2,1)} custom-call(bf16[16,30976]{1,0:T(8,128)(2,1)} %get-tuple-element.83.a_ref, bf16[16,30976]{1,0:T(8,128)(2,1)} %collective-permute-done.3.b_ref, bf16[768,256]{1,0:T(8,128)(2,1)} %constant.68.clone.z_ref, bf16[192,528]{1,0:T(8,128)(2,1)} %constant.69.clone.y_ref), custom_call_target="tpu_custom_call" | custom-call | flops 1046740992 | bytes 2578432 | tf_op jit(solution)/shard_map/density_to_ky_kz/pallas_call | solution.py:280
  82.3 4.5 %all-to-all-done.1.refs_1_ = s16[4,66,16,128]{3,2,1,0:T(8,128)(2,1)} async-done(((s16[4,66,16,128]{3,2,1,0:T(8,128)(2,1)}), s16[4,66,16,128]{3,2,1,0:T(8,128)(2,1)}, u32[]{:S(2)}, u32[]{:S(2)}) %all-to-all-start.1) | async-done | bytes 1081376 | tf_op jit(solution)/shard_map/all_to_all | solution.py:294
  86.8 4.3 all-to-all-start.4
  91.0 1.1 broadcast_select_fusion.6
  92.1 2.5 collective-permute-start.4
  94.6 3.4 collective-permute-done.2.b_ref
  98.0 1.0 copy-done.3
  99.0 10.4 %density_to_ky_kz.8 = s16[4,66,16,128]{3,2,1,0:T(8,128)(2,1)} custom-call(bf16[16,30976]{1,0:T(8,128)(2,1)} %get-tuple-element.77.a_ref, bf16[16,30976]{1,0:T(8,128)(2,1)} %copy-done.3, bf16[768,256]{1,0:T(8,128)(2,1)} %constant.68.clone.z_ref, bf16[192,528]{1,0:T(8,128)(2,1)} %constant.69.clone.y_ref), custom_call_target="tpu_custom_call" | custom-call | flops 1046740992 | bytes 2578432 | tf_op jit(solution)/shard_map/density_to_ky_kz/pallas_call | solution.py:280
  109.3 3.7 all-to-all-start.2
  113.0 1.1 broadcast_select_fusion.5
  114.2 2.5 collective-permute-start.5
  116.6 0.7 collective-permute-done.4.b_ref
  117.3 1.0 copy-done.7
  118.3 10.4 %density_to_ky_kz.10 = s16[4,66,16,128]{3,2,1,0:T(8,128)(2,1)} custom-call(bf16[16,30976]{1,0:T(8,128)(2,1)} %get-tuple-element.79.a_ref, bf16[16,30976]{1,0:T(8,128)(2,1)} %copy-done.7, bf16[768,256]{1,0:T(8,128)(2,1)} %constant.68.clone.z_ref, bf16[192,528]{1,0:T(8,128)(2,1)} %constant.69.clone.y_ref), custom_call_target="tpu_custom_call" | custom-call | flops 1046740992 | bytes 2578432 | tf_op jit(solution)/shard_map/density_to_ky_kz/pallas_call | solution.py:280
  128.8 3.5 all-to-all-start.5
  132.3 7.0 %collective-permute-done.5.b_ref = bf16[16,30976]{1,0:T(8,128)(2,1)} collective-permute-done((bf16[16,30976]{1,0:T(8,128)(2,1)}, bf16[16,30976]{1,0:T(8,128)(2,1)}, u32[]{:S(2)}, u32[]{:S(2)}) %collective-permute-start.5) | collective-permute-done | bytes 991264 | tf_op jit(solution)/shard_map/ppermute | solution.py:344
  139.3 10.3 %density_to_ky_kz.11 = s16[4,66,16,128]{3,2,1,0:T(8,128)(2,1)} custom-call(bf16[16,30976]{1,0:T(8,128)(2,1)} %get-tuple-element.77.a_ref, bf16[16,30976]{1,0:T(8,128)(2,1)} %collective-permute-done.5.b_ref, bf16[768,256]{1,0:T(8,128)(2,1)} %constant.68.clone.z_ref, bf16[192,528]{1,0:T(8,128)(2,1)} %constant.69.clone.y_ref), custom_call_target="tpu_custom_call" | custom-call | flops 1046740992 | bytes 2578432 | tf_op jit(solution)/shard_map/density_to_ky_kz/pallas_call | solution.py:280
  149.7 4.3 all-to-all-start.6
  154.0 17.6 %filter_along_x.2 = s16[4,66,48,128]{3,2,1,0:T(8,128)(2,1)} custom-call(s16[4,66,16,128]{3,2,1,0:T(8,128)(2,1)} %copy-done.4, s16[4,66,16,128]{3,2,1,0:T(8,128)(2,1)} %all-to-all-done.1.refs_1_, s16[4,66,16,128]{3,2,1,0:T(8,128)(2,1)} %copy-done.5, f32[44,96,256]{2,1,0:T(8,128)} %fusion.5.refs_3_, bf16[176,576]{1,0:T(8,128)(2,1)} %constant.71.clone.refs_4_, ...), custom_call_target="tpu_custom_call" | custom-call | flops 3140222976 | bytes 7974912 | tf_op jit(solution)/shard_map/filter_along_x/pallas_call | solution.py:280
  171.6 3.7 all-to-all-start.3
  175.3 17.6 %filter_along_x.3 = s16[4,66,48,128]{3,2,1,0:T(8,128)(2,1)} custom-call(s16[4,66,16,128]{3,2,1,0:T(8,128)(2,1)} %all-to-all-done.4.refs_0_, s16[4,66,16,128]{3,2,1,0:T(8,128)(2,1)} %copy-done.6, s16[4,66,16,128]{3,2,1,0:T(8,128)(2,1)} %all-to-all-done.6.refs_2_, f32[44,96,256]{2,1,0:T(8,128)} %fusion.5.refs_3_, bf16[176,576]{1,0:T(8,128)(2,1)} %constant.71.clone.refs_4_, ...), custom_call_target="tpu_custom_call" | custom-call | flops 3140222976 | bytes 7974912 | tf_op jit(solution)/shard_map/filter_along_x/pallas_call | solution.py:280
  192.9 20.4 %all-to-all-done.3.in_ref = s16[4,66,48,128]{3,2,1,0:T(8,128)(2,1)S(1)} async-done(((s16[4,66,48,128]{3,2,1,0:T(8,128)(2,1)}), s16[4,66,48,128]{3,2,1,0:T(8,128)(2,1)S(1)}, u32[]{:S(2)}, u32[]{:S(2)}) %all-to-all-start.3) | async-done | bytes 3244064 | tf_op jit(solution)/shard_map/all_to_all | solution.py:294
  213.3 1.7 copy-done.1
  215.0 3.7 all-to-all-start.7
  218.7 13.1 %potential_terms.6 = (f32[16,30976]{1,0:T(8,128)}, s16[16,30976]{1,0:T(8,128)(2,1)}) custom-call(s16[4,66,48,128]{3,2,1,0:T(8,128)(2,1)} %copy-done.1, bf16[16,30976]{1,0:T(8,128)(2,1)} %get-tuple-element.83.a_ref, bf16[16,30976]{1,0:T(8,128)(2,1)} %copy-done.2, f32[1]{0:T(128)S(6)} %convert_element_type.35.occ, bf16[768,256]{1,0:T(8,128)(2,1)} %constant.68.clone.z_ref, ...), custom_call_target="tpu_custom_call" | custom-call | flops 1046740992 | bytes 5822468 | tf_op jit(solution)/shard_map/potential_terms/pallas_call | solution.py:280
  231.8 13.0 %potential_terms.7 = (f32[16,30976]{1,0:T(8,128)}, s16[16,30976]{1,0:T(8,128)(2,1)}) custom-call(s16[4,66,48,128]{3,2,1,0:T(8,128)(2,1)} %copy-done.1, bf16[16,30976]{1,0:T(8,128)(2,1)} %get-tuple-element.79.a_ref, bf16[16,30976]{1,0:T(8,128)(2,1)} %collective-permute-done.1.b_ref, f32[1]{0:T(128)S(6)} %convert_element_type.35.occ, ...), custom_call_target="tpu_custom_call" | custom-call | flops 1046740992 | bytes 5822468 | tf_op jit(solution)/shard_map/potential_terms/pallas_call | solution.py:280
  244.8 13.1 %potential_terms.8 = (f32[16,30976]{1,0:T(8,128)}, s16[16,30976]{1,0:T(8,128)(2,1)}) custom-call(s16[4,66,48,128]{3,2,1,0:T(8,128)(2,1)} %copy-done.1, bf16[16,30976]{1,0:T(8,128)(2,1)} %get-tuple-element.77.a_ref, bf16[16,30976]{1,0:T(8,128)(2,1)} %copy-done.3, f32[1]{0:T(128)S(6)} %convert_element_type.35.occ, bf16[768,256]{1,0:T(8,128)(2,1)} %constant.68.clone.z_ref, ...), custom_call_target="tpu_custom_call" | custom-call | flops 1046740992 | bytes 5822468 | tf_op jit(solution)/shard_map/potential_terms/pallas_call | solution.py:280
  257.9 1.7 copy-done
  259.6 13.0 %potential_terms.9 = (f32[16,30976]{1,0:T(8,128)}, s16[16,30976]{1,0:T(8,128)(2,1)}) custom-call(s16[4,66,48,128]{3,2,1,0:T(8,128)(2,1)} %copy-done, bf16[16,30976]{1,0:T(8,128)(2,1)} %get-tuple-element.83.a_ref, bf16[16,30976]{1,0:T(8,128)(2,1)} %collective-permute-done.3.b_ref, f32[1]{0:T(128)S(6)} %convert_element_type.35.occ, ...), custom_call_target="tpu_custom_call" | custom-call | flops 1046740992 | bytes 5822468 | tf_op jit(solution)/shard_map/potential_terms/pallas_call | solution.py:280
  272.5 13.0 %potential_terms.10 = (f32[16,30976]{1,0:T(8,128)}, s16[16,30976]{1,0:T(8,128)(2,1)}) custom-call(s16[4,66,48,128]{3,2,1,0:T(8,128)(2,1)} %copy-done, bf16[16,30976]{1,0:T(8,128)(2,1)} %get-tuple-element.79.a_ref, bf16[16,30976]{1,0:T(8,128)(2,1)} %copy-done.7, f32[1]{0:T(128)S(6)} %convert_element_type.35.occ, bf16[768,256]{1,0:T(8,128)(2,1)} %constant.68.clone.z_ref, ...), custom_call_target="tpu_custom_call" | custom-call | flops 1046740992 | bytes 5822468 | tf_op jit(solution)/shard_map/potential_terms/pallas_call | solution.py:280
  285.5 1.9 collective-permute-start.9
  287.5 1.4 collective-permute-start.12
  288.9 0.1 collective-permute-start.6
  289.0 3.6 collective-permute-start.8
  292.5 13.1 %potential_terms.11 = (f32[16,30976]{1,0:T(8,128)}, s16[16,30976]{1,0:T(8,128)(2,1)}) custom-call(s16[4,66,48,128]{3,2,1,0:T(8,128)(2,1)} %copy-done, bf16[16,30976]{1,0:T(8,128)(2,1)} %get-tuple-element.77.a_ref, bf16[16,30976]{1,0:T(8,128)(2,1)} %collective-permute-done.5.b_ref, f32[1]{0:T(128)S(6)} %convert_element_type.35.occ, ...), custom_call_target="tpu_custom_call" | custom-call | flops 1046740992 | bytes 5822468 | tf_op jit(solution)/shard_map/potential_terms/pallas_call | solution.py:280
  305.6 6.9 %collective-permute-done.9 = s16[16,30976]{1,0:T(8,128)(2,1)} collective-permute-done((s16[16,30976]{1,0:T(8,128)(2,1)}, s16[16,30976]{1,0:T(8,128)(2,1)}, u32[]{:S(2)}, u32[]{:S(2)}) %collective-permute-start.9) | collective-permute-done | bytes 991264 | tf_op jit(solution)/shard_map/ppermute | solution.py:403
  312.5 0.7 collective-permute-start.13
  313.2 2.4 broadcast_select_fusion.4
  315.6 61.9 %collective-permute-start.10 = (s16[16,30976]{1,0:T(8,128)(2,1)}, s16[16,30976]{1,0:T(8,128)(2,1)}, u32[]{:S(2)}, u32[]{:S(2)}) collective-permute-start(s16[16,30976]{1,0:T(8,128)(2,1)} %broadcast_select_fusion.4), channel_id=1, source_target_pairs={{0,4},{4,0},{8,12},{12,8},{16,20},{20,16},{24,28},{28,24},{1,5},{5... | collective-permute-start | bytes 2973704 | tf_op jit(solution)/shard_map/ppermute | solution.py:404
  377.5 2.5 broadcast_select_fusion.3.near_arrived
  380.0 1.0 copy-done.11
  380.9 8.3 %total_terms.3.refs_0_ = f32[44,1,30976]{2,1,0:T(1,128)} custom-call(f32[16,30976]{1,0:T(8,128)} %get-tuple-element.71.far_own, f32[16,30976]{1,0:T(8,128)} %get-tuple-element.72.near_own, s16[16,30976]{1,0:T(8,128)(2,1)} %copy-done.11, s16[16,30976]{1,0:T(8,128)(2,1)} %broadcast_select_fusion.3.near_arrived), custom_call_target="tpu_custom_call" | custom-call | tf_op jit(solution)/shard_map/total_terms/pallas_call | solution.py:419
  389.2 28.0 %collective-permute-done.10.near_arrived = s16[16,30976]{1,0:T(8,128)(2,1)} collective-permute-done((s16[16,30976]{1,0:T(8,128)(2,1)}, s16[16,30976]{1,0:T(8,128)(2,1)}, u32[]{:S(2)}, u32[]{:S(2)}) %collective-permute-start.10) | collective-permute-done | bytes 991264 | tf_op jit(solution)/shard_map/ppermute | solution.py:404
  417.2 8.2 %total_terms.4.refs_0_ = f32[44,1,30976]{2,1,0:T(1,128)} custom-call(f32[16,30976]{1,0:T(8,128)} %get-tuple-element.67.far_own, f32[16,30976]{1,0:T(8,128)} %get-tuple-element.68.near_own, s16[16,30976]{1,0:T(8,128)(2,1)} %copy-done.9, s16[16,30976]{1,0:T(8,128)(2,1)} %collective-permute-done.10.near_arrived, ...), custom_call_target="tpu_custom_call", output_to_operand_aliasing={{}: (4, {})} | custom-call | tf_op jit(solution)/shard_map/total_terms/pallas_call | solution.py:419
  425.5 0.9 copy-done.8
  426.4 1.0 copy-done.10
  427.4 8.3 %total_terms.5 = f32[44,1,30976]{2,1,0:T(1,128)} custom-call(f32[16,30976]{1,0:T(8,128)} %get-tuple-element.54.far_own, f32[16,30976]{1,0:T(8,128)} %get-tuple-element.64.near_own, s16[16,30976]{1,0:T(8,128)(2,1)} %copy-done.8, s16[16,30976]{1,0:T(8,128)(2,1)} %copy-done.10, f32[44,1,30976]{2,1,0:T(1,128)} %total_terms.4.refs_0_), custom_call_target="tpu_custom_call", output_to_operand_aliasing={{}: (4, {})} | custom-call | tf_op jit(solution)/shard_map/total_terms/pallas_call | solution.py:419
  (36 shorter events, 0.1 us)
Async XLA Ops:
  4.3 27.0 %collective-permute-start = (bf16[16,30976]{1,0:T(8,128)(2,1)S(1)}, bf16[16,30976]{1,0:T(8,128)(2,1)S(1)}, u32[]{:S(2)}, u32[]{:S(2)}) collective-permute-start(bf16[16,30976]{1,0:T(8,128)(2,1)S(1)} %get-tuple-element.84), channel_id=1, source_target_pairs={{0,8},{4,12},{8,16},{12,20},{16,24},{20,28},{24,0},{28,4},{1,9},{5... | collective-permute-start | bytes 2973704 | tf_op jit(solution)/shard_map/ppermute | solution.py:341
  31.3 2.7 copy-start.2
  31.3 25.0 %collective-permute-start.1 = (bf16[16,30976]{1,0:T(8,128)(2,1)S(1)}, bf16[16,30976]{1,0:T(8,128)(2,1)}, u32[]{:S(2)}, u32[]{:S(2)}) collective-permute-start(bf16[16,30976]{1,0:T(8,128)(2,1)S(1)} %get-tuple-element.42), channel_id=1, source_target_pairs={{0,8},{4,12},{8,16},{12,20},{16,24},{20,28},{24,0},{28,4},{1,9},{5... | collective-permute-start | bytes 2973704 | tf_op jit(solution)/shard_map/ppermute | solution.py:341
  32.5 39.5 %collective-permute-start.3 = (bf16[16,30976]{1,0:T(8,128)(2,1)}, bf16[16,30976]{1,0:T(8,128)(2,1)}, u32[]{:S(2)}, u32[]{:S(2)}) collective-permute-start(bf16[16,30976]{1,0:T(8,128)(2,1)} %broadcast_select_fusion.7), channel_id=1, source_target_pairs={{0,4},{4,0},{8,12},{12,8},{16,20},{20,16},{24,28},{28,24},{1,5},{5... | collective-permute-start | bytes 2973704 | tf_op jit(solution)/shard_map/ppermute | solution.py:344
  44.4 22.3 %all-to-all-start = ((s16[4,66,16,128]{3,2,1,0:T(8,128)(2,1)}), s16[4,66,16,128]{3,2,1,0:T(8,128)(2,1)S(1)}, u32[]{:S(2)}, u32[]{:S(2)}) async-start(s16[4,66,16,128]{3,2,1,0:T(8,128)(2,1)} %density_to_ky_kz.6), calls=%async_computation | async-start | bytes 2162688 | tf_op jit(solution)/shard_map/all_to_all | solution.py:294
  66.7 1.0 copy-start.4
  67.6 19.1 %all-to-all-start.1 = ((s16[4,66,16,128]{3,2,1,0:T(8,128)(2,1)}), s16[4,66,16,128]{3,2,1,0:T(8,128)(2,1)}, u32[]{:S(2)}, u32[]{:S(2)}) async-start(s16[4,66,16,128]{3,2,1,0:T(8,128)(2,1)} %density_to_ky_kz.7), calls=%async_computation.1 | async-start | bytes 2162688 | tf_op jit(solution)/shard_map/all_to_all | solution.py:294
  71.9 26.1 %collective-permute-start.2 = (bf16[16,30976]{1,0:T(8,128)(2,1)S(1)}, bf16[16,30976]{1,0:T(8,128)(2,1)S(1)}, u32[]{:S(2)}, u32[]{:S(2)}) collective-permute-start(bf16[16,30976]{1,0:T(8,128)(2,1)S(1)} %get-tuple-element.44), channel_id=1, source_target_pairs={{0,8},{4,12},{8,16},{12,20},{16,24},{20,28},{24,0},{28,4},{1,9},{5... | collective-permute-start | bytes 2973704 | tf_op jit(solution)/shard_map/ppermute | solution.py:341
  86.8 22.5 %all-to-all-start.4 = ((s16[4,66,16,128]{3,2,1,0:T(8,128)(2,1)}), s16[4,66,16,128]{3,2,1,0:T(8,128)(2,1)}, u32[]{:S(2)}, u32[]{:S(2)}) async-start(s16[4,66,16,128]{3,2,1,0:T(8,128)(2,1)} %density_to_ky_kz.9), calls=%async_computation.4 | async-start | bytes 2162688 | tf_op jit(solution)/shard_map/all_to_all | solution.py:294
  92.1 25.2 %collective-permute-start.4 = (bf16[16,30976]{1,0:T(8,128)(2,1)}, bf16[16,30976]{1,0:T(8,128)(2,1)S(1)}, u32[]{:S(2)}, u32[]{:S(2)}) collective-permute-start(bf16[16,30976]{1,0:T(8,128)(2,1)} %broadcast_select_fusion.6), channel_id=1, source_target_pairs={{0,4},{4,0},{8,12},{12,8},{16,20},{20,16},{24,28},{28,24},{1,5},{5... | collective-permute-start | bytes 2973704 | tf_op jit(solution)/shard_map/ppermute | solution.py:344
  98.0 1.0 copy-start.3
  109.3 19.4 %all-to-all-start.2 = ((s16[4,66,16,128]{3,2,1,0:T(8,128)(2,1)}), s16[4,66,16,128]{3,2,1,0:T(8,128)(2,1)S(1)}, u32[]{:S(2)}, u32[]{:S(2)}) async-start(s16[4,66,16,128]{3,2,1,0:T(8,128)(2,1)} %density_to_ky_kz.8), calls=%async_computation.2 | async-start | bytes 2162688 | tf_op jit(solution)/shard_map/all_to_all | solution.py:294
  114.2 25.2 %collective-permute-start.5 = (bf16[16,30976]{1,0:T(8,128)(2,1)}, bf16[16,30976]{1,0:T(8,128)(2,1)}, u32[]{:S(2)}, u32[]{:S(2)}) collective-permute-start(bf16[16,30976]{1,0:T(8,128)(2,1)} %broadcast_select_fusion.5), channel_id=1, source_target_pairs={{0,4},{4,0},{8,12},{12,8},{16,20},{20,16},{24,28},{28,24},{1,5},{5... | collective-permute-start | bytes 2973704 | tf_op jit(solution)/shard_map/ppermute | solution.py:344
  117.3 1.0 copy-start.7
  128.8 25.2 %copy-start.5 = (s16[4,66,16,128]{3,2,1,0:T(8,128)(2,1)}, s16[4,66,16,128]{3,2,1,0:T(8,128)(2,1)S(1)}, u32[]{:S(2)}) copy-start(s16[4,66,16,128]{3,2,1,0:T(8,128)(2,1)S(1)} %all-to-all-done.2.refs_2_) | copy-start | bytes 3244036
  128.8 20.9 %all-to-all-start.5 = ((s16[4,66,16,128]{3,2,1,0:T(8,128)(2,1)}), s16[4,66,16,128]{3,2,1,0:T(8,128)(2,1)S(1)}, u32[]{:S(2)}, u32[]{:S(2)}) async-start(s16[4,66,16,128]{3,2,1,0:T(8,128)(2,1)} %density_to_ky_kz.10), calls=%async_computation.5 | async-start | bytes 2162688 | tf_op jit(solution)/shard_map/all_to_all | solution.py:294
  149.7 21.9 %copy-start.6 = (s16[4,66,16,128]{3,2,1,0:T(8,128)(2,1)}, s16[4,66,16,128]{3,2,1,0:T(8,128)(2,1)S(1)}, u32[]{:S(2)}) copy-start(s16[4,66,16,128]{3,2,1,0:T(8,128)(2,1)S(1)} %all-to-all-done.5.refs_1_) | copy-start | bytes 3244036
  149.7 21.9 %all-to-all-start.6 = ((s16[4,66,16,128]{3,2,1,0:T(8,128)(2,1)}), s16[4,66,16,128]{3,2,1,0:T(8,128)(2,1)}, u32[]{:S(2)}, u32[]{:S(2)}) async-start(s16[4,66,16,128]{3,2,1,0:T(8,128)(2,1)} %density_to_ky_kz.11), calls=%async_computation.6 | async-start | bytes 2162688 | tf_op jit(solution)/shard_map/all_to_all | solution.py:294
  171.6 41.7 %all-to-all-start.3 = ((s16[4,66,48,128]{3,2,1,0:T(8,128)(2,1)}), s16[4,66,48,128]{3,2,1,0:T(8,128)(2,1)S(1)}, u32[]{:S(2)}, u32[]{:S(2)}) async-start(s16[4,66,48,128]{3,2,1,0:T(8,128)(2,1)} %filter_along_x.2), calls=%async_computation.3 | async-start | bytes 6488064 | tf_op jit(solution)/shard_map/all_to_all | solution.py:294
  213.3 1.7 copy-start.1
  215.0 42.9 %all-to-all-start.7 = ((s16[4,66,48,128]{3,2,1,0:T(8,128)(2,1)}), s16[4,66,48,128]{3,2,1,0:T(8,128)(2,1)S(1)}, u32[]{:S(2)}, u32[]{:S(2)}) async-start(s16[4,66,48,128]{3,2,1,0:T(8,128)(2,1)} %filter_along_x.3), calls=%async_computation.7 | async-start | bytes 6488064 | tf_op jit(solution)/shard_map/all_to_all | solution.py:294
  257.9 1.7 copy-start
  285.5 26.9 %collective-permute-start.9 = (s16[16,30976]{1,0:T(8,128)(2,1)}, s16[16,30976]{1,0:T(8,128)(2,1)}, u32[]{:S(2)}, u32[]{:S(2)}) collective-permute-start(s16[16,30976]{1,0:T(8,128)(2,1)} %get-tuple-element.70), channel_id=1, source_target_pairs={{0,24},{8,0},{16,8},{24,16},{1,25},{9,1},{17,9},{25,17},{2,26},{10... | collective-permute-start | bytes 2973704 | tf_op jit(solution)/shard_map/ppermute | solution.py:403
  287.5 25.0 %collective-permute-start.12 = (s16[16,30976]{1,0:T(8,128)(2,1)}, s16[16,30976]{1,0:T(8,128)(2,1)}, u32[]{:S(2)}, u32[]{:S(2)}) collective-permute-start(s16[16,30976]{1,0:T(8,128)(2,1)} %get-tuple-element.74), channel_id=1, source_target_pairs={{0,4},{4,0},{8,12},{12,8},{16,20},{20,16},{24,28},{28,24},{1,5},{5... | collective-permute-start | bytes 2973704 | tf_op jit(solution)/shard_map/ppermute | solution.py:400
  288.9 91.1 %collective-permute-start.11 = (s16[16,30976]{1,0:T(8,128)(2,1)}, s16[16,30976]{1,0:T(8,128)(2,1)S(1)}, u32[]{:S(2)}, u32[]{:S(2)}) collective-permute-start(s16[16,30976]{1,0:T(8,128)(2,1)} %get-tuple-element.73), channel_id=1, source_target_pairs={{0,24},{4,28},{8,0},{12,4},{16,8},{20,12},{24,16},{28,20},{1,25},{... | collective-permute-start | bytes 2973704 | tf_op jit(solution)/shard_map/ppermute | solution.py:417
  288.9 136.6 %collective-permute-start.6 = (s16[16,30976]{1,0:T(8,128)(2,1)}, s16[16,30976]{1,0:T(8,128)(2,1)S(1)}, u32[]{:S(2)}, u32[]{:S(2)}) collective-permute-start(s16[16,30976]{1,0:T(8,128)(2,1)} %get-tuple-element.65), channel_id=1, source_target_pairs={{0,24},{4,28},{8,0},{12,4},{16,8},{20,12},{24,16},{28,20},{1,25},{... | collective-permute-start | bytes 2973704 | tf_op jit(solution)/shard_map/ppermute | solution.py:417
  289.0 100.2 %collective-permute-start.8 = (s16[16,30976]{1,0:T(8,128)(2,1)}, s16[16,30976]{1,0:T(8,128)(2,1)S(1)}, u32[]{:S(2)}, u32[]{:S(2)}) collective-permute-start(s16[16,30976]{1,0:T(8,128)(2,1)} %get-tuple-element.69), channel_id=1, source_target_pairs={{0,24},{4,28},{8,0},{12,4},{16,8},{20,12},{24,16},{28,20},{1,25},{... | collective-permute-start | bytes 2973704 | tf_op jit(solution)/shard_map/ppermute | solution.py:417
  312.5 113.0 %collective-permute-start.7 = (s16[16,30976]{1,0:T(8,128)(2,1)}, s16[16,30976]{1,0:T(8,128)(2,1)S(1)}, u32[]{:S(2)}, u32[]{:S(2)}) collective-permute-start(s16[16,30976]{1,0:T(8,128)(2,1)} %get-tuple-element.66), channel_id=1, source_target_pairs={{0,28},{4,0},{8,4},{12,8},{16,12},{20,16},{24,20},{28,24},{1,29},{... | collective-permute-start | bytes 2973704 | tf_op jit(solution)/shard_map/ppermute | solution.py:405
  312.5 3.1 collective-permute-start.13
  315.6 101.6 %collective-permute-start.10 = (s16[16,30976]{1,0:T(8,128)(2,1)}, s16[16,30976]{1,0:T(8,128)(2,1)}, u32[]{:S(2)}, u32[]{:S(2)}) collective-permute-start(s16[16,30976]{1,0:T(8,128)(2,1)} %broadcast_select_fusion.4), channel_id=1, source_target_pairs={{0,4},{4,0},{8,12},{12,8},{16,20},{20,16},{24,28},{28,24},{1,5},{5... | collective-permute-start | bytes 2973704 | tf_op jit(solution)/shard_map/ppermute | solution.py:404
  380.0 1.0 copy-start.11
  389.2 28.0 %copy-start.9 = (s16[16,30976]{1,0:T(8,128)(2,1)}, s16[16,30976]{1,0:T(8,128)(2,1)S(1)}, u32[]{:S(2)}) copy-start(s16[16,30976]{1,0:T(8,128)(2,1)S(1)} %collective-permute-done.8.far_arrived) | copy-start | bytes 2973700
  425.5 1.0 copy-start.8
  426.4 1.0 copy-start.10

commit v6 on v5

--- a/solution.py
+++ b/solution.py
@@ -336,8 +336,8 @@
     far, near = [], []
     for chunk in range(chunks):
         sent = carrying[chunk]
-        if far:
-            sent, far[-1] = lax.optimization_barrier((sent, far[-1]))
+        if chunk >= 2:
+            sent, far[chunk - 2] = lax.optimization_barrier((sent, far[chunk - 2]))
         far.append(lax.ppermute(sent, "band", upward))
     far[0], profile = lax.optimization_barrier((far[0], profile))
     for chunk in range(chunks):
@@ -398,23 +398,31 @@
         route = chunk % 3
         if route == 0:
             crossed = lax.ppermute(terms, "band", swap)
+            crossed, far_arrived[-1] = lax.optimization_barrier((crossed, far_arrived[-1]))
             return jnp.where(is_odd, lax.ppermute(crossed, "band", odd_downward), crossed)
         if route == 1:
             lowered = lax.ppermute(terms, "band", even_downward)
             return lax.ppermute(jnp.where(is_odd, terms, lowered), "band", swap)
         return lax.ppermute(terms, "band", downward_one)
 
-    far_parts, near_parts = [], []
-    for wire, visitor, parts in ((far_wire, far, far_parts), (near_wire, near, near_parts)):
-        for chunk in range(chunks):
-            parts.append(back(wire, chunk, visitor, factors))
-            factors, *parts[-1] = lax.optimization_barrier((factors, *parts[-1]))
+    far_parts, near_parts, far_arrived = [], [], []
+    for chunk in range(chunks):
+        own, terms = back(far_wire, chunk, far, factors)
+        factors, terms = lax.optimization_barrier((factors, terms))
+        far_parts.append(own)
+        far_arrived.append(lax.ppermute(terms, "band", downward))
+    for chunk in range(chunks):
+        if chunk >= 1:
+            factors, far_arrived[chunk - 1] = lax.optimization_barrier((factors, far_arrived[chunk - 1]))
+        own, terms = back(near_wire, chunk, near, factors)
+        factors, terms = lax.optimization_barrier((factors, terms))
+        near_parts.append((own, terms))
     width = 16 * grid_size
     spec = pl.BlockSpec((ROWS, width), lambda i: (0, i))
     result = None
     for chunk in range(chunks):
-        (far_own, far_return), (near_own, near_return) = far_parts[chunk], near_parts[chunk]
-        operands = [far_own, near_own, lax.ppermute(far_return, "band", downward), returned(chunk, near_return)]
+        near_own, near_return = near_parts[chunk]
+        operands = [far_parts[chunk], near_own, far_arrived[chunk], returned(chunk, near_return)]
         started = [] if result is None else [result]
         result = pl.pallas_call(
             total_kernel,

time: 437 us -> 392 us (0.90)
  starting transfers between devices: 110 us -> 49.1 us
  waiting for transfers between devices: 91.9 us -> 110 us
    ppermute x1, starting transfers between devices: 61.9 us -> 0.01 us  [returned(): return lax.ppermute(jnp.where(is_odd, terms, lowered), 'band', swap)]
    ppermute x3, waiting for transfers between devices: 0.01 us -> 11.3 us  [shards(): far_arrived.append(lax.ppermute(terms, 'band', downward))]
    ppermute x3, waiting for transfers between devices: 24.4 us -> 30.9 us  [shards(): far.append(lax.ppermute(sent, 'band', upward))]
    unnamed x24 -> x26, local copies, waits for them, and re-layouts: 9.17 us -> 9.39 us
  transfers between devices with their start and end apart: 22 -> 22, of which waited for: 9 -> 9; matrix products, arithmetic and copies ran while one was open for 5% -> 4% of each run, Pallas kernels for 38% -> 49%
where the time goes in v6:
time: 392 us; the launch traced here: 391 us
  Pallas kernels  200 us (51%)
  waiting for transfers between devices  110 us (28%)
  starting transfers between devices  49.1 us (13%)
  other arithmetic  17 us (4%)
  local copies, waits for them, and re-layouts  12.9 us (3%)
    pallas_call x14, Pallas kernels, call(): pl.pallas_call(kernel, grid=(1,) if in_specs else (), out_shape=out_shape...  176 us
    all_to_all x8, starting transfers between devices, exchange(): return lax.all_to_all(wire, 'fft', split_axis=0, concat_axis=0, tiled=True)  30.9 us
    ppermute x3, waiting for transfers between devices, shards(): far.append(lax.ppermute(sent, 'band', upward))  30.9 us
    ppermute x1, waiting for transfers between devices, returned(): return lax.ppermute(jnp.where(is_odd, terms, lowered), 'band', swap)  30.2 us
    pallas_call x3, Pallas kernels, shards(): pl.pallas_call(total_kernel, grid=(cells // width,), out_shape=jax.ShapeD...  24.8 us
    all_to_all x8, waiting for transfers between devices, exchange(): return lax.all_to_all(wire, 'fft', split_axis=0, concat_axis=0, tiled=True)  21.8 us
    ppermute x3, waiting for transfers between devices, shards(): far_arrived.append(lax.ppermute(terms, 'band', downward))  11.3 us
    ppermute x3, waiting for transfers between devices, shards(): lax.ppermute(jnp.where(is_odd, far[chunk], carrying[chunk]), 'band', swap)  10.1 us
  transfers between devices with their start and end apart: 22, of which 9 were waited for; matrix products, arithmetic and copies ran while one was open for 4% of the time, Pallas kernels for 49%

profile of v6, /device:TPU:0, one launch (start us, length us, event | category | flops | bytes accessed | tf_op | source)
XLA Modules:
  0.0 390.7 jit_solution(10592776149896478890)
XLA Ops:
  0.0 1.6 slice_bitcast_fusion.1
  1.6 1.9 slice_bitcast_fusion
  4.2 2.4 fusion.25
  6.6 3.0 collective-permute-start.1
  9.7 1.6 collective-permute-start
  11.3 0.1 broadcast_add_fusion
  11.3 23.3 %collective-permute-done.1.b_ref = bf16[16,30976]{1,0:T(8,128)(2,1)S(1)} collective-permute-done((bf16[16,30976]{1,0:T(8,128)(2,1)}, bf16[16,30976]{1,0:T(8,128)(2,1)S(1)}, u32[]{:S(2)}, u32[]{:S(2)}) %collective-permute-start.1) | collective-permute-done | bytes 991264 | tf_op jit(solution)/shard_map/ppermute | solution.py:341
  34.7 1.0 copy-done.2
  35.7 10.4 %density_to_ky_kz.7 = s16[4,66,16,128]{3,2,1,0:T(8,128)(2,1)} custom-call(bf16[16,30976]{1,0:T(8,128)(2,1)} %get-tuple-element.79.a_ref, bf16[16,30976]{1,0:T(8,128)(2,1)} %copy-done.2, bf16[768,256]{1,0:T(8,128)(2,1)} %constant.68.clone.z_ref, bf16[192,528]{1,0:T(8,128)(2,1)} %constant.69.clone.y_ref), custom_call_target="tpu_custom_call" | custom-call | flops 1046740992 | bytes 2578432 | tf_op jit(solution)/shard_map/density_to_ky_kz/pallas_call | solution.py:280
  46.1 4.2 %all-to-all-start.1 = ((s16[4,66,16,128]{3,2,1,0:T(8,128)(2,1)}), s16[4,66,16,128]{3,2,1,0:T(8,128)(2,1)}, u32[]{:S(2)}, u32[]{:S(2)}) async-start(s16[4,66,16,128]{3,2,1,0:T(8,128)(2,1)} %density_to_ky_kz.7), calls=%async_computation.1 | async-start | bytes 2162688 | tf_op jit(solution)/shard_map/all_to_all | solution.py:294
  50.3 6.2 %fusion.5.refs_3_ = f32[44,96,256]{2,1,0:T(8,128)} fusion(f32[256]{0:T(256)S(1)} %fusion.22, f32[44,96]{1,0:T(8,128)S(1)} %broadcast_add_fusion), kind=kLoop, calls=%fused_computation.9 | loop fusion | flops 29196288 | bytes 4343296 | tf_op jit(solution)/shard_map/mul | solution.py:79
  56.6 1.0 copy-done.4
  57.6 10.4 %density_to_ky_kz.6 = s16[4,66,16,128]{3,2,1,0:T(8,128)(2,1)} custom-call(bf16[16,30976]{1,0:T(8,128)(2,1)} %get-tuple-element.81.a_ref, bf16[16,30976]{1,0:T(8,128)(2,1)} %copy-done.4, bf16[768,256]{1,0:T(8,128)(2,1)} %constant.68.clone.z_ref, bf16[192,528]{1,0:T(8,128)(2,1)} %constant.69.clone.y_ref), custom_call_target="tpu_custom_call" | custom-call | flops 1046740992 | bytes 2578432 | tf_op jit(solution)/shard_map/density_to_ky_kz/pallas_call | solution.py:280
  68.0 4.2 %all-to-all-start = ((s16[4,66,16,128]{3,2,1,0:T(8,128)(2,1)}), s16[4,66,16,128]{3,2,1,0:T(8,128)(2,1)}, u32[]{:S(2)}, u32[]{:S(2)}) async-start(s16[4,66,16,128]{3,2,1,0:T(8,128)(2,1)} %density_to_ky_kz.6), calls=%async_computation | async-start | bytes 2162688 | tf_op jit(solution)/shard_map/all_to_all | solution.py:294
  72.3 2.4 broadcast_select_fusion.6
  74.7 0.5 collective-permute-start.4
  75.2 7.6 %collective-permute-done.2.b_ref = bf16[16,30976]{1,0:T(8,128)(2,1)} collective-permute-done((bf16[16,30976]{1,0:T(8,128)(2,1)S(1)}, bf16[16,30976]{1,0:T(8,128)(2,1)}, u32[]{:S(2)}, u32[]{:S(2)}) %collective-permute-start.2) | collective-permute-done | bytes 991264 | tf_op jit(solution)/shard_map/ppermute | solution.py:341
  82.7 10.3 %density_to_ky_kz.8 = s16[4,66,16,128]{3,2,1,0:T(8,128)(2,1)} custom-call(bf16[16,30976]{1,0:T(8,128)(2,1)} %get-tuple-element.73.a_ref, bf16[16,30976]{1,0:T(8,128)(2,1)} %collective-permute-done.2.b_ref, bf16[768,256]{1,0:T(8,128)(2,1)} %constant.68.clone.z_ref, bf16[192,528]{1,0:T(8,128)(2,1)} %constant.69.clone.y_ref), custom_call_target="tpu_custom_call" | custom-call | flops 1046740992 | bytes 2578432 | tf_op jit(solution)/shard_map/density_to_ky_kz/pallas_call | solution.py:280
  93.1 3.5 all-to-all-start.2
  96.6 2.4 broadcast_select_fusion.7
  99.0 0.6 collective-permute-start.3
  99.6 10.4 %density_to_ky_kz.10 = s16[4,66,16,128]{3,2,1,0:T(8,128)(2,1)} custom-call(bf16[16,30976]{1,0:T(8,128)(2,1)} %get-tuple-element.79.a_ref, bf16[16,30976]{1,0:T(8,128)(2,1)} %collective-permute-done.4.b_ref, bf16[768,256]{1,0:T(8,128)(2,1)} %constant.68.clone.z_ref, bf16[192,528]{1,0:T(8,128)(2,1)} %constant.69.clone.y_ref), custom_call_target="tpu_custom_call" | custom-call | flops 1046740992 | bytes 2578432 | tf_op jit(solution)/shard_map/density_to_ky_kz/pallas_call | solution.py:280
  109.9 1.5 all-to-all-done.2.refs_2_
  111.4 4.4 %all-to-all-start.5 = ((s16[4,66,16,128]{3,2,1,0:T(8,128)(2,1)}), s16[4,66,16,128]{3,2,1,0:T(8,128)(2,1)}, u32[]{:S(2)}, u32[]{:S(2)}) async-start(s16[4,66,16,128]{3,2,1,0:T(8,128)(2,1)} %density_to_ky_kz.10), calls=%async_computation.5 | async-start | bytes 2162688 | tf_op jit(solution)/shard_map/all_to_all | solution.py:294
  115.9 1.1 broadcast_select_fusion.5
  116.9 3.0 collective-permute-start.5
  119.9 4.1 %collective-permute-done.3.b_ref = bf16[16,30976]{1,0:T(8,128)(2,1)S(1)} collective-permute-done((bf16[16,30976]{1,0:T(8,128)(2,1)}, bf16[16,30976]{1,0:T(8,128)(2,1)S(1)}, u32[]{:S(2)}, u32[]{:S(2)}) %collective-permute-start.3) | collective-permute-done | bytes 991264 | tf_op jit(solution)/shard_map/ppermute | solution.py:344
  123.9 1.0 copy-done.9
  124.9 10.4 %density_to_ky_kz.9 = s16[4,66,16,128]{3,2,1,0:T(8,128)(2,1)} custom-call(bf16[16,30976]{1,0:T(8,128)(2,1)} %get-tuple-element.81.a_ref, bf16[16,30976]{1,0:T(8,128)(2,1)} %copy-done.9, bf16[768,256]{1,0:T(8,128)(2,1)} %constant.68.clone.z_ref, bf16[192,528]{1,0:T(8,128)(2,1)} %constant.69.clone.y_ref), custom_call_target="tpu_custom_call" | custom-call | flops 1046740992 | bytes 2578432 | tf_op jit(solution)/shard_map/density_to_ky_kz/pallas_call | solution.py:280
  135.3 3.5 all-to-all-start.4
  138.8 6.0 %collective-permute-done.5.b_ref = bf16[16,30976]{1,0:T(8,128)(2,1)} collective-permute-done((bf16[16,30976]{1,0:T(8,128)(2,1)}, bf16[16,30976]{1,0:T(8,128)(2,1)}, u32[]{:S(2)}, u32[]{:S(2)}) %collective-permute-start.5) | collective-permute-done | bytes 991264 | tf_op jit(solution)/shard_map/ppermute | solution.py:344
  144.8 10.4 %density_to_ky_kz.11 = s16[4,66,16,128]{3,2,1,0:T(8,128)(2,1)} custom-call(bf16[16,30976]{1,0:T(8,128)(2,1)} %get-tuple-element.73.a_ref, bf16[16,30976]{1,0:T(8,128)(2,1)} %collective-permute-done.5.b_ref, bf16[768,256]{1,0:T(8,128)(2,1)} %constant.68.clone.z_ref, bf16[192,528]{1,0:T(8,128)(2,1)} %constant.69.clone.y_ref), custom_call_target="tpu_custom_call" | custom-call | flops 1046740992 | bytes 2578432 | tf_op jit(solution)/shard_map/density_to_ky_kz/pallas_call | solution.py:280
  155.2 3.5 all-to-all-start.6
  158.8 17.6 %filter_along_x.2 = s16[4,66,48,128]{3,2,1,0:T(8,128)(2,1)} custom-call(s16[4,66,16,128]{3,2,1,0:T(8,128)(2,1)} %all-to-all-done.refs_0_, s16[4,66,16,128]{3,2,1,0:T(8,128)(2,1)} %all-to-all-done.1.refs_1_, s16[4,66,16,128]{3,2,1,0:T(8,128)(2,1)} %copy-done.6, f32[44,96,256]{2,1,0:T(8,128)} %fusion.5.refs_3_, bf16[176,576]{1,0:T(8,128)(2,1)} %constant.71.clone.refs_4_, ...), custom_call_target="tpu_custom_call" | custom-call | flops 3140222976 | bytes 7974912 | tf_op jit(solution)/shard_map/filter_along_x/pallas_call | solution.py:280
  176.4 1.0 copy-done.8
  177.4 3.7 all-to-all-start.3
  181.1 17.6 %filter_along_x.3 = s16[4,66,48,128]{3,2,1,0:T(8,128)(2,1)} custom-call(s16[4,66,16,128]{3,2,1,0:T(8,128)(2,1)} %copy-done.7, s16[4,66,16,128]{3,2,1,0:T(8,128)(2,1)} %all-to-all-done.5.refs_1_, s16[4,66,16,128]{3,2,1,0:T(8,128)(2,1)} %copy-done.8, f32[44,96,256]{2,1,0:T(8,128)} %fusion.5.refs_3_, bf16[176,576]{1,0:T(8,128)(2,1)} %constant.71.clone.refs_4_, ...), custom_call_target="tpu_custom_call" | custom-call | flops 3140222976 | bytes 7974912 | tf_op jit(solution)/shard_map/filter_along_x/pallas_call | solution.py:280
  198.7 20.3 %all-to-all-done.3.in_ref = s16[4,66,48,128]{3,2,1,0:T(8,128)(2,1)S(1)} async-done(((s16[4,66,48,128]{3,2,1,0:T(8,128)(2,1)}), s16[4,66,48,128]{3,2,1,0:T(8,128)(2,1)S(1)}, u32[]{:S(2)}, u32[]{:S(2)}) %all-to-all-start.3) | async-done | bytes 3244064 | tf_op jit(solution)/shard_map/all_to_all | solution.py:294
  219.1 1.7 copy-done.1
  220.8 3.7 all-to-all-start.7
  224.5 13.0 %potential_terms.6 = (f32[16,30976]{1,0:T(8,128)}, s16[16,30976]{1,0:T(8,128)(2,1)}) custom-call(s16[4,66,48,128]{3,2,1,0:T(8,128)(2,1)} %copy-done.1, bf16[16,30976]{1,0:T(8,128)(2,1)} %get-tuple-element.81.a_ref, bf16[16,30976]{1,0:T(8,128)(2,1)} %copy-done.4, f32[1]{0:T(128)S(6)} %convert_element_type.39.occ, bf16[768,256]{1,0:T(8,128)(2,1)} %constant.68.clone.z_ref, ...), custom_call_target="tpu_custom_call" | custom-call | flops 1046740992 | bytes 5822468 | tf_op jit(solution)/shard_map/potential_terms/pallas_call | solution.py:280
  237.5 0.3 collective-permute-start.6
  237.8 13.0 %potential_terms.7 = (f32[16,30976]{1,0:T(8,128)}, s16[16,30976]{1,0:T(8,128)(2,1)}) custom-call(s16[4,66,48,128]{3,2,1,0:T(8,128)(2,1)} %copy-done.1, bf16[16,30976]{1,0:T(8,128)(2,1)} %get-tuple-element.79.a_ref, bf16[16,30976]{1,0:T(8,128)(2,1)} %copy-done.2, f32[1]{0:T(128)S(6)} %convert_element_type.39.occ, bf16[768,256]{1,0:T(8,128)(2,1)} %constant.68.clone.z_ref, ...), custom_call_target="tpu_custom_call" | custom-call | flops 1046740992 | bytes 5822468 | tf_op jit(solution)/shard_map/potential_terms/pallas_call | solution.py:280
  250.8 13.1 %potential_terms.8 = (f32[16,30976]{1,0:T(8,128)}, s16[16,30976]{1,0:T(8,128)(2,1)}) custom-call(s16[4,66,48,128]{3,2,1,0:T(8,128)(2,1)} %copy-done.1, bf16[16,30976]{1,0:T(8,128)(2,1)} %get-tuple-element.73.a_ref, bf16[16,30976]{1,0:T(8,128)(2,1)} %collective-permute-done.2.b_ref, f32[1]{0:T(128)S(6)} %convert_element_type.39.occ, ...), custom_call_target="tpu_custom_call" | custom-call | flops 1046740992 | bytes 5822468 | tf_op jit(solution)/shard_map/potential_terms/pallas_call | solution.py:280
  263.9 0.4 collective-permute-start.9
  264.3 0.7 collective-permute-start.7
  265.0 1.7 copy-done
  266.7 13.0 %potential_terms.9 = (f32[16,30976]{1,0:T(8,128)}, s16[16,30976]{1,0:T(8,128)(2,1)}) custom-call(s16[4,66,48,128]{3,2,1,0:T(8,128)(2,1)} %copy-done, bf16[16,30976]{1,0:T(8,128)(2,1)} %get-tuple-element.81.a_ref, bf16[16,30976]{1,0:T(8,128)(2,1)} %copy-done.9, f32[1]{0:T(128)S(6)} %convert_element_type.39.occ, bf16[768,256]{1,0:T(8,128)(2,1)} %constant.68.clone.z_ref, ...), custom_call_target="tpu_custom_call" | custom-call | flops 1046740992 | bytes 5822468 | tf_op jit(solution)/shard_map/potential_terms/pallas_call | solution.py:280
  279.7 0.6 collective-permute-start.8
  280.3 13.0 %potential_terms.10 = (f32[16,30976]{1,0:T(8,128)}, s16[16,30976]{1,0:T(8,128)(2,1)}) custom-call(s16[4,66,48,128]{3,2,1,0:T(8,128)(2,1)} %copy-done, bf16[16,30976]{1,0:T(8,128)(2,1)} %get-tuple-element.79.a_ref, bf16[16,30976]{1,0:T(8,128)(2,1)} %collective-permute-done.4.b_ref, f32[1]{0:T(128)S(6)} %convert_element_type.39.occ, ...), custom_call_target="tpu_custom_call" | custom-call | flops 1046740992 | bytes 5822468 | tf_op jit(solution)/shard_map/potential_terms/pallas_call | solution.py:280
  293.3 5.6 %collective-permute-start.11 = (s16[16,30976]{1,0:T(8,128)(2,1)}, s16[16,30976]{1,0:T(8,128)(2,1)S(1)}, u32[]{:S(2)}, u32[]{:S(2)}) collective-permute-start(s16[16,30976]{1,0:T(8,128)(2,1)} %get-tuple-element.66), channel_id=1, source_target_pairs={{0,24},{8,0},{16,8},{24,16},{1,25},{9,1},{17,9},{25,17},{2,26},{10... | collective-permute-start | bytes 2973704 | tf_op jit(solution)/shard_map/ppermute | solution.py:404
  298.9 11.3 %collective-permute-done.7.far_arrived = s16[16,30976]{1,0:T(8,128)(2,1)} collective-permute-done((s16[16,30976]{1,0:T(8,128)(2,1)}, s16[16,30976]{1,0:T(8,128)(2,1)}, u32[]{:S(2)}, u32[]{:S(2)}) %collective-permute-start.7) | collective-permute-done | bytes 991264 | tf_op jit(solution)/shard_map/ppermute | solution.py:413
  310.2 13.0 %potential_terms.11 = (f32[16,30976]{1,0:T(8,128)}, s16[16,30976]{1,0:T(8,128)(2,1)}) custom-call(s16[4,66,48,128]{3,2,1,0:T(8,128)(2,1)} %copy-done, bf16[16,30976]{1,0:T(8,128)(2,1)} %get-tuple-element.73.a_ref, bf16[16,30976]{1,0:T(8,128)(2,1)} %collective-permute-done.5.b_ref, f32[1]{0:T(128)S(6)} %convert_element_type.39.occ, ...), custom_call_target="tpu_custom_call" | custom-call | flops 1046740992 | bytes 5822468 | tf_op jit(solution)/shard_map/potential_terms/pallas_call | solution.py:280
  323.2 1.3 collective-permute-start.10
  324.6 0.7 collective-permute-start.13
  325.3 6.1 %collective-permute-done.11 = s16[16,30976]{1,0:T(8,128)(2,1)S(1)} collective-permute-done((s16[16,30976]{1,0:T(8,128)(2,1)}, s16[16,30976]{1,0:T(8,128)(2,1)S(1)}, u32[]{:S(2)}, u32[]{:S(2)}) %collective-permute-start.11) | collective-permute-done | bytes 991264 | tf_op jit(solution)/shard_map/ppermute | solution.py:404
  331.3 1.2 broadcast_select_fusion.4
  332.6 1.2 broadcast_select_fusion.3.near_arrived
  333.7 8.3 %total_terms.3.refs_0_ = f32[44,1,30976]{2,1,0:T(1,128)} custom-call(f32[16,30976]{1,0:T(8,128)} %get-tuple-element.67.far_own, f32[16,30976]{1,0:T(8,128)} %get-tuple-element.68.near_own, s16[16,30976]{1,0:T(8,128)(2,1)} %collective-permute-done.6.far_arrived, s16[16,30976]{1,0:T(8,128)(2,1)} %broadcast_select_fusion.3.near_arrived), custom_call_target="tpu_custom_call" | custom-call | tf_op jit(solution)/shard_map/total_terms/pallas_call | solution.py:427
  342.0 30.2 %collective-permute-done.12.near_arrived = s16[16,30976]{1,0:T(8,128)(2,1)S(1)} collective-permute-done((s16[16,30976]{1,0:T(8,128)(2,1)}, s16[16,30976]{1,0:T(8,128)(2,1)S(1)}, u32[]{:S(2)}, u32[]{:S(2)}) %collective-permute-start.12) | collective-permute-done | bytes 991264 | tf_op jit(solution)/shard_map/ppermute | solution.py:405
  372.2 1.0 copy-done.12
  373.2 8.3 %total_terms.4.refs_0_ = f32[44,1,30976]{2,1,0:T(1,128)} custom-call(f32[16,30976]{1,0:T(8,128)} %get-tuple-element.63.far_own, f32[16,30976]{1,0:T(8,128)} %get-tuple-element.64.near_own, s16[16,30976]{1,0:T(8,128)(2,1)} %collective-permute-done.7.far_arrived, s16[16,30976]{1,0:T(8,128)(2,1)} %copy-done.12, ...), custom_call_target="tpu_custom_call", output_to_operand_aliasing={{}: (4, {})} | custom-call | tf_op jit(solution)/shard_map/total_terms/pallas_call | solution.py:427
  381.4 1.0 copy-done.10
  382.4 8.3 %total_terms.5 = f32[44,1,30976]{2,1,0:T(1,128)} custom-call(f32[16,30976]{1,0:T(8,128)} %get-tuple-element.46.far_own, f32[16,30976]{1,0:T(8,128)} %get-tuple-element.57.near_own, s16[16,30976]{1,0:T(8,128)(2,1)} %collective-permute-done.9.far_arrived, s16[16,30976]{1,0:T(8,128)(2,1)} %copy-done.10, ...), custom_call_target="tpu_custom_call", output_to_operand_aliasing={{}: (4, {})} | custom-call | tf_op jit(solution)/shard_map/total_terms/pallas_call | solution.py:427
  (37 shorter events, 0.1 us)
Async XLA Ops:
  6.6 28.0 %collective-permute-start.1 = (bf16[16,30976]{1,0:T(8,128)(2,1)}, bf16[16,30976]{1,0:T(8,128)(2,1)S(1)}, u32[]{:S(2)}, u32[]{:S(2)}) collective-permute-start(bf16[16,30976]{1,0:T(8,128)(2,1)} %get-tuple-element.80), channel_id=1, source_target_pairs={{0,8},{4,12},{8,16},{12,20},{16,24},{20,28},{24,0},{28,4},{1,9},{5... | collective-permute-start | bytes 2973704 | tf_op jit(solution)/shard_map/ppermute | solution.py:341
  9.7 46.9 %collective-permute-start = (bf16[16,30976]{1,0:T(8,128)(2,1)}, bf16[16,30976]{1,0:T(8,128)(2,1)S(1)}, u32[]{:S(2)}, u32[]{:S(2)}) collective-permute-start(bf16[16,30976]{1,0:T(8,128)(2,1)} %get-tuple-element.82), channel_id=1, source_target_pairs={{0,8},{4,12},{8,16},{12,20},{16,24},{20,28},{24,0},{28,4},{1,9},{5... | collective-permute-start | bytes 2973704 | tf_op jit(solution)/shard_map/ppermute | solution.py:341
  34.7 1.0 copy-start.2
  46.1 22.0 %all-to-all-start.1 = ((s16[4,66,16,128]{3,2,1,0:T(8,128)(2,1)}), s16[4,66,16,128]{3,2,1,0:T(8,128)(2,1)}, u32[]{:S(2)}, u32[]{:S(2)}) async-start(s16[4,66,16,128]{3,2,1,0:T(8,128)(2,1)} %density_to_ky_kz.7), calls=%async_computation.1 | async-start | bytes 2162688 | tf_op jit(solution)/shard_map/all_to_all | solution.py:294
  50.3 22.0 %copy-start.3 = (bf16[16,30976]{1,0:T(8,128)(2,1)S(1)}, bf16[16,30976]{1,0:T(8,128)(2,1)}, u32[]{:S(2)}) copy-start(bf16[16,30976]{1,0:T(8,128)(2,1)} %copy-done.2) | copy-start | bytes 2973700
  56.6 1.1 copy-start.4
  56.6 26.2 %collective-permute-start.2 = (bf16[16,30976]{1,0:T(8,128)(2,1)S(1)}, bf16[16,30976]{1,0:T(8,128)(2,1)}, u32[]{:S(2)}, u32[]{:S(2)}) collective-permute-start(bf16[16,30976]{1,0:T(8,128)(2,1)S(1)} %get-tuple-element.40), channel_id=1, source_target_pairs={{0,8},{4,12},{8,16},{12,20},{16,24},{20,28},{24,0},{28,4},{1,9},{5... | collective-permute-start | bytes 2973704 | tf_op jit(solution)/shard_map/ppermute | solution.py:341
  68.0 25.0 %all-to-all-start = ((s16[4,66,16,128]{3,2,1,0:T(8,128)(2,1)}), s16[4,66,16,128]{3,2,1,0:T(8,128)(2,1)}, u32[]{:S(2)}, u32[]{:S(2)}) async-start(s16[4,66,16,128]{3,2,1,0:T(8,128)(2,1)} %density_to_ky_kz.6), calls=%async_computation | async-start | bytes 2162688 | tf_op jit(solution)/shard_map/all_to_all | solution.py:294
  72.3 24.3 %copy-start.5 = (bf16[16,30976]{1,0:T(8,128)(2,1)S(1)}, bf16[16,30976]{1,0:T(8,128)(2,1)}, u32[]{:S(2)}) copy-start(bf16[16,30976]{1,0:T(8,128)(2,1)} %copy-done.4) | copy-start | bytes 2973700
  74.7 24.9 %collective-permute-start.4 = (bf16[16,30976]{1,0:T(8,128)(2,1)}, bf16[16,30976]{1,0:T(8,128)(2,1)}, u32[]{:S(2)}, u32[]{:S(2)}) collective-permute-start(bf16[16,30976]{1,0:T(8,128)(2,1)} %broadcast_select_fusion.6), channel_id=1, source_target_pairs={{0,4},{4,0},{8,12},{12,8},{16,20},{20,16},{24,28},{28,24},{1,5},{5... | collective-permute-start | bytes 2973704 | tf_op jit(solution)/shard_map/ppermute | solution.py:344
  93.1 18.3 %all-to-all-start.2 = ((s16[4,66,16,128]{3,2,1,0:T(8,128)(2,1)}), s16[4,66,16,128]{3,2,1,0:T(8,128)(2,1)S(1)}, u32[]{:S(2)}, u32[]{:S(2)}) async-start(s16[4,66,16,128]{3,2,1,0:T(8,128)(2,1)} %density_to_ky_kz.8), calls=%async_computation.2 | async-start | bytes 2162688 | tf_op jit(solution)/shard_map/all_to_all | solution.py:294
  99.0 24.9 %collective-permute-start.3 = (bf16[16,30976]{1,0:T(8,128)(2,1)}, bf16[16,30976]{1,0:T(8,128)(2,1)S(1)}, u32[]{:S(2)}, u32[]{:S(2)}) collective-permute-start(bf16[16,30976]{1,0:T(8,128)(2,1)} %broadcast_select_fusion.7), channel_id=1, source_target_pairs={{0,4},{4,0},{8,12},{12,8},{16,20},{20,16},{24,28},{28,24},{1,5},{5... | collective-permute-start | bytes 2973704 | tf_op jit(solution)/shard_map/ppermute | solution.py:344
  111.4 23.9 %copy-start.6 = (s16[4,66,16,128]{3,2,1,0:T(8,128)(2,1)}, s16[4,66,16,128]{3,2,1,0:T(8,128)(2,1)S(1)}, u32[]{:S(2)}) copy-start(s16[4,66,16,128]{3,2,1,0:T(8,128)(2,1)S(1)} %all-to-all-done.2.refs_2_) | copy-start | bytes 3244036
  111.4 23.9 %all-to-all-start.5 = ((s16[4,66,16,128]{3,2,1,0:T(8,128)(2,1)}), s16[4,66,16,128]{3,2,1,0:T(8,128)(2,1)}, u32[]{:S(2)}, u32[]{:S(2)}) async-start(s16[4,66,16,128]{3,2,1,0:T(8,128)(2,1)} %density_to_ky_kz.10), calls=%async_computation.5 | async-start | bytes 2162688 | tf_op jit(solution)/shard_map/all_to_all | solution.py:294
  116.9 27.9 %collective-permute-start.5 = (bf16[16,30976]{1,0:T(8,128)(2,1)}, bf16[16,30976]{1,0:T(8,128)(2,1)}, u32[]{:S(2)}, u32[]{:S(2)}) collective-permute-start(bf16[16,30976]{1,0:T(8,128)(2,1)} %broadcast_select_fusion.5), channel_id=1, source_target_pairs={{0,4},{4,0},{8,12},{12,8},{16,20},{20,16},{24,28},{28,24},{1,5},{5... | collective-permute-start | bytes 2973704 | tf_op jit(solution)/shard_map/ppermute | solution.py:344
  123.9 1.0 copy-start.9
  135.3 19.9 %all-to-all-start.4 = ((s16[4,66,16,128]{3,2,1,0:T(8,128)(2,1)}), s16[4,66,16,128]{3,2,1,0:T(8,128)(2,1)S(1)}, u32[]{:S(2)}, u32[]{:S(2)}) async-start(s16[4,66,16,128]{3,2,1,0:T(8,128)(2,1)} %density_to_ky_kz.9), calls=%async_computation.4 | async-start | bytes 2162688 | tf_op jit(solution)/shard_map/all_to_all | solution.py:294
  155.2 21.2 %copy-start.7 = (s16[4,66,16,128]{3,2,1,0:T(8,128)(2,1)}, s16[4,66,16,128]{3,2,1,0:T(8,128)(2,1)S(1)}, u32[]{:S(2)}) copy-start(s16[4,66,16,128]{3,2,1,0:T(8,128)(2,1)S(1)} %all-to-all-done.4.refs_0_) | copy-start | bytes 3244036
  155.2 21.2 %all-to-all-start.6 = ((s16[4,66,16,128]{3,2,1,0:T(8,128)(2,1)}), s16[4,66,16,128]{3,2,1,0:T(8,128)(2,1)S(1)}, u32[]{:S(2)}, u32[]{:S(2)}) async-start(s16[4,66,16,128]{3,2,1,0:T(8,128)(2,1)} %density_to_ky_kz.11), calls=%async_computation.6 | async-start | bytes 2162688 | tf_op jit(solution)/shard_map/all_to_all | solution.py:294
  176.4 1.0 copy-start.8
  177.4 41.7 %all-to-all-start.3 = ((s16[4,66,48,128]{3,2,1,0:T(8,128)(2,1)}), s16[4,66,48,128]{3,2,1,0:T(8,128)(2,1)S(1)}, u32[]{:S(2)}, u32[]{:S(2)}) async-start(s16[4,66,48,128]{3,2,1,0:T(8,128)(2,1)} %filter_along_x.2), calls=%async_computation.3 | async-start | bytes 6488064 | tf_op jit(solution)/shard_map/all_to_all | solution.py:294
  219.1 1.7 copy-start.1
  220.8 44.3 %all-to-all-start.7 = ((s16[4,66,48,128]{3,2,1,0:T(8,128)(2,1)}), s16[4,66,48,128]{3,2,1,0:T(8,128)(2,1)S(1)}, u32[]{:S(2)}, u32[]{:S(2)}) async-start(s16[4,66,48,128]{3,2,1,0:T(8,128)(2,1)} %filter_along_x.3), calls=%async_computation.7 | async-start | bytes 6488064 | tf_op jit(solution)/shard_map/all_to_all | solution.py:294
  237.5 42.2 %collective-permute-start.6 = (s16[16,30976]{1,0:T(8,128)(2,1)}, s16[16,30976]{1,0:T(8,128)(2,1)}, u32[]{:S(2)}, u32[]{:S(2)}) collective-permute-start(s16[16,30976]{1,0:T(8,128)(2,1)} %get-tuple-element.51), channel_id=1, source_target_pairs={{0,24},{4,28},{8,0},{12,4},{16,8},{20,12},{24,16},{28,20},{1,25},{... | collective-permute-start | bytes 2973704 | tf_op jit(solution)/shard_map/ppermute | solution.py:413
  263.9 60.7 %collective-permute-start.9 = (s16[16,30976]{1,0:T(8,128)(2,1)}, s16[16,30976]{1,0:T(8,128)(2,1)}, u32[]{:S(2)}, u32[]{:S(2)}) collective-permute-start(s16[16,30976]{1,0:T(8,128)(2,1)} %get-tuple-element.59), channel_id=1, source_target_pairs={{0,24},{4,28},{8,0},{12,4},{16,8},{20,12},{24,16},{28,20},{1,25},{... | collective-permute-start | bytes 2973704 | tf_op jit(solution)/shard_map/ppermute | solution.py:413
  264.3 45.9 %collective-permute-start.7 = (s16[16,30976]{1,0:T(8,128)(2,1)}, s16[16,30976]{1,0:T(8,128)(2,1)}, u32[]{:S(2)}, u32[]{:S(2)}) collective-permute-start(s16[16,30976]{1,0:T(8,128)(2,1)} %get-tuple-element.55), channel_id=1, source_target_pairs={{0,24},{4,28},{8,0},{12,4},{16,8},{20,12},{24,16},{28,20},{1,25},{... | collective-permute-start | bytes 2973704 | tf_op jit(solution)/shard_map/ppermute | solution.py:413
  265.0 1.7 copy-start
  279.7 44.9 %collective-permute-start.8 = (s16[16,30976]{1,0:T(8,128)(2,1)}, s16[16,30976]{1,0:T(8,128)(2,1)S(1)}, u32[]{:S(2)}, u32[]{:S(2)}) collective-permute-start(s16[16,30976]{1,0:T(8,128)(2,1)} %get-tuple-element.58), channel_id=1, source_target_pairs={{0,4},{4,0},{8,12},{12,8},{16,20},{20,16},{24,28},{28,24},{1,5},{5... | collective-permute-start | bytes 2973704 | tf_op jit(solution)/shard_map/ppermute | solution.py:400
  293.3 38.1 %copy-start.11 = (s16[16,30976]{1,0:T(8,128)(2,1)S(1)}, s16[16,30976]{1,0:T(8,128)(2,1)}, u32[]{:S(2)}) copy-start(s16[16,30976]{1,0:T(8,128)(2,1)} %get-tuple-element.66) | copy-start | bytes 2973700
  293.3 38.1 %collective-permute-start.11 = (s16[16,30976]{1,0:T(8,128)(2,1)}, s16[16,30976]{1,0:T(8,128)(2,1)S(1)}, u32[]{:S(2)}, u32[]{:S(2)}) collective-permute-start(s16[16,30976]{1,0:T(8,128)(2,1)} %get-tuple-element.66), channel_id=1, source_target_pairs={{0,24},{8,0},{16,8},{24,16},{1,25},{9,1},{17,9},{25,17},{2,26},{10... | collective-permute-start | bytes 2973704 | tf_op jit(solution)/shard_map/ppermute | solution.py:404
  323.2 58.2 %collective-permute-start.10 = (s16[16,30976]{1,0:T(8,128)(2,1)}, s16[16,30976]{1,0:T(8,128)(2,1)S(1)}, u32[]{:S(2)}, u32[]{:S(2)}) collective-permute-start(s16[16,30976]{1,0:T(8,128)(2,1)} %get-tuple-element.62), channel_id=1, source_target_pairs={{0,28},{4,0},{8,4},{12,8},{16,12},{20,16},{24,20},{28,24},{1,29},{... | collective-permute-start | bytes 2973704 | tf_op jit(solution)/shard_map/ppermute | solution.py:406
  324.6 8.0 %collective-permute-start.13 = (s16[16,30976]{1,0:T(8,128)(2,1)S(1)}, s16[16,30976]{1,0:T(8,128)(2,1)S(1)}, u32[]{:S(2)}, u32[]{:S(2)}) collective-permute-start(s16[16,30976]{1,0:T(8,128)(2,1)S(1)} %collective-permute-done.8), channel_id=1, source_target_pairs={{4,28},{12,4},{20,12},{28,20},{5,29},{13,5},{21,13},{29,21},{6,30}... | collective-permute-start | bytes 2973704 | tf_op jit(solution)/shard_map/ppermute | solution.py:402
  332.6 39.6 %collective-permute-start.12 = (s16[16,30976]{1,0:T(8,128)(2,1)}, s16[16,30976]{1,0:T(8,128)(2,1)S(1)}, u32[]{:S(2)}, u32[]{:S(2)}) collective-permute-start(s16[16,30976]{1,0:T(8,128)(2,1)} %broadcast_select_fusion.4), channel_id=1, source_target_pairs={{0,4},{4,0},{8,12},{12,8},{16,20},{20,16},{24,28},{28,24},{1,5},{5... | collective-permute-start | bytes 2973704 | tf_op jit(solution)/shard_map/ppermute | solution.py:405
  372.2 1.0 copy-start.12
  381.4 1.0 copy-start.10

commit v7 on v5

--- a/solution.py
+++ b/solution.py
@@ -211,7 +211,8 @@
         out_ref[:, 2 * half + row] = to_wire(shared_lanes(codes[0], codes[1]))
 
 
-def back_kernel(blocks, block_rows, in_ref, a_ref, b_ref, occ, z_ref, y_ref, own_ref, ret_ref, buf, rows_z, field):
+def back_kernel(blocks, block_rows, adding, in_ref, a_ref, b_ref, occ, z_ref, y_ref, *refs):
+    own_ref, ret_ref, buf, rows_z, field = refs[adding:]
     cells = a_ref.shape[1]
     grid_size = rows_z.shape[0]
     half = in_ref.shape[1] // 3
@@ -264,13 +265,15 @@
         visitor = b_ref[:, lanes].astype(F32)
         own_ref[:, lanes] = potential * visitor * (-0.5 * visitor[CHUNK:])
         terms = potential * a_ref[:, lanes].astype(F32) * home
+        if adding:
+            terms = terms + decoded(from_wire(refs[0][:, lanes])) * occ[1]
         ret_ref[:, lanes] = to_wire(coded(terms))
 
 
-def total_kernel(far_own, near_own, far_arrived, near_arrived, *refs):
+def total_kernel(far_own, near_own, far_arrived, near_arrived, flags, *refs):
     out_ref = refs[-1]
     total = far_own[...] + near_own[...]
-    total = total + decoded(from_wire(far_arrived[...])) + decoded(from_wire(near_arrived[...]))
+    total = total + decoded(from_wire(far_arrived[...])) + decoded(from_wire(near_arrived[...])) * flags[2]
     out_ref[:, 0, :] = total[: out_ref.shape[0]]
 
 
@@ -320,9 +323,6 @@
     occupied = band_occ.astype(BF16)
     upward = [(i, (i + 2) % bands) for i in range(bands)]
     downward = [(i, (i - 2) % bands) for i in range(bands)]
-    odd_downward = [pair for pair in downward if pair[0] % 2 == 1]
-    even_downward = [pair for pair in downward if pair[0] % 2 == 0]
-    downward_one = [(i, (i - 1) % bands) for i in range(bands)]
     swap = [(i, i ^ 1) for i in range(bands)]
     is_odd = lax.axis_index("band") % 2 == 1
 
@@ -336,8 +336,6 @@
     far, near = [], []
     for chunk in range(chunks):
         sent = carrying[chunk]
-        if far:
-            sent, far[-1] = lax.optimization_barrier((sent, far[-1]))
         far.append(lax.ppermute(sent, "band", upward))
     far[0], profile = lax.optimization_barrier((far[0], profile))
     for chunk in range(chunks):
@@ -368,11 +366,11 @@
             [*wires, profile, x_forward, x_back],
         )
 
-    def back(wire, chunk, visitor, factors):
+    def back(wire, chunk, visitor, factors, added=()):
         whole = pl.BlockSpec(memory_space=pltpu.VMEM)
         piece = pl.BlockSpec((blocks, 3 * half, ROWS, 128), lambda i: (0, 0, chunk, 0))
         return call(
-            functools.partial(back_kernel, blocks, block_rows),
+            functools.partial(back_kernel, blocks, block_rows, len(added)),
             [
                 jax.ShapeDtypeStruct((ROWS, cells), F32),
                 jax.ShapeDtypeStruct((ROWS, cells), jnp.int16),
@@ -384,45 +382,41 @@
             ],
             "potential_terms",
             flops,
-            [wire, home[chunk], visitor[chunk], factors, z_table, y_back],
-            [piece, whole, whole, pl.BlockSpec(memory_space=pltpu.SMEM), whole, whole],
+            [wire, home[chunk], visitor[chunk], factors, z_table, y_back, *added],
+            [piece, whole, whole, pl.BlockSpec(memory_space=pltpu.SMEM)] + [whole] * (2 + len(added)),
         )
 
-    factors = occupied.astype(F32)
+    odd = is_odd.astype(F32)
+    factors = flags = jnp.stack([occupied.astype(F32)[0], odd, 1.0 - odd])
 
     far_wires = [exchange(forward(chunk, far)) for chunk in range(chunks)]
     near_wires = [exchange(forward(chunk, near)) for chunk in range(chunks)]
+    near_wire = exchange(filtered(near_wires))
     far_wire = exchange(filtered(far_wires))
-    near_wire = exchange(filtered(near_wires))
-    def returned(chunk, terms):
-        route = chunk % 3
-        if route == 0:
-            crossed = lax.ppermute(terms, "band", swap)
-            return jnp.where(is_odd, lax.ppermute(crossed, "band", odd_downward), crossed)
-        if route == 1:
-            lowered = lax.ppermute(terms, "band", even_downward)
-            return lax.ppermute(jnp.where(is_odd, terms, lowered), "band", swap)
-        return lax.ppermute(terms, "band", downward_one)
-
-    far_parts, near_parts = [], []
-    for wire, visitor, parts in ((far_wire, far, far_parts), (near_wire, near, near_parts)):
-        for chunk in range(chunks):
-            parts.append(back(wire, chunk, visitor, factors))
-            factors, *parts[-1] = lax.optimization_barrier((factors, *parts[-1]))
+    near_own, crossed, far_own, arrived = [], [], [], []
+    for chunk in range(chunks):
+        own, terms = back(near_wire, chunk, near, factors)
+        factors, terms = lax.optimization_barrier((factors, terms))
+        near_own.append(own)
+        crossed.append(lax.ppermute(terms, "band", swap))
+    for chunk in range(chunks):
+        own, terms = back(far_wire, chunk, far, factors, [crossed[chunk]])
+        factors, terms = lax.optimization_barrier((factors, terms))
+        far_own.append(own)
+        arrived.append(lax.ppermute(terms, "band", downward))
     width = 16 * grid_size
     spec = pl.BlockSpec((ROWS, width), lambda i: (0, i))
     result = None
     for chunk in range(chunks):
-        (far_own, far_return), (near_own, near_return) = far_parts[chunk], near_parts[chunk]
-        operands = [far_own, near_own, lax.ppermute(far_return, "band", downward), returned(chunk, near_return)]
+        operands = [far_own[chunk], near_own[chunk], arrived[chunk], crossed[chunk], flags]
         started = [] if result is None else [result]
         result = pl.pallas_call(
             total_kernel,
             grid=(cells // width,),
             out_shape=jax.ShapeDtypeStruct((slab, 1, cells), F32),
-            in_specs=[spec] * 4 + [pl.BlockSpec(memory_space=pl.ANY)] * len(started),
+            in_specs=[spec] * 4 + [pl.BlockSpec(memory_space=pltpu.SMEM)] + [pl.BlockSpec(memory_space=pl.ANY)] * len(started),
             out_specs=pl.BlockSpec((min(CHUNK, slab), 1, width), functools.partial(lambda at, i: (at, 0, i), chunk)),
-            input_output_aliases={4: 0} if started else {},
+            input_output_aliases={5: 0} if started else {},
             compiler_params=pltpu.CompilerParams(vmem_limit_bytes=VMEM_BYTES),
             name="total_terms",
         )(*operands, *started)

time: 437 us -> 369 us (0.84)
  starting transfers between devices: 110 us -> 48.4 us
  waiting for transfers between devices: 91.9 us -> 85.4 us
    ppermute x8 -> x6, starting transfers between devices: 69.6 us -> 8.26 us  [the longest x3 4.5 us: shards(): arrived.append(lax.ppermute(terms, 'band', downward))]
    ppermute x3, waiting for transfers between devices: 24.4 us -> 17.9 us  [shards(): far.append(lax.ppermute(sent, 'band', upward))]
    ppermute x8 -> x6, waiting for transfers between devices: 34.9 us -> 29.5 us  [the longest x3 24.2 us: shards(): arrived.append(lax.ppermute(terms, 'band', downward))]
    ppermute x3, waiting for transfers between devices: 7.76 us -> 13.1 us  [shards(): lax.ppermute(jnp.where(is_odd, far[chunk], carrying[chunk]), 'band', swap)]
    unnamed x24 -> x26, local copies, waits for them, and re-layouts: 9.17 us -> 9.26 us
  transfers between devices with their start and end apart: 22 -> 20, of which waited for: 9 -> 11; matrix products, arithmetic and copies ran while one was open for 5% -> 4% of each run, Pallas kernels for 38% -> 53%
where the time goes in v7:
time: 369 us; the launch traced here: 368 us
  Pallas kernels  203 us (55%)
  waiting for transfers between devices  85.4 us (23%)
  starting transfers between devices  48.4 us (13%)
  other arithmetic  17 us (5%)
  local copies, waits for them, and re-layouts  12.8 us (3%)
    pallas_call x14, Pallas kernels, call(): pl.pallas_call(kernel, grid=(1,) if in_specs else (), out_shape=out_shape...  178 us
    all_to_all x8, starting transfers between devices, exchange(): return lax.all_to_all(wire, 'fft', split_axis=0, concat_axis=0, tiled=True)  30.2 us
    pallas_call x3, Pallas kernels, shards(): pl.pallas_call(total_kernel, grid=(cells // width,), out_shape=jax.ShapeD...  25.1 us
    all_to_all x8, waiting for transfers between devices, exchange(): return lax.all_to_all(wire, 'fft', split_axis=0, concat_axis=0, tiled=True)  24.9 us
    ppermute x3, waiting for transfers between devices, shards(): arrived.append(lax.ppermute(terms, 'band', downward))  24.2 us
    ppermute x3, waiting for transfers between devices, shards(): far.append(lax.ppermute(sent, 'band', upward))  17.9 us
    ppermute x3, waiting for transfers between devices, shards(): lax.ppermute(jnp.where(is_odd, far[chunk], carrying[chunk]), 'band', swap)  13.1 us
    unnamed x26, local copies, waits for them, and re-layouts  9.26 us
  transfers between devices with their start and end apart: 20, of which 11 were waited for; matrix products, arithmetic and copies ran while one was open for 4% of the time, Pallas kernels for 53%

profile of v7, /device:TPU:0, one launch (start us, length us, event | category | flops | bytes accessed | tf_op | source)
XLA Modules:
  0.0 367.7 jit_solution(3414828450457568207)
XLA Ops:
  0.0 1.6 slice_bitcast_fusion
  1.6 1.9 slice_bitcast_fusion.1
  4.2 2.8 broadcast_select_fusion
  7.0 3.0 collective-permute-start
  10.1 1.6 collective-permute-start.1
  11.6 1.6 collective-permute-start.2
  13.3 6.2 %fusion.5.refs_3_ = f32[44,96,256]{2,1,0:T(8,128)} fusion(f32[256]{0:T(256)S(1)} %fusion.22, f32[44,96]{1,0:T(8,128)S(1)} %broadcast_add_fusion), kind=kLoop, calls=%fused_computation.9 | loop fusion | flops 29196288 | bytes 4343296 | tf_op jit(solution)/shard_map/mul | solution.py:79
  19.5 15.5 %collective-permute-done.b_ref = bf16[16,30976]{1,0:T(8,128)(2,1)S(1)} collective-permute-done((bf16[16,30976]{1,0:T(8,128)(2,1)}, bf16[16,30976]{1,0:T(8,128)(2,1)S(1)}, u32[]{:S(2)}, u32[]{:S(2)}) %collective-permute-start) | collective-permute-done | bytes 991264 | tf_op jit(solution)/shard_map/ppermute | solution.py:339
  35.1 1.0 copy-done.4
  36.0 10.4 %density_to_ky_kz.6 = s16[4,66,16,128]{3,2,1,0:T(8,128)(2,1)} custom-call(bf16[16,30976]{1,0:T(8,128)(2,1)} %get-tuple-element.65.a_ref, bf16[16,30976]{1,0:T(8,128)(2,1)} %copy-done.4, bf16[768,256]{1,0:T(8,128)(2,1)} %constant.68.clone.z_ref, bf16[192,528]{1,0:T(8,128)(2,1)} %constant.69.clone.y_ref), custom_call_target="tpu_custom_call" | custom-call | flops 1046740992 | bytes 2578432 | tf_op jit(solution)/shard_map/density_to_ky_kz/pallas_call | solution.py:283
  46.4 3.5 all-to-all-start
  49.9 2.3 broadcast_select_fusion.5
  52.2 1.8 collective-permute-start.3
  53.9 2.4 collective-permute-done.1.b_ref
  56.3 1.0 copy-done.3
  57.3 10.3 %density_to_ky_kz.7 = s16[4,66,16,128]{3,2,1,0:T(8,128)(2,1)} custom-call(bf16[16,30976]{1,0:T(8,128)(2,1)} %get-tuple-element.63.a_ref, bf16[16,30976]{1,0:T(8,128)(2,1)} %copy-done.3, bf16[768,256]{1,0:T(8,128)(2,1)} %constant.68.clone.z_ref, bf16[192,528]{1,0:T(8,128)(2,1)} %constant.69.clone.y_ref), custom_call_target="tpu_custom_call" | custom-call | flops 1046740992 | bytes 2578432 | tf_op jit(solution)/shard_map/density_to_ky_kz/pallas_call | solution.py:283
  67.6 4.2 %all-to-all-start.1 = ((s16[4,66,16,128]{3,2,1,0:T(8,128)(2,1)}), s16[4,66,16,128]{3,2,1,0:T(8,128)(2,1)}, u32[]{:S(2)}, u32[]{:S(2)}) async-start(s16[4,66,16,128]{3,2,1,0:T(8,128)(2,1)} %density_to_ky_kz.7), calls=%async_computation.1 | async-start | bytes 2162688 | tf_op jit(solution)/shard_map/all_to_all | solution.py:297
  71.9 2.3 broadcast_select_fusion.4
  74.2 1.8 collective-permute-start.4
  76.0 0.8 collective-permute-done.3.b_ref
  76.8 10.4 %density_to_ky_kz.9 = s16[4,66,16,128]{3,2,1,0:T(8,128)(2,1)} custom-call(bf16[16,30976]{1,0:T(8,128)(2,1)} %get-tuple-element.65.a_ref, bf16[16,30976]{1,0:T(8,128)(2,1)} %collective-permute-done.3.b_ref, bf16[768,256]{1,0:T(8,128)(2,1)} %constant.68.clone.z_ref, bf16[192,528]{1,0:T(8,128)(2,1)} %constant.69.clone.y_ref), custom_call_target="tpu_custom_call" | custom-call | flops 1046740992 | bytes 2578432 | tf_op jit(solution)/shard_map/density_to_ky_kz/pallas_call | solution.py:283
  87.2 3.5 all-to-all-start.4
  90.7 2.6 broadcast_select_fusion.3
  93.4 0.3 collective-permute-start.5
  93.7 5.6 %collective-permute-done.4.b_ref = bf16[16,30976]{1,0:T(8,128)(2,1)} collective-permute-done((bf16[16,30976]{1,0:T(8,128)(2,1)}, bf16[16,30976]{1,0:T(8,128)(2,1)}, u32[]{:S(2)}, u32[]{:S(2)}) %collective-permute-start.4) | collective-permute-done | bytes 991264 | tf_op jit(solution)/shard_map/ppermute | solution.py:342
  99.2 10.4 %density_to_ky_kz.10 = s16[4,66,16,128]{3,2,1,0:T(8,128)(2,1)} custom-call(bf16[16,30976]{1,0:T(8,128)(2,1)} %get-tuple-element.63.a_ref, bf16[16,30976]{1,0:T(8,128)(2,1)} %collective-permute-done.4.b_ref, bf16[768,256]{1,0:T(8,128)(2,1)} %constant.68.clone.z_ref, bf16[192,528]{1,0:T(8,128)(2,1)} %constant.69.clone.y_ref), custom_call_target="tpu_custom_call" | custom-call | flops 1046740992 | bytes 2578432 | tf_op jit(solution)/shard_map/density_to_ky_kz/pallas_call | solution.py:283
  109.7 3.7 %all-to-all-start.5 = ((s16[4,66,16,128]{3,2,1,0:T(8,128)(2,1)}), s16[4,66,16,128]{3,2,1,0:T(8,128)(2,1)S(1)}, u32[]{:S(2)}, u32[]{:S(2)}) async-start(s16[4,66,16,128]{3,2,1,0:T(8,128)(2,1)} %density_to_ky_kz.10), calls=%async_computation.5 | async-start | bytes 2162688 | tf_op jit(solution)/shard_map/all_to_all | solution.py:297
  113.4 6.7 %collective-permute-done.5.b_ref = bf16[16,30976]{1,0:T(8,128)(2,1)} collective-permute-done((bf16[16,30976]{1,0:T(8,128)(2,1)}, bf16[16,30976]{1,0:T(8,128)(2,1)}, u32[]{:S(2)}, u32[]{:S(2)}) %collective-permute-start.5) | collective-permute-done | bytes 991264 | tf_op jit(solution)/shard_map/ppermute | solution.py:342
  120.1 10.3 %density_to_ky_kz.11 = s16[4,66,16,128]{3,2,1,0:T(8,128)(2,1)} custom-call(bf16[16,30976]{1,0:T(8,128)(2,1)} %get-tuple-element.58.a_ref, bf16[16,30976]{1,0:T(8,128)(2,1)} %collective-permute-done.5.b_ref, bf16[768,256]{1,0:T(8,128)(2,1)} %constant.68.clone.z_ref, bf16[192,528]{1,0:T(8,128)(2,1)} %constant.69.clone.y_ref), custom_call_target="tpu_custom_call" | custom-call | flops 1046740992 | bytes 2578432 | tf_op jit(solution)/shard_map/density_to_ky_kz/pallas_call | solution.py:283
  130.4 4.2 %all-to-all-start.6 = ((s16[4,66,16,128]{3,2,1,0:T(8,128)(2,1)}), s16[4,66,16,128]{3,2,1,0:T(8,128)(2,1)}, u32[]{:S(2)}, u32[]{:S(2)}) async-start(s16[4,66,16,128]{3,2,1,0:T(8,128)(2,1)} %density_to_ky_kz.11), calls=%async_computation.6 | async-start | bytes 2162688 | tf_op jit(solution)/shard_map/all_to_all | solution.py:297
  134.7 10.3 %density_to_ky_kz.8 = s16[4,66,16,128]{3,2,1,0:T(8,128)(2,1)} custom-call(bf16[16,30976]{1,0:T(8,128)(2,1)} %get-tuple-element.58.a_ref, bf16[16,30976]{1,0:T(8,128)(2,1)} %copy-done.2, bf16[768,256]{1,0:T(8,128)(2,1)} %constant.68.clone.z_ref, bf16[192,528]{1,0:T(8,128)(2,1)} %constant.69.clone.y_ref), custom_call_target="tpu_custom_call" | custom-call | flops 1046740992 | bytes 2578432 | tf_op jit(solution)/shard_map/density_to_ky_kz/pallas_call | solution.py:283
  145.0 4.5 %all-to-all-done.6.refs_2_ = s16[4,66,16,128]{3,2,1,0:T(8,128)(2,1)} async-done(((s16[4,66,16,128]{3,2,1,0:T(8,128)(2,1)}), s16[4,66,16,128]{3,2,1,0:T(8,128)(2,1)}, u32[]{:S(2)}, u32[]{:S(2)}) %all-to-all-start.6) | async-done | bytes 1081376 | tf_op jit(solution)/shard_map/all_to_all | solution.py:297
  149.5 3.5 all-to-all-start.2
  153.1 17.6 %filter_along_x.3 = s16[4,66,48,128]{3,2,1,0:T(8,128)(2,1)} custom-call(s16[4,66,16,128]{3,2,1,0:T(8,128)(2,1)} %copy-done.6, s16[4,66,16,128]{3,2,1,0:T(8,128)(2,1)} %copy-done.7, s16[4,66,16,128]{3,2,1,0:T(8,128)(2,1)} %all-to-all-done.6.refs_2_, f32[44,96,256]{2,1,0:T(8,128)} %fusion.5.refs_3_, bf16[176,576]{1,0:T(8,128)(2,1)} %constant.71.clone.refs_4_, ...), custom_call_target="tpu_custom_call" | custom-call | flops 3140222976 | bytes 7974912 | tf_op jit(solution)/shard_map/filter_along_x/pallas_call | solution.py:283
  170.7 1.0 copy-done.8
  171.7 3.7 %all-to-all-start.7 = ((s16[4,66,48,128]{3,2,1,0:T(8,128)(2,1)}), s16[4,66,48,128]{3,2,1,0:T(8,128)(2,1)S(1)}, u32[]{:S(2)}, u32[]{:S(2)}) async-start(s16[4,66,48,128]{3,2,1,0:T(8,128)(2,1)} %filter_along_x.3), calls=%async_computation.7 | async-start | bytes 6488064 | tf_op jit(solution)/shard_map/all_to_all | solution.py:297
  175.5 17.6 %filter_along_x.2 = s16[4,66,48,128]{3,2,1,0:T(8,128)(2,1)} custom-call(s16[4,66,16,128]{3,2,1,0:T(8,128)(2,1)} %copy-done.5, s16[4,66,16,128]{3,2,1,0:T(8,128)(2,1)} %all-to-all-done.1.refs_1_, s16[4,66,16,128]{3,2,1,0:T(8,128)(2,1)} %copy-done.8, f32[44,96,256]{2,1,0:T(8,128)} %fusion.5.refs_3_, bf16[176,576]{1,0:T(8,128)(2,1)} %constant.71.clone.refs_4_, ...), custom_call_target="tpu_custom_call" | custom-call | flops 3140222976 | bytes 7974912 | tf_op jit(solution)/shard_map/filter_along_x/pallas_call | solution.py:283
  193.1 20.3 %all-to-all-done.7.in_ref = s16[4,66,48,128]{3,2,1,0:T(8,128)(2,1)S(1)} async-done(((s16[4,66,48,128]{3,2,1,0:T(8,128)(2,1)}), s16[4,66,48,128]{3,2,1,0:T(8,128)(2,1)S(1)}, u32[]{:S(2)}, u32[]{:S(2)}) %all-to-all-start.7) | async-done | bytes 3244064 | tf_op jit(solution)/shard_map/all_to_all | solution.py:297
  213.4 1.7 copy-done.1
  215.1 3.7 %all-to-all-start.3 = ((s16[4,66,48,128]{3,2,1,0:T(8,128)(2,1)}), s16[4,66,48,128]{3,2,1,0:T(8,128)(2,1)S(1)}, u32[]{:S(2)}, u32[]{:S(2)}) async-start(s16[4,66,48,128]{3,2,1,0:T(8,128)(2,1)} %filter_along_x.2), calls=%async_computation.3 | async-start | bytes 6488064 | tf_op jit(solution)/shard_map/all_to_all | solution.py:297
  218.8 0.6 pad_maximum_fusion.occ.flags
  219.4 13.0 %potential_terms.6 = (f32[16,30976]{1,0:T(8,128)}, s16[16,30976]{1,0:T(8,128)(2,1)}) custom-call(s16[4,66,48,128]{3,2,1,0:T(8,128)(2,1)} %copy-done.1, bf16[16,30976]{1,0:T(8,128)(2,1)} %get-tuple-element.65.a_ref, bf16[16,30976]{1,0:T(8,128)(2,1)} %collective-permute-done.3.b_ref, f32[3]{0:T(128)} %pad_maximum_fusion.occ.flags, ...), custom_call_target="tpu_custom_call" | custom-call | flops 1046740992 | bytes 5822476 | tf_op jit(solution)/shard_map/potential_terms/pallas_call | solution.py:283
  232.4 1.7 collective-permute-start.6
  234.2 13.0 %potential_terms.7 = (f32[16,30976]{1,0:T(8,128)}, s16[16,30976]{1,0:T(8,128)(2,1)}) custom-call(s16[4,66,48,128]{3,2,1,0:T(8,128)(2,1)} %copy-done.1, bf16[16,30976]{1,0:T(8,128)(2,1)} %get-tuple-element.63.a_ref, bf16[16,30976]{1,0:T(8,128)(2,1)} %collective-permute-done.4.b_ref, f32[3]{0:T(128)} %pad_maximum_fusion.occ.flags, ...), custom_call_target="tpu_custom_call" | custom-call | flops 1046740992 | bytes 5822476 | tf_op jit(solution)/shard_map/potential_terms/pallas_call | solution.py:283
  247.2 0.3 collective-permute-start.7
  247.5 13.0 %potential_terms.8 = (f32[16,30976]{1,0:T(8,128)}, s16[16,30976]{1,0:T(8,128)(2,1)}) custom-call(s16[4,66,48,128]{3,2,1,0:T(8,128)(2,1)} %copy-done.1, bf16[16,30976]{1,0:T(8,128)(2,1)} %get-tuple-element.58.a_ref, bf16[16,30976]{1,0:T(8,128)(2,1)} %collective-permute-done.5.b_ref, f32[3]{0:T(128)} %pad_maximum_fusion.occ.flags, ...), custom_call_target="tpu_custom_call" | custom-call | flops 1046740992 | bytes 5822476 | tf_op jit(solution)/shard_map/potential_terms/pallas_call | solution.py:283
  260.5 1.7 collective-permute-start.8
  262.3 1.7 copy-done
  264.0 13.9 %potential_terms.9 = (f32[16,30976]{1,0:T(8,128)}, s16[16,30976]{1,0:T(8,128)(2,1)}) custom-call(s16[4,66,48,128]{3,2,1,0:T(8,128)(2,1)} %copy-done, bf16[16,30976]{1,0:T(8,128)(2,1)} %get-tuple-element.65.a_ref, bf16[16,30976]{1,0:T(8,128)(2,1)} %copy-done.4, f32[3]{0:T(128)} %pad_maximum_fusion.occ.flags, bf16[768,256]{1,0:T(8,128)(2,1)} %constant.68.clone.z_ref, ...), custom_call_target="tpu_custom_call" | custom-call | flops 1046740992 | bytes 6813708 | tf_op jit(solution)/shard_map/potential_terms/pallas_call | solution.py:283
  277.9 0.8 collective-permute-done.7.refs_0_.near_arrived
  278.7 13.9 %potential_terms.10 = (f32[16,30976]{1,0:T(8,128)}, s16[16,30976]{1,0:T(8,128)(2,1)}) custom-call(s16[4,66,48,128]{3,2,1,0:T(8,128)(2,1)} %copy-done, bf16[16,30976]{1,0:T(8,128)(2,1)} %get-tuple-element.63.a_ref, bf16[16,30976]{1,0:T(8,128)(2,1)} %copy-done.3, f32[3]{0:T(128)} %pad_maximum_fusion.occ.flags, bf16[768,256]{1,0:T(8,128)(2,1)} %constant.68.clone.z_ref, ...), custom_call_target="tpu_custom_call" | custom-call | flops 1046740992 | bytes 6813708 | tf_op jit(solution)/shard_map/potential_terms/pallas_call | solution.py:283
  292.6 2.0 collective-permute-start.10
  294.6 0.5 collective-permute-start.11
  295.1 4.4 %collective-permute-done.8.refs_0_.near_arrived = s16[16,30976]{1,0:T(8,128)(2,1)} collective-permute-done((s16[16,30976]{1,0:T(8,128)(2,1)}, s16[16,30976]{1,0:T(8,128)(2,1)}, u32[]{:S(2)}, u32[]{:S(2)}) %collective-permute-start.8) | collective-permute-done | bytes 991264 | tf_op jit(solution)/shard_map/ppermute | solution.py:401
  299.5 13.9 %potential_terms.11 = (f32[16,30976]{1,0:T(8,128)}, s16[16,30976]{1,0:T(8,128)(2,1)}) custom-call(s16[4,66,48,128]{3,2,1,0:T(8,128)(2,1)} %copy-done, bf16[16,30976]{1,0:T(8,128)(2,1)} %get-tuple-element.58.a_ref, bf16[16,30976]{1,0:T(8,128)(2,1)} %copy-done.2, f32[3]{0:T(128)} %pad_maximum_fusion.occ.flags, bf16[768,256]{1,0:T(8,128)(2,1)} %constant.68.clone.z_ref, ...), custom_call_target="tpu_custom_call" | custom-call | flops 1046740992 | bytes 6813708 | tf_op jit(solution)/shard_map/potential_terms/pallas_call | solution.py:283
  313.5 2.0 collective-permute-start.9
  315.5 23.5 %collective-permute-done.11.far_arrived = s16[16,30976]{1,0:T(8,128)(2,1)S(1)} collective-permute-done((s16[16,30976]{1,0:T(8,128)(2,1)S(1)}, s16[16,30976]{1,0:T(8,128)(2,1)S(1)}, u32[]{:S(2)}, u32[]{:S(2)}) %collective-permute-start.11) | collective-permute-done | bytes 991264 | tf_op jit(solution)/shard_map/ppermute | solution.py:406
  338.9 1.0 copy-done.11
  339.9 8.4 %total_terms.3.refs_0_ = f32[44,1,30976]{2,1,0:T(1,128)} custom-call(f32[16,30976]{1,0:T(8,128)} %get-tuple-element.52.far_own, f32[16,30976]{1,0:T(8,128)} %get-tuple-element.53.near_own, s16[16,30976]{1,0:T(8,128)(2,1)} %copy-done.11, s16[16,30976]{1,0:T(8,128)(2,1)} %collective-permute-done.6.refs_0_.near_arrived, f32[3]{0:T(128)} %pad_maximum_fusion.occ.flags), custom_call_target="tpu_custom_call" | custom-call | tf_op jit(solution)/shard_map/total_terms/pallas_call | solution.py:413
  348.3 1.0 copy-done.9
  349.2 8.4 %total_terms.4.refs_0_ = f32[44,1,30976]{2,1,0:T(1,128)} custom-call(f32[16,30976]{1,0:T(8,128)} %get-tuple-element.49.far_own, f32[16,30976]{1,0:T(8,128)} %get-tuple-element.50.near_own, s16[16,30976]{1,0:T(8,128)(2,1)} %copy-done.9, s16[16,30976]{1,0:T(8,128)(2,1)} %collective-permute-done.7.refs_0_.near_arrived, ...), custom_call_target="tpu_custom_call", output_to_operand_aliasing={{}: (5, {})} | custom-call | tf_op jit(solution)/shard_map/total_terms/pallas_call | solution.py:413
  357.6 0.8 collective-permute-done.9.far_arrived
  358.4 1.0 copy-done.10
  359.3 8.3 %total_terms.5 = f32[44,1,30976]{2,1,0:T(1,128)} custom-call(f32[16,30976]{1,0:T(8,128)} %get-tuple-element.45.far_own, f32[16,30976]{1,0:T(8,128)} %get-tuple-element.46.near_own, s16[16,30976]{1,0:T(8,128)(2,1)} %copy-done.10, s16[16,30976]{1,0:T(8,128)(2,1)} %collective-permute-done.8.refs_0_.near_arrived, ...), custom_call_target="tpu_custom_call", output_to_operand_aliasing={{}: (5, {})} | custom-call | tf_op jit(solution)/shard_map/total_terms/pallas_call | solution.py:413
  (32 shorter events, 0.2 us)
Async XLA Ops:
  7.0 28.0 %collective-permute-start = (bf16[16,30976]{1,0:T(8,128)(2,1)}, bf16[16,30976]{1,0:T(8,128)(2,1)S(1)}, u32[]{:S(2)}, u32[]{:S(2)}) collective-permute-start(bf16[16,30976]{1,0:T(8,128)(2,1)} %get-tuple-element.66), channel_id=1, source_target_pairs={{0,8},{4,12},{8,16},{12,20},{16,24},{20,28},{24,0},{28,4},{1,9},{5... | collective-permute-start | bytes 2973704 | tf_op jit(solution)/shard_map/ppermute | solution.py:339
  10.1 46.2 %collective-permute-start.1 = (bf16[16,30976]{1,0:T(8,128)(2,1)}, bf16[16,30976]{1,0:T(8,128)(2,1)S(1)}, u32[]{:S(2)}, u32[]{:S(2)}) collective-permute-start(bf16[16,30976]{1,0:T(8,128)(2,1)} %get-tuple-element.64), channel_id=1, source_target_pairs={{0,8},{4,12},{8,16},{12,20},{16,24},{20,28},{24,0},{28,4},{1,9},{5... | collective-permute-start | bytes 2973704 | tf_op jit(solution)/shard_map/ppermute | solution.py:339
  11.6 79.1 %collective-permute-start.2 = (bf16[16,30976]{1,0:T(8,128)(2,1)}, bf16[16,30976]{1,0:T(8,128)(2,1)S(1)}, u32[]{:S(2)}, u32[]{:S(2)}) collective-permute-start(bf16[16,30976]{1,0:T(8,128)(2,1)} %get-tuple-element.57), channel_id=1, source_target_pairs={{0,8},{4,12},{8,16},{12,20},{16,24},{20,28},{24,0},{28,4},{1,9},{5... | collective-permute-start | bytes 2973704 | tf_op jit(solution)/shard_map/ppermute | solution.py:339
  35.1 1.0 copy-start.4
  46.4 21.3 %all-to-all-start = ((s16[4,66,16,128]{3,2,1,0:T(8,128)(2,1)}), s16[4,66,16,128]{3,2,1,0:T(8,128)(2,1)S(1)}, u32[]{:S(2)}, u32[]{:S(2)}) async-start(s16[4,66,16,128]{3,2,1,0:T(8,128)(2,1)} %density_to_ky_kz.6), calls=%async_computation | async-start | bytes 2162688 | tf_op jit(solution)/shard_map/all_to_all | solution.py:297
  52.2 24.6 %collective-permute-start.3 = (bf16[16,30976]{1,0:T(8,128)(2,1)}, bf16[16,30976]{1,0:T(8,128)(2,1)}, u32[]{:S(2)}, u32[]{:S(2)}) collective-permute-start(bf16[16,30976]{1,0:T(8,128)(2,1)} %broadcast_select_fusion.5), channel_id=1, source_target_pairs={{0,4},{4,0},{8,12},{12,8},{16,20},{20,16},{24,28},{28,24},{1,5},{5... | collective-permute-start | bytes 2973704 | tf_op jit(solution)/shard_map/ppermute | solution.py:342
  56.3 1.0 copy-start.3
  67.6 19.5 %copy-start.5 = (s16[4,66,16,128]{3,2,1,0:T(8,128)(2,1)}, s16[4,66,16,128]{3,2,1,0:T(8,128)(2,1)S(1)}, u32[]{:S(2)}) copy-start(s16[4,66,16,128]{3,2,1,0:T(8,128)(2,1)S(1)} %all-to-all-done.refs_0_) | copy-start | bytes 3244036
  67.6 19.5 %all-to-all-start.1 = ((s16[4,66,16,128]{3,2,1,0:T(8,128)(2,1)}), s16[4,66,16,128]{3,2,1,0:T(8,128)(2,1)}, u32[]{:S(2)}, u32[]{:S(2)}) async-start(s16[4,66,16,128]{3,2,1,0:T(8,128)(2,1)} %density_to_ky_kz.7), calls=%async_computation.1 | async-start | bytes 2162688 | tf_op jit(solution)/shard_map/all_to_all | solution.py:297
  74.2 25.0 %collective-permute-start.4 = (bf16[16,30976]{1,0:T(8,128)(2,1)}, bf16[16,30976]{1,0:T(8,128)(2,1)}, u32[]{:S(2)}, u32[]{:S(2)}) collective-permute-start(bf16[16,30976]{1,0:T(8,128)(2,1)} %broadcast_select_fusion.4), channel_id=1, source_target_pairs={{0,4},{4,0},{8,12},{12,8},{16,20},{20,16},{24,28},{28,24},{1,5},{5... | collective-permute-start | bytes 2973704 | tf_op jit(solution)/shard_map/ppermute | solution.py:342
  87.2 22.5 %all-to-all-start.4 = ((s16[4,66,16,128]{3,2,1,0:T(8,128)(2,1)}), s16[4,66,16,128]{3,2,1,0:T(8,128)(2,1)S(1)}, u32[]{:S(2)}, u32[]{:S(2)}) async-start(s16[4,66,16,128]{3,2,1,0:T(8,128)(2,1)} %density_to_ky_kz.9), calls=%async_computation.4 | async-start | bytes 2162688 | tf_op jit(solution)/shard_map/all_to_all | solution.py:297
  90.7 19.0 %copy-start.2 = (bf16[16,30976]{1,0:T(8,128)(2,1)}, bf16[16,30976]{1,0:T(8,128)(2,1)S(1)}, u32[]{:S(2)}) copy-start(bf16[16,30976]{1,0:T(8,128)(2,1)S(1)} %collective-permute-done.2.b_ref) | copy-start | bytes 2973700
  93.4 26.7 %collective-permute-start.5 = (bf16[16,30976]{1,0:T(8,128)(2,1)}, bf16[16,30976]{1,0:T(8,128)(2,1)}, u32[]{:S(2)}, u32[]{:S(2)}) collective-permute-start(bf16[16,30976]{1,0:T(8,128)(2,1)} %broadcast_select_fusion.3), channel_id=1, source_target_pairs={{0,4},{4,0},{8,12},{12,8},{16,20},{20,16},{24,28},{28,24},{1,5},{5... | collective-permute-start | bytes 2973704 | tf_op jit(solution)/shard_map/ppermute | solution.py:342
  109.7 35.3 %copy-start.6 = (s16[4,66,16,128]{3,2,1,0:T(8,128)(2,1)}, s16[4,66,16,128]{3,2,1,0:T(8,128)(2,1)S(1)}, u32[]{:S(2)}) copy-start(s16[4,66,16,128]{3,2,1,0:T(8,128)(2,1)S(1)} %all-to-all-done.4.refs_0_) | copy-start | bytes 3244036
  109.7 20.7 %all-to-all-start.5 = ((s16[4,66,16,128]{3,2,1,0:T(8,128)(2,1)}), s16[4,66,16,128]{3,2,1,0:T(8,128)(2,1)S(1)}, u32[]{:S(2)}, u32[]{:S(2)}) async-start(s16[4,66,16,128]{3,2,1,0:T(8,128)(2,1)} %density_to_ky_kz.10), calls=%async_computation.5 | async-start | bytes 2162688 | tf_op jit(solution)/shard_map/all_to_all | solution.py:297
  130.4 22.7 %copy-start.7 = (s16[4,66,16,128]{3,2,1,0:T(8,128)(2,1)}, s16[4,66,16,128]{3,2,1,0:T(8,128)(2,1)S(1)}, u32[]{:S(2)}) copy-start(s16[4,66,16,128]{3,2,1,0:T(8,128)(2,1)S(1)} %all-to-all-done.5.refs_1_) | copy-start | bytes 3244036
  130.4 19.1 %all-to-all-start.6 = ((s16[4,66,16,128]{3,2,1,0:T(8,128)(2,1)}), s16[4,66,16,128]{3,2,1,0:T(8,128)(2,1)}, u32[]{:S(2)}, u32[]{:S(2)}) async-start(s16[4,66,16,128]{3,2,1,0:T(8,128)(2,1)} %density_to_ky_kz.11), calls=%async_computation.6 | async-start | bytes 2162688 | tf_op jit(solution)/shard_map/all_to_all | solution.py:297
  149.5 21.2 %all-to-all-start.2 = ((s16[4,66,16,128]{3,2,1,0:T(8,128)(2,1)}), s16[4,66,16,128]{3,2,1,0:T(8,128)(2,1)S(1)}, u32[]{:S(2)}, u32[]{:S(2)}) async-start(s16[4,66,16,128]{3,2,1,0:T(8,128)(2,1)} %density_to_ky_kz.8), calls=%async_computation.2 | async-start | bytes 2162688 | tf_op jit(solution)/shard_map/all_to_all | solution.py:297
  170.7 1.0 copy-start.8
  171.7 41.7 %all-to-all-start.7 = ((s16[4,66,48,128]{3,2,1,0:T(8,128)(2,1)}), s16[4,66,48,128]{3,2,1,0:T(8,128)(2,1)S(1)}, u32[]{:S(2)}, u32[]{:S(2)}) async-start(s16[4,66,48,128]{3,2,1,0:T(8,128)(2,1)} %filter_along_x.3), calls=%async_computation.7 | async-start | bytes 6488064 | tf_op jit(solution)/shard_map/all_to_all | solution.py:297
  213.4 1.7 copy-start.1
  215.1 47.2 %all-to-all-start.3 = ((s16[4,66,48,128]{3,2,1,0:T(8,128)(2,1)}), s16[4,66,48,128]{3,2,1,0:T(8,128)(2,1)S(1)}, u32[]{:S(2)}, u32[]{:S(2)}) async-start(s16[4,66,48,128]{3,2,1,0:T(8,128)(2,1)} %filter_along_x.2), calls=%async_computation.3 | async-start | bytes 6488064 | tf_op jit(solution)/shard_map/all_to_all | solution.py:297
  232.4 29.8 %collective-permute-start.6 = (s16[16,30976]{1,0:T(8,128)(2,1)}, s16[16,30976]{1,0:T(8,128)(2,1)}, u32[]{:S(2)}, u32[]{:S(2)}) collective-permute-start(s16[16,30976]{1,0:T(8,128)(2,1)} %get-tuple-element.38), channel_id=1, source_target_pairs={{0,4},{4,0},{8,12},{12,8},{16,20},{20,16},{24,28},{28,24},{1,5},{5... | collective-permute-start | bytes 2973704 | tf_op jit(solution)/shard_map/ppermute | solution.py:401
  247.2 31.5 %collective-permute-start.7 = (s16[16,30976]{1,0:T(8,128)(2,1)}, s16[16,30976]{1,0:T(8,128)(2,1)}, u32[]{:S(2)}, u32[]{:S(2)}) collective-permute-start(s16[16,30976]{1,0:T(8,128)(2,1)} %get-tuple-element.41), channel_id=1, source_target_pairs={{0,4},{4,0},{8,12},{12,8},{16,20},{20,16},{24,28},{28,24},{1,5},{5... | collective-permute-start | bytes 2973704 | tf_op jit(solution)/shard_map/ppermute | solution.py:401
  260.5 39.0 %collective-permute-start.8 = (s16[16,30976]{1,0:T(8,128)(2,1)}, s16[16,30976]{1,0:T(8,128)(2,1)}, u32[]{:S(2)}, u32[]{:S(2)}) collective-permute-start(s16[16,30976]{1,0:T(8,128)(2,1)} %get-tuple-element.44), channel_id=1, source_target_pairs={{0,4},{4,0},{8,12},{12,8},{16,20},{20,16},{24,28},{28,24},{1,5},{5... | collective-permute-start | bytes 2973704 | tf_op jit(solution)/shard_map/ppermute | solution.py:401
  262.3 1.7 copy-start
  277.9 16.7 %copy-start.12 = (s16[16,30976]{1,0:T(8,128)(2,1)S(1)}, s16[16,30976]{1,0:T(8,128)(2,1)}, u32[]{:S(2)}) copy-start(s16[16,30976]{1,0:T(8,128)(2,1)} %get-tuple-element.54) | copy-start | bytes 2973700
  292.6 55.7 %collective-permute-start.10 = (s16[16,30976]{1,0:T(8,128)(2,1)}, s16[16,30976]{1,0:T(8,128)(2,1)S(1)}, u32[]{:S(2)}, u32[]{:S(2)}) collective-permute-start(s16[16,30976]{1,0:T(8,128)(2,1)} %get-tuple-element.51), channel_id=1, source_target_pairs={{0,24},{4,28},{8,0},{12,4},{16,8},{20,12},{24,16},{28,20},{1,25},{... | collective-permute-start | bytes 2973704 | tf_op jit(solution)/shard_map/ppermute | solution.py:406
  294.6 44.3 %collective-permute-start.11 = (s16[16,30976]{1,0:T(8,128)(2,1)S(1)}, s16[16,30976]{1,0:T(8,128)(2,1)S(1)}, u32[]{:S(2)}, u32[]{:S(2)}) collective-permute-start(s16[16,30976]{1,0:T(8,128)(2,1)S(1)} %copy-done.12), channel_id=1, source_target_pairs={{0,24},{4,28},{8,0},{12,4},{16,8},{20,12},{24,16},{28,20},{1,25},{... | collective-permute-start | bytes 2973704 | tf_op jit(solution)/shard_map/ppermute | solution.py:406
  313.5 44.9 %collective-permute-start.9 = (s16[16,30976]{1,0:T(8,128)(2,1)}, s16[16,30976]{1,0:T(8,128)(2,1)S(1)}, u32[]{:S(2)}, u32[]{:S(2)}) collective-permute-start(s16[16,30976]{1,0:T(8,128)(2,1)} %get-tuple-element.48), channel_id=1, source_target_pairs={{0,24},{4,28},{8,0},{12,4},{16,8},{20,12},{24,16},{28,20},{1,25},{... | collective-permute-start | bytes 2973704 | tf_op jit(solution)/shard_map/ppermute | solution.py:406
  338.9 1.0 copy-start.11
  348.3 1.0 copy-start.9
  358.4 1.0 copy-start.10

commit v8 on v7

--- a/solution.py
+++ b/solution.py
@@ -400,6 +400,8 @@
         near_own.append(own)
         crossed.append(lax.ppermute(terms, "band", swap))
     for chunk in range(chunks):
+        if chunk >= 2:
+            factors, arrived[chunk - 2] = lax.optimization_barrier((factors, arrived[chunk - 2]))
         own, terms = back(far_wire, chunk, far, factors, [crossed[chunk]])
         factors, terms = lax.optimization_barrier((factors, terms))
         far_own.append(own)

time: 369 us -> 355 us (0.962)
  waiting for transfers between devices: 85.4 us -> 70.1 us
    ppermute x3, waiting for transfers between devices: 24.2 us -> 3.92 us  [shards(): arrived.append(lax.ppermute(terms, 'band', downward))]
    ppermute x3, waiting for transfers between devices: 5.25 us -> 10.2 us  [shards(): crossed.append(lax.ppermute(terms, 'band', swap))]
  transfers between devices with their start and end apart: 20 -> 20, of which waited for: 11 -> 10; matrix products, arithmetic and copies ran while one was open for 4% -> 4% of each run, Pallas kernels for 53% -> 55%
where the time goes in v8:
time: 355 us; the launch traced here: 353 us
  Pallas kernels  203 us (57%)
  waiting for transfers between devices  70.1 us (20%)
  starting transfers between devices  49.4 us (14%)
  other arithmetic  16.9 us (5%)
  local copies, waits for them, and re-layouts  12.8 us (4%)
    pallas_call x14, Pallas kernels, call(): pl.pallas_call(kernel, grid=(1,) if in_specs else (), out_shape=out_shape...  178 us
    all_to_all x8, starting transfers between devices, exchange(): return lax.all_to_all(wire, 'fft', split_axis=0, concat_axis=0, tiled=True)  30.2 us
    pallas_call x3, Pallas kernels, shards(): pl.pallas_call(total_kernel, grid=(cells // width,), out_shape=jax.ShapeD...  25.1 us
    all_to_all x8, waiting for transfers between devices, exchange(): return lax.all_to_all(wire, 'fft', split_axis=0, concat_axis=0, tiled=True)  24.9 us
    ppermute x3, waiting for transfers between devices, shards(): far.append(lax.ppermute(sent, 'band', upward))  17.9 us
    ppermute x3, waiting for transfers between devices, shards(): lax.ppermute(jnp.where(is_odd, far[chunk], carrying[chunk]), 'band', swap)  13.2 us
    ppermute x3, waiting for transfers between devices, shards(): crossed.append(lax.ppermute(terms, 'band', swap))  10.2 us
    unnamed x26, local copies, waits for them, and re-layouts  9.26 us
  transfers between devices with their start and end apart: 20, of which 10 were waited for; matrix products, arithmetic and copies ran while one was open for 4% of the time, Pallas kernels for 55%

profile of v8, /device:TPU:0, one launch (start us, length us, event | category | flops | bytes accessed | tf_op | source)
XLA Modules:
  0.0 353.4 jit_solution(11642009317370423438)
XLA Ops:
  0.0 1.6 slice_bitcast_fusion
  1.6 1.9 slice_bitcast_fusion.1
  4.2 2.8 broadcast_select_fusion
  7.0 3.0 collective-permute-start
  10.1 1.6 collective-permute-start.1
  11.6 1.6 collective-permute-start.2
  13.3 0.1 broadcast_add_fusion
  13.3 6.2 %fusion.5.refs_3_ = f32[44,96,256]{2,1,0:T(8,128)} fusion(f32[256]{0:T(256)S(1)} %fusion.22, f32[44,96]{1,0:T(8,128)S(1)} %broadcast_add_fusion), kind=kLoop, calls=%fused_computation.9 | loop fusion | flops 29196288 | bytes 4343296 | tf_op jit(solution)/shard_map/mul | solution.py:79
  19.5 15.5 %collective-permute-done.b_ref = bf16[16,30976]{1,0:T(8,128)(2,1)S(1)} collective-permute-done((bf16[16,30976]{1,0:T(8,128)(2,1)}, bf16[16,30976]{1,0:T(8,128)(2,1)S(1)}, u32[]{:S(2)}, u32[]{:S(2)}) %collective-permute-start) | collective-permute-done | bytes 991264 | tf_op jit(solution)/shard_map/ppermute | solution.py:339
  35.1 1.0 copy-done.4
  36.0 10.4 %density_to_ky_kz.6 = s16[4,66,16,128]{3,2,1,0:T(8,128)(2,1)} custom-call(bf16[16,30976]{1,0:T(8,128)(2,1)} %get-tuple-element.69.a_ref, bf16[16,30976]{1,0:T(8,128)(2,1)} %copy-done.4, bf16[768,256]{1,0:T(8,128)(2,1)} %constant.68.clone.z_ref, bf16[192,528]{1,0:T(8,128)(2,1)} %constant.69.clone.y_ref), custom_call_target="tpu_custom_call" | custom-call | flops 1046740992 | bytes 2578432 | tf_op jit(solution)/shard_map/density_to_ky_kz/pallas_call | solution.py:283
  46.4 3.5 all-to-all-start
  49.9 2.3 broadcast_select_fusion.5
  52.2 1.8 collective-permute-start.3
  53.9 2.4 collective-permute-done.1.b_ref
  56.3 1.0 copy-done.3
  57.3 10.3 %density_to_ky_kz.7 = s16[4,66,16,128]{3,2,1,0:T(8,128)(2,1)} custom-call(bf16[16,30976]{1,0:T(8,128)(2,1)} %get-tuple-element.67.a_ref, bf16[16,30976]{1,0:T(8,128)(2,1)} %copy-done.3, bf16[768,256]{1,0:T(8,128)(2,1)} %constant.68.clone.z_ref, bf16[192,528]{1,0:T(8,128)(2,1)} %constant.69.clone.y_ref), custom_call_target="tpu_custom_call" | custom-call | flops 1046740992 | bytes 2578432 | tf_op jit(solution)/shard_map/density_to_ky_kz/pallas_call | solution.py:283
  67.6 4.2 %all-to-all-start.1 = ((s16[4,66,16,128]{3,2,1,0:T(8,128)(2,1)}), s16[4,66,16,128]{3,2,1,0:T(8,128)(2,1)}, u32[]{:S(2)}, u32[]{:S(2)}) async-start(s16[4,66,16,128]{3,2,1,0:T(8,128)(2,1)} %density_to_ky_kz.7), calls=%async_computation.1 | async-start | bytes 2162688 | tf_op jit(solution)/shard_map/all_to_all | solution.py:297
  71.9 2.3 broadcast_select_fusion.4
  74.2 1.8 collective-permute-start.4
  76.0 0.8 collective-permute-done.3.b_ref
  76.8 10.4 %density_to_ky_kz.9 = s16[4,66,16,128]{3,2,1,0:T(8,128)(2,1)} custom-call(bf16[16,30976]{1,0:T(8,128)(2,1)} %get-tuple-element.69.a_ref, bf16[16,30976]{1,0:T(8,128)(2,1)} %collective-permute-done.3.b_ref, bf16[768,256]{1,0:T(8,128)(2,1)} %constant.68.clone.z_ref, bf16[192,528]{1,0:T(8,128)(2,1)} %constant.69.clone.y_ref), custom_call_target="tpu_custom_call" | custom-call | flops 1046740992 | bytes 2578432 | tf_op jit(solution)/shard_map/density_to_ky_kz/pallas_call | solution.py:283
  87.2 3.5 all-to-all-start.4
  90.7 2.6 broadcast_select_fusion.3
  93.3 0.3 collective-permute-start.5
  93.6 5.6 %collective-permute-done.4.b_ref = bf16[16,30976]{1,0:T(8,128)(2,1)} collective-permute-done((bf16[16,30976]{1,0:T(8,128)(2,1)}, bf16[16,30976]{1,0:T(8,128)(2,1)}, u32[]{:S(2)}, u32[]{:S(2)}) %collective-permute-start.4) | collective-permute-done | bytes 991264 | tf_op jit(solution)/shard_map/ppermute | solution.py:342
  99.2 10.3 %density_to_ky_kz.10 = s16[4,66,16,128]{3,2,1,0:T(8,128)(2,1)} custom-call(bf16[16,30976]{1,0:T(8,128)(2,1)} %get-tuple-element.67.a_ref, bf16[16,30976]{1,0:T(8,128)(2,1)} %collective-permute-done.4.b_ref, bf16[768,256]{1,0:T(8,128)(2,1)} %constant.68.clone.z_ref, bf16[192,528]{1,0:T(8,128)(2,1)} %constant.69.clone.y_ref), custom_call_target="tpu_custom_call" | custom-call | flops 1046740992 | bytes 2578432 | tf_op jit(solution)/shard_map/density_to_ky_kz/pallas_call | solution.py:283
  109.6 3.7 %all-to-all-start.5 = ((s16[4,66,16,128]{3,2,1,0:T(8,128)(2,1)}), s16[4,66,16,128]{3,2,1,0:T(8,128)(2,1)S(1)}, u32[]{:S(2)}, u32[]{:S(2)}) async-start(s16[4,66,16,128]{3,2,1,0:T(8,128)(2,1)} %density_to_ky_kz.10), calls=%async_computation.5 | async-start | bytes 2162688 | tf_op jit(solution)/shard_map/all_to_all | solution.py:297
  113.3 6.8 %collective-permute-done.5.b_ref = bf16[16,30976]{1,0:T(8,128)(2,1)} collective-permute-done((bf16[16,30976]{1,0:T(8,128)(2,1)}, bf16[16,30976]{1,0:T(8,128)(2,1)}, u32[]{:S(2)}, u32[]{:S(2)}) %collective-permute-start.5) | collective-permute-done | bytes 991264 | tf_op jit(solution)/shard_map/ppermute | solution.py:342
  120.1 10.4 %density_to_ky_kz.11 = s16[4,66,16,128]{3,2,1,0:T(8,128)(2,1)} custom-call(bf16[16,30976]{1,0:T(8,128)(2,1)} %get-tuple-element.62.a_ref, bf16[16,30976]{1,0:T(8,128)(2,1)} %collective-permute-done.5.b_ref, bf16[768,256]{1,0:T(8,128)(2,1)} %constant.68.clone.z_ref, bf16[192,528]{1,0:T(8,128)(2,1)} %constant.69.clone.y_ref), custom_call_target="tpu_custom_call" | custom-call | flops 1046740992 | bytes 2578432 | tf_op jit(solution)/shard_map/density_to_ky_kz/pallas_call | solution.py:283
  130.4 4.3 %all-to-all-start.6 = ((s16[4,66,16,128]{3,2,1,0:T(8,128)(2,1)}), s16[4,66,16,128]{3,2,1,0:T(8,128)(2,1)}, u32[]{:S(2)}, u32[]{:S(2)}) async-start(s16[4,66,16,128]{3,2,1,0:T(8,128)(2,1)} %density_to_ky_kz.11), calls=%async_computation.6 | async-start | bytes 2162688 | tf_op jit(solution)/shard_map/all_to_all | solution.py:297
  134.7 10.4 %density_to_ky_kz.8 = s16[4,66,16,128]{3,2,1,0:T(8,128)(2,1)} custom-call(bf16[16,30976]{1,0:T(8,128)(2,1)} %get-tuple-element.62.a_ref, bf16[16,30976]{1,0:T(8,128)(2,1)} %copy-done.2, bf16[768,256]{1,0:T(8,128)(2,1)} %constant.68.clone.z_ref, bf16[192,528]{1,0:T(8,128)(2,1)} %constant.69.clone.y_ref), custom_call_target="tpu_custom_call" | custom-call | flops 1046740992 | bytes 2578432 | tf_op jit(solution)/shard_map/density_to_ky_kz/pallas_call | solution.py:283
  145.1 4.5 %all-to-all-done.6.refs_2_ = s16[4,66,16,128]{3,2,1,0:T(8,128)(2,1)} async-done(((s16[4,66,16,128]{3,2,1,0:T(8,128)(2,1)}), s16[4,66,16,128]{3,2,1,0:T(8,128)(2,1)}, u32[]{:S(2)}, u32[]{:S(2)}) %all-to-all-start.6) | async-done | bytes 1081376 | tf_op jit(solution)/shard_map/all_to_all | solution.py:297
  149.6 3.5 all-to-all-start.2
  153.1 17.6 %filter_along_x.3 = s16[4,66,48,128]{3,2,1,0:T(8,128)(2,1)} custom-call(s16[4,66,16,128]{3,2,1,0:T(8,128)(2,1)} %copy-done.7, s16[4,66,16,128]{3,2,1,0:T(8,128)(2,1)} %copy-done.8, s16[4,66,16,128]{3,2,1,0:T(8,128)(2,1)} %all-to-all-done.6.refs_2_, f32[44,96,256]{2,1,0:T(8,128)} %fusion.5.refs_3_, bf16[176,576]{1,0:T(8,128)(2,1)} %constant.71.clone.refs_4_, ...), custom_call_target="tpu_custom_call" | custom-call | flops 3140222976 | bytes 7974912 | tf_op jit(solution)/shard_map/filter_along_x/pallas_call | solution.py:283
  170.7 1.0 copy-done.9
  171.8 3.7 %all-to-all-start.7 = ((s16[4,66,48,128]{3,2,1,0:T(8,128)(2,1)}), s16[4,66,48,128]{3,2,1,0:T(8,128)(2,1)S(1)}, u32[]{:S(2)}, u32[]{:S(2)}) async-start(s16[4,66,48,128]{3,2,1,0:T(8,128)(2,1)} %filter_along_x.3), calls=%async_computation.7 | async-start | bytes 6488064 | tf_op jit(solution)/shard_map/all_to_all | solution.py:297
  175.5 17.6 %filter_along_x.2 = s16[4,66,48,128]{3,2,1,0:T(8,128)(2,1)} custom-call(s16[4,66,16,128]{3,2,1,0:T(8,128)(2,1)} %copy-done.6, s16[4,66,16,128]{3,2,1,0:T(8,128)(2,1)} %all-to-all-done.1.refs_1_, s16[4,66,16,128]{3,2,1,0:T(8,128)(2,1)} %copy-done.9, f32[44,96,256]{2,1,0:T(8,128)} %fusion.5.refs_3_, bf16[176,576]{1,0:T(8,128)(2,1)} %constant.71.clone.refs_4_, ...), custom_call_target="tpu_custom_call" | custom-call | flops 3140222976 | bytes 7974912 | tf_op jit(solution)/shard_map/filter_along_x/pallas_call | solution.py:283
  193.1 20.4 %all-to-all-done.7.in_ref = s16[4,66,48,128]{3,2,1,0:T(8,128)(2,1)S(1)} async-done(((s16[4,66,48,128]{3,2,1,0:T(8,128)(2,1)}), s16[4,66,48,128]{3,2,1,0:T(8,128)(2,1)S(1)}, u32[]{:S(2)}, u32[]{:S(2)}) %all-to-all-start.7) | async-done | bytes 3244064 | tf_op jit(solution)/shard_map/all_to_all | solution.py:297
  213.4 1.7 copy-done.1
  215.1 3.7 %all-to-all-start.3 = ((s16[4,66,48,128]{3,2,1,0:T(8,128)(2,1)}), s16[4,66,48,128]{3,2,1,0:T(8,128)(2,1)S(1)}, u32[]{:S(2)}, u32[]{:S(2)}) async-start(s16[4,66,48,128]{3,2,1,0:T(8,128)(2,1)} %filter_along_x.2), calls=%async_computation.3 | async-start | bytes 6488064 | tf_op jit(solution)/shard_map/all_to_all | solution.py:297
  218.8 0.6 pad_maximum_fusion.occ.flags
  219.4 13.0 %potential_terms.6 = (f32[16,30976]{1,0:T(8,128)}, s16[16,30976]{1,0:T(8,128)(2,1)}) custom-call(s16[4,66,48,128]{3,2,1,0:T(8,128)(2,1)} %copy-done.1, bf16[16,30976]{1,0:T(8,128)(2,1)} %get-tuple-element.69.a_ref, bf16[16,30976]{1,0:T(8,128)(2,1)} %collective-permute-done.3.b_ref, f32[3]{0:T(128)} %pad_maximum_fusion.occ.flags, ...), custom_call_target="tpu_custom_call" | custom-call | flops 1046740992 | bytes 5822476 | tf_op jit(solution)/shard_map/potential_terms/pallas_call | solution.py:283
  232.5 1.7 collective-permute-start.6
  234.2 13.0 %potential_terms.7 = (f32[16,30976]{1,0:T(8,128)}, s16[16,30976]{1,0:T(8,128)(2,1)}) custom-call(s16[4,66,48,128]{3,2,1,0:T(8,128)(2,1)} %copy-done.1, bf16[16,30976]{1,0:T(8,128)(2,1)} %get-tuple-element.67.a_ref, bf16[16,30976]{1,0:T(8,128)(2,1)} %collective-permute-done.4.b_ref, f32[3]{0:T(128)} %pad_maximum_fusion.occ.flags, ...), custom_call_target="tpu_custom_call" | custom-call | flops 1046740992 | bytes 5822476 | tf_op jit(solution)/shard_map/potential_terms/pallas_call | solution.py:283
  247.2 13.1 %potential_terms.8 = (f32[16,30976]{1,0:T(8,128)}, s16[16,30976]{1,0:T(8,128)(2,1)}) custom-call(s16[4,66,48,128]{3,2,1,0:T(8,128)(2,1)} %copy-done.1, bf16[16,30976]{1,0:T(8,128)(2,1)} %get-tuple-element.62.a_ref, bf16[16,30976]{1,0:T(8,128)(2,1)} %collective-permute-done.5.b_ref, f32[3]{0:T(128)} %pad_maximum_fusion.occ.flags, ...), custom_call_target="tpu_custom_call" | custom-call | flops 1046740992 | bytes 5822476 | tf_op jit(solution)/shard_map/potential_terms/pallas_call | solution.py:283
  260.3 0.3 collective-permute-start.7
  260.6 1.7 copy-done
  262.3 13.9 %potential_terms.9 = (f32[16,30976]{1,0:T(8,128)}, s16[16,30976]{1,0:T(8,128)(2,1)}) custom-call(s16[4,66,48,128]{3,2,1,0:T(8,128)(2,1)} %copy-done, bf16[16,30976]{1,0:T(8,128)(2,1)} %get-tuple-element.69.a_ref, bf16[16,30976]{1,0:T(8,128)(2,1)} %copy-done.4, f32[3]{0:T(128)} %pad_maximum_fusion.occ.flags, bf16[768,256]{1,0:T(8,128)(2,1)} %constant.68.clone.z_ref, ...), custom_call_target="tpu_custom_call" | custom-call | flops 1046740992 | bytes 6813708 | tf_op jit(solution)/shard_map/potential_terms/pallas_call | solution.py:283
  276.2 2.0 collective-permute-start.8
  278.2 1.5 collective-permute-start.9
  279.8 5.6 %collective-permute-done.7.refs_0_.near_arrived = s16[16,30976]{1,0:T(8,128)(2,1)} collective-permute-done((s16[16,30976]{1,0:T(8,128)(2,1)}, s16[16,30976]{1,0:T(8,128)(2,1)}, u32[]{:S(2)}, u32[]{:S(2)}) %collective-permute-start.7) | collective-permute-done | bytes 991264 | tf_op jit(solution)/shard_map/ppermute | solution.py:401
  285.4 14.0 %potential_terms.10 = (f32[16,30976]{1,0:T(8,128)}, s16[16,30976]{1,0:T(8,128)(2,1)}) custom-call(s16[4,66,48,128]{3,2,1,0:T(8,128)(2,1)} %copy-done, bf16[16,30976]{1,0:T(8,128)(2,1)} %get-tuple-element.67.a_ref, bf16[16,30976]{1,0:T(8,128)(2,1)} %copy-done.3, f32[3]{0:T(128)} %pad_maximum_fusion.occ.flags, bf16[768,256]{1,0:T(8,128)(2,1)} %constant.68.clone.z_ref, ...), custom_call_target="tpu_custom_call" | custom-call | flops 1046740992 | bytes 6813708 | tf_op jit(solution)/shard_map/potential_terms/pallas_call | solution.py:283
  299.4 1.8 collective-permute-start.11
  301.2 4.6 %collective-permute-done.9.refs_0_.near_arrived = s16[16,30976]{1,0:T(8,128)(2,1)S(1)} collective-permute-done((s16[16,30976]{1,0:T(8,128)(2,1)}, s16[16,30976]{1,0:T(8,128)(2,1)S(1)}, u32[]{:S(2)}, u32[]{:S(2)}) %collective-permute-start.9) | collective-permute-done | bytes 991264 | tf_op jit(solution)/shard_map/ppermute | solution.py:401
  305.8 1.0 copy-done.5
  306.7 13.9 %potential_terms.11 = (f32[16,30976]{1,0:T(8,128)}, s16[16,30976]{1,0:T(8,128)(2,1)}) custom-call(s16[4,66,48,128]{3,2,1,0:T(8,128)(2,1)} %copy-done, bf16[16,30976]{1,0:T(8,128)(2,1)} %get-tuple-element.62.a_ref, bf16[16,30976]{1,0:T(8,128)(2,1)} %copy-done.2, f32[3]{0:T(128)} %pad_maximum_fusion.occ.flags, bf16[768,256]{1,0:T(8,128)(2,1)} %constant.68.clone.z_ref, ...), custom_call_target="tpu_custom_call" | custom-call | flops 1046740992 | bytes 6813708 | tf_op jit(solution)/shard_map/potential_terms/pallas_call | solution.py:283
  320.6 1.8 collective-permute-start.10
  322.5 8.3 %total_terms.3.refs_0_ = f32[44,1,30976]{2,1,0:T(1,128)} custom-call(f32[16,30976]{1,0:T(8,128)} %get-tuple-element.56.far_own, f32[16,30976]{1,0:T(8,128)} %get-tuple-element.57.near_own, s16[16,30976]{1,0:T(8,128)(2,1)} %copy-done.10, s16[16,30976]{1,0:T(8,128)(2,1)} %collective-permute-done.6.refs_0_.near_arrived, f32[3]{0:T(128)} %pad_maximum_fusion.occ.flags), custom_call_target="tpu_custom_call" | custom-call | tf_op jit(solution)/shard_map/total_terms/pallas_call | solution.py:415
  330.8 1.0 copy-done.11
  331.8 8.4 %total_terms.4.refs_0_ = f32[44,1,30976]{2,1,0:T(1,128)} custom-call(f32[16,30976]{1,0:T(8,128)} %get-tuple-element.53.far_own, f32[16,30976]{1,0:T(8,128)} %get-tuple-element.54.near_own, s16[16,30976]{1,0:T(8,128)(2,1)} %copy-done.11, s16[16,30976]{1,0:T(8,128)(2,1)} %collective-permute-done.7.refs_0_.near_arrived, ...), custom_call_target="tpu_custom_call", output_to_operand_aliasing={{}: (5, {})} | custom-call | tf_op jit(solution)/shard_map/total_terms/pallas_call | solution.py:415
  340.1 3.9 %collective-permute-done.10.far_arrived = s16[16,30976]{1,0:T(8,128)(2,1)S(1)} collective-permute-done((s16[16,30976]{1,0:T(8,128)(2,1)}, s16[16,30976]{1,0:T(8,128)(2,1)S(1)}, u32[]{:S(2)}, u32[]{:S(2)}) %collective-permute-start.10) | collective-permute-done | bytes 991264 | tf_op jit(solution)/shard_map/ppermute | solution.py:408
  344.0 1.0 copy-done.12
  345.0 8.3 %total_terms.5 = f32[44,1,30976]{2,1,0:T(1,128)} custom-call(f32[16,30976]{1,0:T(8,128)} %get-tuple-element.49.far_own, f32[16,30976]{1,0:T(8,128)} %get-tuple-element.50.near_own, s16[16,30976]{1,0:T(8,128)(2,1)} %copy-done.12, s16[16,30976]{1,0:T(8,128)(2,1)} %copy-done.5, f32[3]{0:T(128)} %pad_maximum_fusion.occ.flags, ...), custom_call_target="tpu_custom_call", output_to_operand_aliasing={{}: (5, {})} | custom-call | tf_op jit(solution)/shard_map/total_terms/pallas_call | solution.py:415
  (32 shorter events, 0.1 us)
Async XLA Ops:
  7.0 28.0 %collective-permute-start = (bf16[16,30976]{1,0:T(8,128)(2,1)}, bf16[16,30976]{1,0:T(8,128)(2,1)S(1)}, u32[]{:S(2)}, u32[]{:S(2)}) collective-permute-start(bf16[16,30976]{1,0:T(8,128)(2,1)} %get-tuple-element.70), channel_id=1, source_target_pairs={{0,8},{4,12},{8,16},{12,20},{16,24},{20,28},{24,0},{28,4},{1,9},{5... | collective-permute-start | bytes 2973704 | tf_op jit(solution)/shard_map/ppermute | solution.py:339
  10.1 46.2 %collective-permute-start.1 = (bf16[16,30976]{1,0:T(8,128)(2,1)}, bf16[16,30976]{1,0:T(8,128)(2,1)S(1)}, u32[]{:S(2)}, u32[]{:S(2)}) collective-permute-start(bf16[16,30976]{1,0:T(8,128)(2,1)} %get-tuple-element.68), channel_id=1, source_target_pairs={{0,8},{4,12},{8,16},{12,20},{16,24},{20,28},{24,0},{28,4},{1,9},{5... | collective-permute-start | bytes 2973704 | tf_op jit(solution)/shard_map/ppermute | solution.py:339
  11.6 79.1 %collective-permute-start.2 = (bf16[16,30976]{1,0:T(8,128)(2,1)}, bf16[16,30976]{1,0:T(8,128)(2,1)S(1)}, u32[]{:S(2)}, u32[]{:S(2)}) collective-permute-start(bf16[16,30976]{1,0:T(8,128)(2,1)} %get-tuple-element.61), channel_id=1, source_target_pairs={{0,8},{4,12},{8,16},{12,20},{16,24},{20,28},{24,0},{28,4},{1,9},{5... | collective-permute-start | bytes 2973704 | tf_op jit(solution)/shard_map/ppermute | solution.py:339
  35.1 1.0 copy-start.4
  46.4 21.3 %all-to-all-start = ((s16[4,66,16,128]{3,2,1,0:T(8,128)(2,1)}), s16[4,66,16,128]{3,2,1,0:T(8,128)(2,1)S(1)}, u32[]{:S(2)}, u32[]{:S(2)}) async-start(s16[4,66,16,128]{3,2,1,0:T(8,128)(2,1)} %density_to_ky_kz.6), calls=%async_computation | async-start | bytes 2162688 | tf_op jit(solution)/shard_map/all_to_all | solution.py:297
  52.2 24.6 %collective-permute-start.3 = (bf16[16,30976]{1,0:T(8,128)(2,1)}, bf16[16,30976]{1,0:T(8,128)(2,1)}, u32[]{:S(2)}, u32[]{:S(2)}) collective-permute-start(bf16[16,30976]{1,0:T(8,128)(2,1)} %broadcast_select_fusion.5), channel_id=1, source_target_pairs={{0,4},{4,0},{8,12},{12,8},{16,20},{20,16},{24,28},{28,24},{1,5},{5... | collective-permute-start | bytes 2973704 | tf_op jit(solution)/shard_map/ppermute | solution.py:342
  56.3 1.0 copy-start.3
  67.6 19.5 %copy-start.6 = (s16[4,66,16,128]{3,2,1,0:T(8,128)(2,1)}, s16[4,66,16,128]{3,2,1,0:T(8,128)(2,1)S(1)}, u32[]{:S(2)}) copy-start(s16[4,66,16,128]{3,2,1,0:T(8,128)(2,1)S(1)} %all-to-all-done.refs_0_) | copy-start | bytes 3244036
  67.6 19.5 %all-to-all-start.1 = ((s16[4,66,16,128]{3,2,1,0:T(8,128)(2,1)}), s16[4,66,16,128]{3,2,1,0:T(8,128)(2,1)}, u32[]{:S(2)}, u32[]{:S(2)}) async-start(s16[4,66,16,128]{3,2,1,0:T(8,128)(2,1)} %density_to_ky_kz.7), calls=%async_computation.1 | async-start | bytes 2162688 | tf_op jit(solution)/shard_map/all_to_all | solution.py:297
  74.2 25.0 %collective-permute-start.4 = (bf16[16,30976]{1,0:T(8,128)(2,1)}, bf16[16,30976]{1,0:T(8,128)(2,1)}, u32[]{:S(2)}, u32[]{:S(2)}) collective-permute-start(bf16[16,30976]{1,0:T(8,128)(2,1)} %broadcast_select_fusion.4), channel_id=1, source_target_pairs={{0,4},{4,0},{8,12},{12,8},{16,20},{20,16},{24,28},{28,24},{1,5},{5... | collective-permute-start | bytes 2973704 | tf_op jit(solution)/shard_map/ppermute | solution.py:342
  87.2 22.4 %all-to-all-start.4 = ((s16[4,66,16,128]{3,2,1,0:T(8,128)(2,1)}), s16[4,66,16,128]{3,2,1,0:T(8,128)(2,1)S(1)}, u32[]{:S(2)}, u32[]{:S(2)}) async-start(s16[4,66,16,128]{3,2,1,0:T(8,128)(2,1)} %density_to_ky_kz.9), calls=%async_computation.4 | async-start | bytes 2162688 | tf_op jit(solution)/shard_map/all_to_all | solution.py:297
  90.7 18.9 %copy-start.2 = (bf16[16,30976]{1,0:T(8,128)(2,1)}, bf16[16,30976]{1,0:T(8,128)(2,1)S(1)}, u32[]{:S(2)}) copy-start(bf16[16,30976]{1,0:T(8,128)(2,1)S(1)} %collective-permute-done.2.b_ref) | copy-start | bytes 2973700
  93.3 26.7 %collective-permute-start.5 = (bf16[16,30976]{1,0:T(8,128)(2,1)}, bf16[16,30976]{1,0:T(8,128)(2,1)}, u32[]{:S(2)}, u32[]{:S(2)}) collective-permute-start(bf16[16,30976]{1,0:T(8,128)(2,1)} %broadcast_select_fusion.3), channel_id=1, source_target_pairs={{0,4},{4,0},{8,12},{12,8},{16,20},{20,16},{24,28},{28,24},{1,5},{5... | collective-permute-start | bytes 2973704 | tf_op jit(solution)/shard_map/ppermute | solution.py:342
  109.6 35.5 %copy-start.7 = (s16[4,66,16,128]{3,2,1,0:T(8,128)(2,1)}, s16[4,66,16,128]{3,2,1,0:T(8,128)(2,1)S(1)}, u32[]{:S(2)}) copy-start(s16[4,66,16,128]{3,2,1,0:T(8,128)(2,1)S(1)} %all-to-all-done.4.refs_0_) | copy-start | bytes 3244036
  109.6 20.8 %all-to-all-start.5 = ((s16[4,66,16,128]{3,2,1,0:T(8,128)(2,1)}), s16[4,66,16,128]{3,2,1,0:T(8,128)(2,1)S(1)}, u32[]{:S(2)}, u32[]{:S(2)}) async-start(s16[4,66,16,128]{3,2,1,0:T(8,128)(2,1)} %density_to_ky_kz.10), calls=%async_computation.5 | async-start | bytes 2162688 | tf_op jit(solution)/shard_map/all_to_all | solution.py:297
  130.4 22.7 %copy-start.8 = (s16[4,66,16,128]{3,2,1,0:T(8,128)(2,1)}, s16[4,66,16,128]{3,2,1,0:T(8,128)(2,1)S(1)}, u32[]{:S(2)}) copy-start(s16[4,66,16,128]{3,2,1,0:T(8,128)(2,1)S(1)} %all-to-all-done.5.refs_1_) | copy-start | bytes 3244036
  130.4 19.2 %all-to-all-start.6 = ((s16[4,66,16,128]{3,2,1,0:T(8,128)(2,1)}), s16[4,66,16,128]{3,2,1,0:T(8,128)(2,1)}, u32[]{:S(2)}, u32[]{:S(2)}) async-start(s16[4,66,16,128]{3,2,1,0:T(8,128)(2,1)} %density_to_ky_kz.11), calls=%async_computation.6 | async-start | bytes 2162688 | tf_op jit(solution)/shard_map/all_to_all | solution.py:297
  149.6 21.1 %all-to-all-start.2 = ((s16[4,66,16,128]{3,2,1,0:T(8,128)(2,1)}), s16[4,66,16,128]{3,2,1,0:T(8,128)(2,1)S(1)}, u32[]{:S(2)}, u32[]{:S(2)}) async-start(s16[4,66,16,128]{3,2,1,0:T(8,128)(2,1)} %density_to_ky_kz.8), calls=%async_computation.2 | async-start | bytes 2162688 | tf_op jit(solution)/shard_map/all_to_all | solution.py:297
  170.7 1.0 copy-start.9
  171.8 41.7 %all-to-all-start.7 = ((s16[4,66,48,128]{3,2,1,0:T(8,128)(2,1)}), s16[4,66,48,128]{3,2,1,0:T(8,128)(2,1)S(1)}, u32[]{:S(2)}, u32[]{:S(2)}) async-start(s16[4,66,48,128]{3,2,1,0:T(8,128)(2,1)} %filter_along_x.3), calls=%async_computation.7 | async-start | bytes 6488064 | tf_op jit(solution)/shard_map/all_to_all | solution.py:297
  213.4 1.7 copy-start.1
  215.1 45.5 %all-to-all-start.3 = ((s16[4,66,48,128]{3,2,1,0:T(8,128)(2,1)}), s16[4,66,48,128]{3,2,1,0:T(8,128)(2,1)S(1)}, u32[]{:S(2)}, u32[]{:S(2)}) async-start(s16[4,66,48,128]{3,2,1,0:T(8,128)(2,1)} %filter_along_x.2), calls=%async_computation.3 | async-start | bytes 6488064 | tf_op jit(solution)/shard_map/all_to_all | solution.py:297
  232.5 28.1 %collective-permute-start.6 = (s16[16,30976]{1,0:T(8,128)(2,1)}, s16[16,30976]{1,0:T(8,128)(2,1)}, u32[]{:S(2)}, u32[]{:S(2)}) collective-permute-start(s16[16,30976]{1,0:T(8,128)(2,1)} %get-tuple-element.40), channel_id=1, source_target_pairs={{0,4},{4,0},{8,12},{12,8},{16,20},{20,16},{24,28},{28,24},{1,5},{5... | collective-permute-start | bytes 2973704 | tf_op jit(solution)/shard_map/ppermute | solution.py:401
  260.3 25.1 %collective-permute-start.7 = (s16[16,30976]{1,0:T(8,128)(2,1)}, s16[16,30976]{1,0:T(8,128)(2,1)}, u32[]{:S(2)}, u32[]{:S(2)}) collective-permute-start(s16[16,30976]{1,0:T(8,128)(2,1)} %get-tuple-element.43), channel_id=1, source_target_pairs={{0,4},{4,0},{8,12},{12,8},{16,20},{20,16},{24,28},{28,24},{1,5},{5... | collective-permute-start | bytes 2973704 | tf_op jit(solution)/shard_map/ppermute | solution.py:401
  260.6 1.7 copy-start
  276.2 25.0 %collective-permute-start.8 = (s16[16,30976]{1,0:T(8,128)(2,1)}, s16[16,30976]{1,0:T(8,128)(2,1)S(1)}, u32[]{:S(2)}, u32[]{:S(2)}) collective-permute-start(s16[16,30976]{1,0:T(8,128)(2,1)} %get-tuple-element.46), channel_id=1, source_target_pairs={{0,24},{4,28},{8,0},{12,4},{16,8},{20,12},{24,16},{28,20},{1,25},{... | collective-permute-start | bytes 2973704 | tf_op jit(solution)/shard_map/ppermute | solution.py:408
  278.2 27.5 %collective-permute-start.9 = (s16[16,30976]{1,0:T(8,128)(2,1)}, s16[16,30976]{1,0:T(8,128)(2,1)S(1)}, u32[]{:S(2)}, u32[]{:S(2)}) collective-permute-start(s16[16,30976]{1,0:T(8,128)(2,1)} %get-tuple-element.48), channel_id=1, source_target_pairs={{0,4},{4,0},{8,12},{12,8},{16,20},{20,16},{24,28},{28,24},{1,5},{5... | collective-permute-start | bytes 2973704 | tf_op jit(solution)/shard_map/ppermute | solution.py:401
  299.4 31.4 %collective-permute-start.11 = (s16[16,30976]{1,0:T(8,128)(2,1)}, s16[16,30976]{1,0:T(8,128)(2,1)S(1)}, u32[]{:S(2)}, u32[]{:S(2)}) collective-permute-start(s16[16,30976]{1,0:T(8,128)(2,1)} %get-tuple-element.55), channel_id=1, source_target_pairs={{0,24},{4,28},{8,0},{12,4},{16,8},{20,12},{24,16},{28,20},{1,25},{... | collective-permute-start | bytes 2973704 | tf_op jit(solution)/shard_map/ppermute | solution.py:408
  301.2 21.3 %copy-start.10 = (s16[16,30976]{1,0:T(8,128)(2,1)}, s16[16,30976]{1,0:T(8,128)(2,1)S(1)}, u32[]{:S(2)}) copy-start(s16[16,30976]{1,0:T(8,128)(2,1)S(1)} %collective-permute-done.8.far_arrived) | copy-start | bytes 2973700
  305.8 1.0 copy-start.5
  320.6 23.4 %collective-permute-start.10 = (s16[16,30976]{1,0:T(8,128)(2,1)}, s16[16,30976]{1,0:T(8,128)(2,1)S(1)}, u32[]{:S(2)}, u32[]{:S(2)}) collective-permute-start(s16[16,30976]{1,0:T(8,128)(2,1)} %get-tuple-element.52), channel_id=1, source_target_pairs={{0,24},{4,28},{8,0},{12,4},{16,8},{20,12},{24,16},{28,20},{1,25},{... | collective-permute-start | bytes 2973704 | tf_op jit(solution)/shard_map/ppermute | solution.py:408
  330.8 1.0 copy-start.11
  344.0 1.0 copy-start.12
